TPU v7x, 256 devices: a whole 4x4x8 slice. The times are simulated.
256 devices in a mesh: net: 4 (over x_lo, core), ctg: 64 (over z, x_hi, y).
Axes of the slice: x: 4 (x_hi: 2, x_lo: 2; x = x_hi * 2 + x_lo), y: 4, z: 8, core: 2. Of those that a mesh axis runs over, the one named last changes fastest.
Arguments:
- angle_dir: float32 [256, 16, 16384], P('ctg', None, 'net'), may hold values from -6 to 6
- dispatch_dir: float32 [16, 5120], P(None, 'net'), may hold values from -6 to 6
- barrier: bfloat16 [256, 16, 16384], P('ctg', None, 'net'), may hold values from 0.19921875 to 2
- angle_reg: float32 [16, 16384], P(None, 'net'), may hold values from 0.5 to 2
- dispatch_reg: float32 [16, 5120], P(None, 'net'), may hold values from 1 to 10
- susceptance: float32 [22528], P('net'), may hold values from 0.2 to 2
- from_bus: int32 [22528], P('net'), may hold values from 0 to 16383, as said below
- to_bus: int32 [22528], P('net'), may hold values from 1 to 16383, as said below
- outage: int32 [256], P('ctg'), may hold values from 0 to 22527
- gen_bus: int32 [5120], P('net'), may hold values from 0 to 16383, as said below
Outputs:
- angle_out: float32 [256, 16, 16384], P('ctg', None, 'net')
- dispatch_out: float32 [16, 5120], P(None, 'net')
Inputs may be any that keep to these rules, and one draw needn't show every extreme that they name: Branch k lies in network block k // 5632: from_bus[k] is a bus of that block, numbered k's block times 4096 onward. to_bus[k] - from_bus[k] is between 1 and 128, and equals 128 for some branch of every block. `gen_bus`: generator g sits at a bus of network block g // 1280.
All inputs are finite; a program needn't handle non-finite values.
Results may differ from a plain program's by a relative error of at most 0.0003.
Values sent between devices are 32-bit elements; how exact they have to be, the bound alone decides.
No kernel may reach another device: no remote copies, remote signals or barrier semaphores. Data moves between devices by JAX's collectives and lax.ppermute only.
A program may use at most 64 MiB of HBM per device.

v0:
```python
import jax
import jax.numpy as jnp
from jax import lax
from jax.sharding import PartitionSpec as P

BUS_DEV = 4096
RIM = 128


def shifted(block, axis, distance):
    devices = range(lax.axis_size(axis))
    route = [(i - distance, i) for i in devices if i - distance in devices]
    return lax.ppermute(block, axis, route)


def build_band(susceptance, from_local, to_local):
    width = BUS_DEV + RIM
    count = width // RIM
    from_tile = from_local // RIM
    from_pos = from_local % RIM
    to_tile = to_local // RIM
    to_pos = to_local % RIM
    same_tile = from_tile == to_tile
    diag_tiles = jnp.zeros((count, RIM, RIM), jnp.float32)
    diag_tiles = diag_tiles.at[from_tile, from_pos, from_pos].add(susceptance)
    diag_tiles = diag_tiles.at[to_tile, to_pos, to_pos].add(susceptance)
    inside = jnp.where(same_tile, -susceptance, 0.0)
    diag_tiles = diag_tiles.at[from_tile, from_pos, to_pos].add(inside)
    diag_tiles = diag_tiles.at[from_tile, to_pos, from_pos].add(inside)
    across = jnp.where(same_tile, 0.0, -susceptance)
    upper_tiles = jnp.zeros((count - 1, RIM, RIM), jnp.float32)
    upper_tiles = upper_tiles.at[jnp.minimum(from_tile, count - 2), from_pos, to_pos].add(across)
    return (diag_tiles, upper_tiles)


def apply_band(extended, diag_tiles, upper_tiles):
    cases, periods, width = extended.shape
    count = width // RIM
    tiles = extended.reshape(cases, periods, count, RIM)
    highest = lax.Precision.HIGHEST
    own_part = jnp.einsum("cpjr,jrs->cpjs", tiles, diag_tiles, precision=highest)
    below_part = jnp.einsum("cpjr,jrs->cpjs", tiles[:, :, :-1], upper_tiles, precision=highest)
    above_part = jnp.einsum("cpjs,jrs->cpjr", tiles[:, :, 1:], upper_tiles, precision=highest)
    zero_tile = jnp.zeros((cases, periods, 1, RIM), jnp.float32)
    total = (
        own_part
        + jnp.concatenate([zero_tile, below_part], axis=2)
        + jnp.concatenate([above_part, zero_tile], axis=2)
    )
    return total.reshape(cases, periods, width)


def apply_network(field, band, outage_from, outage_to, outage_susc, outage_sel):
    upper_part = shifted(field[..., :RIM], "net", -1)
    extended = jnp.concatenate([field, upper_part], axis=-1)
    accum = apply_band(extended, band[0], band[1])
    from_val = jnp.take_along_axis(
        extended,
        jnp.broadcast_to(outage_from[:, None, None], (field.shape[0], field.shape[1], 1)),
        axis=2,
    )
    to_val = jnp.take_along_axis(
        extended,
        jnp.broadcast_to(outage_to[:, None, None], (field.shape[0], field.shape[1], 1)),
        axis=2,
    )
    outage_flow = outage_susc[:, None, None] * (from_val - to_val)
    accum = accum - outage_flow * outage_sel[:, None, :]
    returned = shifted(accum[..., BUS_DEV:], "net", 1)
    leading = accum[..., :RIM] + returned
    return jnp.concatenate([leading, accum[..., RIM:BUS_DEV]], axis=-1)


def body(
    angle_dir,
    dispatch_dir,
    barrier,
    angle_reg,
    dispatch_reg,
    susceptance,
    from_bus,
    to_bus,
    outage,
    gen_bus,
):
    block_index = lax.axis_index("net")
    bus_offset = block_index * BUS_DEV
    from_local = from_bus - bus_offset
    to_local = to_bus - bus_offset
    gen_local = gen_bus - bus_offset
    band = build_band(susceptance, from_local, to_local)
    branch_count = susceptance.shape[0]
    outage_local = outage - block_index * branch_count
    present = (outage_local >= 0) & (outage_local < branch_count)
    safe_index = jnp.clip(outage_local, 0, branch_count - 1)
    outage_from = from_local[safe_index]
    outage_to = to_local[safe_index]
    outage_susc = jnp.where(present, susceptance[safe_index], 0.0)
    positions = jnp.arange(BUS_DEV + RIM, dtype=jnp.int32)
    outage_sel = (positions[None, :] == outage_from[:, None]).astype(jnp.float32) - (
        positions[None, :] == outage_to[:, None]
    ).astype(jnp.float32)
    inject = (
        jnp.zeros((dispatch_dir.shape[0], BUS_DEV), jnp.float32).at[:, gen_local].add(dispatch_dir)
    )
    resid = (
        apply_network(angle_dir, band, outage_from, outage_to, outage_susc, outage_sel)
        - inject[None, :, :]
    )
    weighted = barrier.astype(jnp.float32) * resid
    angle_out = (
        apply_network(weighted, band, outage_from, outage_to, outage_susc, outage_sel)
        + angle_reg[None, :, :] * angle_dir
    )
    local_total = jnp.sum(weighted, axis=0)
    case_count = float(angle_dir.shape[0] * lax.axis_size("ctg"))
    summed = lax.psum(local_total, "ctg")
    dispatch_out = dispatch_reg * dispatch_dir - summed[:, gen_local] / case_count
    return (angle_out, dispatch_out)


def solution(mesh):
    placed = (
        P("ctg", None, "net"),
        P(None, "net"),
        P("ctg", None, "net"),
        P(None, "net"),
        P(None, "net"),
        P("net"),
        P("net"),
        P("net"),
        P("ctg"),
        P("net"),
    )
    return jax.shard_map(
        body,
        mesh=mesh,
        in_specs=placed,
        out_specs=(P("ctg", None, "net"), P(None, "net")),
        check_vma=False,
    )
```

profile of v0, /device:TPU:2, one launch (start us, length us, event | category | flops | bytes accessed | tf_op | source)
XLA Modules:
  0.0 952.8 jit_solution(3046573139266170972)
XLA Ops:
  8.0 1.9 collective-permute-start
  9.9 1.3 constant_dynamic-update-slice_fusion.1
  16.8 30.6 %scatter_custom_fusion.1 = f32[540672]{0:T(1024)S(1)} fusion(s32[5632]{0:T(1024)} %broadcast_select_fusion.4, f32[5632]{0:T(1024)S(1)} %copy-done.3, f32[]{:T(128)} %constant.68.clone.1), kind=kCustom, calls=%fused_computation.19 | custom fusion | flops 5632 | bytes 2163200
  47.3 31.3 %scatter_fusion = f32[540672]{0:T(1024)S(1)} fusion(f32[540672]{0:T(1024)S(1)} %scatter_custom_fusion.1, s32[5632]{0:T(1024)S(1)} %broadcast_select_fusion.3, f32[5632]{0:T(1024)S(1)} %copy-done.3), kind=kCustom, calls=%fused_computation.10 | custom fusion | flops 5632 | bytes 90112
  78.7 31.3 %scatter_fusion.1 = f32[540672]{0:T(1024)S(1)} fusion(f32[540672]{0:T(1024)S(1)} %scatter_fusion, s32[5632]{0:T(1024)S(1)} %broadcast_select_fusion.2, f32[5632]{0:T(1024)S(1)} %get-tuple-element.21), kind=kCustom, calls=%fused_computation.11 | custom fusion | flops 5632 | bytes 90112
  110.0 31.3 %scatter_fusion.2 = f32[540672]{0:T(1024)S(1)} fusion(f32[540672]{0:T(1024)S(1)} %scatter_fusion.1, s32[5632]{0:T(1024)S(1)} %broadcast_select_fusion.1, f32[5632]{0:T(1024)S(1)} %get-tuple-element.21), kind=kCustom, calls=%fused_computation.12 | custom fusion | flops 5632 | bytes 90112
  141.3 31.5 %scatter_custom_fusion.5 = f32[524288]{0:T(1024)} fusion(s32[5632]{0:T(1024)} %broadcast_select_fusion, f32[5632]{0:T(1024)S(1)} %negate_select_fusion.6, f32[]{:T(128)} %constant.68.clone.1), kind=kCustom, calls=%fused_computation.26 | custom fusion | flops 5632 | bytes 2097664
  174.9 5.1 fusion.36
  180.1 2.9 fusion.35
  184.1 1.0 gather_fusion.5
  185.2 3.4 fusion.34
  189.1 2.4 collective-permute-start.1
  191.5 1.1 copy.34
  192.6 10.5 %scatter_custom_fusion = f32[16,4096]{0,1:T(8,128)} fusion(s32[1280]{0:T(1024)S(1)} %compare_select_fusion.5, f32[1280,16]{1,0:T(8,128)} %copy.34, f32[]{:T(128)} %constant.68.clone.1), kind=kCustom, calls=%fused_computation.28 | custom fusion | flops 20480 | bytes 262656 | tf_op jit(solution)/shard_map/scatter-add | solution.py:104
  203.1 2.9 copy.35
  207.3 4.0 collective-permute-start.2
  211.3 1.4 collective-permute-done.2
  212.7 1.2 pad_maximum_fusion
  215.8 1.4 copy.52
  217.4 1.4 copy-done.1
  218.8 3.0 fusion.38
  221.8 3.0 fusion.37
  224.8 5.1 fusion.39
  230.2 1.5 bitcast_subtract_fusion
  231.7 1.9 collective-permute-start.3
  233.7 1.1 copy.41
  234.8 1.1 copy.40
  235.9 1.9 copy.42
  238.0 1.1 copy-done.4
  239.1 1.1 maximum_add_fusion
  240.2 700.9 %all-reduce.6.cloned.1.call-done = f32[16,4096]{0,1:T(8,128)} async-done(((f32[16,4096]{0,1:T(8,128)}), f32[16,4096]{0,1:T(8,128)}) %all-reduce.6.cloned.1.call-update) | async-done | bytes 262160 | tf_op jit(solution)/shard_map/psum | solution.py:117
  941.1 3.9 gather_fusion.3
  (138 shorter events, 14.5 us)
Async XLA Ops:
  7.2 4.1 copy-start.36
  7.2 4.1 copy-start.3
  7.2 4.1 copy-start.15
  7.2 4.1 copy-start.14
  7.2 933.9 %all-reduce.6.cloned.1.call-start = ((), (), s32[]{:S(2)}) async-start(), calls=%async_computation | async-start | bytes 4194304 | tf_op jit(solution)/shard_map/psum | solution.py:117
  8.0 164.8 %collective-permute-start = (f32[4,16,128]{2,1,0:T(8,128)S(1)}, f32[4,16,128]{2,1,0:T(8,128)S(1)}, u32[]{:S(2)}, u32[]{:S(2)}) collective-permute-start(f32[4,16,128]{2,1,0:T(8,128)S(1)} %slice.36), channel_id=1, source_target_pairs={{64,0},{128,64},{192,128},{65,1},{129,65},{193,129},{66,2},{130,66... | collective-permute-start | bytes 98312 | tf_op jit(solution)/shard_map/ppermute | solution.py:13
  11.4 2.7 copy-start.33
  11.4 2.7 copy-start.34
  12.0 3.9 copy-start.19
  12.0 3.9 copy-start.22
  12.8 175.9 %copy-start.16 = (s32[4]{0:T(128)}, s32[4]{0:T(128)S(1)}, u32[]{:S(2)}) copy-start(s32[4]{0:T(128)S(1)} %gather_fusion.1) | copy-start | bytes 52
  12.8 3.9 copy-start.25
  12.8 3.9 copy-start.28
  13.5 175.2 %copy-start.10 = (f32[4,4224]{1,0:T(4,128)}, f32[4,4224]{1,0:T(4,128)S(1)}, u32[]{:S(2)}) copy-start(f32[4,4224]{1,0:T(4,128)S(1)} %convert_subtract_fusion) | copy-start | bytes 202756
  185.2 3.4 copy-start.20
  185.2 3.4 copy-start.23
  185.2 3.4 copy-start.26
  185.2 3.5 copy-start.29
  185.2 3.5 copy-start.31
  185.2 3.5 copy-start.7
  185.2 3.5 copy-start.8
  189.1 17.0 %collective-permute-start.1 = (f32[4,16,128]{2,1,0:T(8,128)S(1)}, f32[4,16,128]{2,1,0:T(8,128)S(1)}, u32[]{:S(2)}, u32[]{:S(2)}) collective-permute-start(f32[4,16,128]{2,1,0:T(8,128)S(1)} %slice.89), channel_id=1, source_target_pairs={{0,64},{64,128},{128,192},{1,65},{65,129},{129,193},{2,66},{66,130... | collective-permute-start | bytes 98312 | tf_op jit(solution)/shard_map/ppermute | solution.py:13
  207.3 5.4 collective-permute-start.2
  224.8 5.4 copy-start.17
  224.8 5.4 copy-start.21
  224.8 5.4 copy-start.24
  224.8 5.4 copy-start.27
  224.8 5.4 copy-start.30
  224.8 5.4 copy-start.32
  224.8 5.4 copy-start.5
  224.8 5.4 copy-start.6
  231.7 6.2 collective-permute-start.3
  (10 other events, 16.9 us)
Sparse Core Ops, SparseCore 0:
  238.0 703.0 all-reduce.5
where the time goes:
time: 954 us; the launch traced here: 953 us
  waiting for transfers between devices  702 us (74%)
  other arithmetic  174 us (18%)
  local copies, waits for them, and re-layouts  28.9 us (3%)
  matrix products  22.5 us (2%)
  between operations  14.8 us (2%)
  starting transfers between devices  10.3 us (1%)
    psum x1, waiting for transfers between devices, body(): summed = lax.psum(local_total, 'ctg')  701 us
    unnamed x12, other arithmetic  158 us
    unnamed x6, matrix products  22.5 us
  transfers between devices with their start and end apart: 5, of which 2 were waited for; matrix products, arithmetic and copies ran while one was open for 19% of the time, Pallas kernels for 0%

commit v1 on v0

v1 whole, which is shorter than its diff:
```python
import jax
import jax.numpy as jnp
from jax import lax
from jax.experimental import pallas as pl
from jax.experimental.pallas import tpu as pltpu
from jax.sharding import PartitionSpec as P

BUS_DEV = 4096
BR_DEV = 5632
G_DEV = 1280
RIM = 128
PERIODS = 16
TILES = BUS_DEV // RIM
BR_ROWS = BR_DEV // RIM
CASES = 4
ROWS = CASES * PERIODS
VMEM_LIMIT = 56 * 1024 * 1024
BF16 = jnp.bfloat16
F32 = jnp.float32


def split(value):
    high = value.astype(BF16)
    low = (value - high.astype(F32)).astype(BF16)
    return high, low


def dot_last(left, right):
    return lax.dot_general(
        left, right, (((1,), (1,)), ((), ())), preferred_element_type=F32
    )


def dot_plain(left, right):
    return jnp.dot(left, right, preferred_element_type=F32)


def whole(ref_space=pltpu.VMEM):
    return pl.BlockSpec(memory_space=ref_space)


def pack_kernel(from_ref, to_ref, susc_ref, last_ref, out_ref):
    for row in range(BR_ROWS):
        cols = pl.ds(row * RIM, RIM)
        out_ref[row : row + 1, :] = from_ref[:, cols].astype(F32)
        out_ref[BR_ROWS + row : BR_ROWS + row + 1, :] = to_ref[:, cols].astype(F32)
        out_ref[2 * BR_ROWS + row : 2 * BR_ROWS + row + 1, :] = susc_ref[:, cols]
    out_ref[136:200, :] = last_ref[...]


def pack(from_bus, to_bus, susceptance, field):
    row = pl.BlockSpec((1, BR_DEV), lambda i: (0, 0))
    return pl.pallas_call(
        pack_kernel,
        grid=(1,),
        in_specs=[row, row, row, pl.BlockSpec((ROWS, RIM), lambda i: (0, TILES - 1))],
        out_specs=pl.BlockSpec((200, RIM), lambda i: (0, 0)),
        out_shape=jax.ShapeDtypeStruct((200, RIM), F32),
        name="pack",
    )(from_bus, to_bus, susceptance, field)


def end_rows(to_pos, susc):
    high, low = split(susc)
    spots = lax.broadcasted_iota(jnp.int32, (RIM, to_pos.shape[1]), 0)
    hit = spots == to_pos
    zero = jnp.zeros((), BF16)
    return jnp.concatenate(
        [jnp.where(hit, high, zero), jnp.where(hit, low, zero)], axis=0
    )


def wide_tiles(block):
    rows = lax.broadcasted_iota(jnp.int32, (RIM, RIM), 0)
    cols = lax.broadcasted_iota(jnp.int32, (RIM, RIM), 1)
    inside = cols > rows
    return jnp.concatenate(
        [jnp.where(inside, block, 0.0), jnp.where(inside, 0.0, block)], axis=1
    )


BUILD_ROWS = 512


def band_kernel(from_ref, to_ref, susc_ref, base_ref, high_ref, low_ref, ends_ref):
    step = pl.program_id(0)

    @pl.when(step == 0)
    def _():
        ends_ref[...] = end_rows((to_ref[...] - base_ref[0]) % RIM, susc_ref[...])

    from_local = from_ref[...] - base_ref[0] - step * BUILD_ROWS
    spots = lax.broadcasted_iota(jnp.int32, (BUILD_ROWS, BR_DEV), 0)
    starts = jnp.where(spots == from_local, 1.0, 0.0).astype(BF16)
    both = dot_last(starts, ends_ref[...])
    block = both[:, :RIM] + both[:, RIM:]
    for tile in range(BUILD_ROWS // RIM):
        high, low = split(wide_tiles(block[tile * RIM : (tile + 1) * RIM]))
        high_ref[tile] = high
        low_ref[tile] = low


def build_band(from_bus, to_bus, susceptance, base):
    row = pl.BlockSpec((1, BR_DEV), lambda i: (0, 0))
    step = BUILD_ROWS // RIM
    out = pl.BlockSpec((step, RIM, 2 * RIM), lambda i: (i, 0, 0))
    shape = jax.ShapeDtypeStruct((TILES, RIM, 2 * RIM), BF16)
    return pl.pallas_call(
        band_kernel,
        grid=(TILES // step,),
        in_specs=[row, row, row, whole(pltpu.SMEM)],
        out_specs=[out, out],
        out_shape=[shape, shape],
        scratch_shapes=[pltpu.VMEM((2 * RIM, BR_DEV), BF16)],
        compiler_params=pltpu.CompilerParams(vmem_limit_bytes=VMEM_LIMIT),
        cost_estimate=pl.CostEstimate(
            flops=2 * BUS_DEV * BR_DEV * 2 * RIM, bytes_accessed=4 << 20, transcendentals=0
        ),
        name="band",
    )(from_bus, to_bus, susceptance, base)


def outage_row(from_at, to_at, tile):
    spots = lax.broadcasted_iota(jnp.int32, (1, RIM), 1) + (tile + 1) * RIM
    return jnp.where(spots == from_at, 1.0, 0.0) - jnp.where(spots == to_at, 1.0, 0.0)


def stack_parts(values):
    high, low = split(values)
    return jnp.concatenate([high, low, jnp.ones((16, RIM), BF16)], axis=0)


def apply_tiles(tile_of, stacks, high_ref, low_ref, cross_high, cross_low, ends, susc, emit):
    flows = [jnp.zeros((PERIODS, RIM), F32) for _ in range(CASES)]
    for tile in range(-1, TILES + 1):
        value = tile_of(tile)
        stacks[tile + 1] = stack_parts(value)
        for case in range(CASES):
            mask = outage_row(ends[case][0], ends[case][1], tile)
            flows[case] += value[case * PERIODS : (case + 1) * PERIODS] * mask
    drops = [
        susc[case] * jnp.sum(flows[case], axis=1, keepdims=True) for case in range(CASES)
    ]
    before = dot_plain(stacks[0], cross_high) + dot_plain(stacks[0], cross_low)
    for tile in range(TILES):
        own = stacks[tile + 1]
        high, low = high_ref[tile], low_ref[tile]
        ahead = dot_plain(own, high) + dot_plain(own, low)
        near = jnp.concatenate([own, stacks[tile + 2]], axis=1)
        sums = before + ahead[:, :RIM] + dot_last(near, high) + dot_last(near, low)
        before = ahead[:, RIM:]
        degrees = sums[2 * ROWS : 2 * ROWS + 1]
        value = tile_of(tile)
        result = degrees * value - (sums[:ROWS] + sums[ROWS : 2 * ROWS])
        parts = []
        for case in range(CASES):
            mask = outage_row(ends[case][0], ends[case][1], tile)
            parts.append(
                result[case * PERIODS : (case + 1) * PERIODS] - drops[case] * mask
            )
        emit(tile, jnp.concatenate(parts, axis=0))


def resid_kernel(
    place_ref,
    outage_ref,
    field_ref,
    barrier_ref,
    high_ref,
    low_ref,
    from_ref,
    to_ref,
    susc_ref,
    left_ref,
    right_ref,
    dispatch_ref,
    gen_ref,
    weighted_ref,
    first_ref,
    last_ref,
    partial_ref,
    cross_high_ref,
    cross_low_ref,
    ends_ref,
    stacks,
    inject,
    total,
):
    block = place_ref[0]
    base = block * BUS_DEV
    keep = jnp.where(block > 0, 1.0, 0.0)
    left_from = jnp.concatenate(
        [left_ref[r : r + 1] for r in range(BR_ROWS)], axis=1
    ).astype(jnp.int32)
    left_to = jnp.concatenate(
        [left_ref[BR_ROWS + r : BR_ROWS + r + 1] for r in range(BR_ROWS)], axis=1
    ).astype(jnp.int32)
    left_susc = jnp.concatenate(
        [left_ref[2 * BR_ROWS + r : 2 * BR_ROWS + r + 1] for r in range(BR_ROWS)], axis=1
    )
    crosses = left_to >= base
    left_ends = end_rows(
        (left_to - base) % RIM, jnp.where(crosses, left_susc, 0.0) * keep
    )
    spots = lax.broadcasted_iota(jnp.int32, (RIM, BR_DEV), 0) + (base - RIM)
    starts = jnp.where(spots == left_from, 1.0, 0.0).astype(BF16)
    both = dot_last(starts, left_ends)
    cross_high, cross_low = split(both[:, :RIM] + both[:, RIM:])
    cross_high_ref[...] = cross_high
    cross_low_ref[...] = cross_low

    branch = lax.broadcasted_iota(jnp.int32, (1, BR_DEV), 1)
    ends, susc = [], []
    for case in range(CASES):
        own_hit = branch == outage_ref[case] - block * BR_DEV
        left_hit = branch == outage_ref[case] - (block - 1) * BR_DEV
        pick = lambda own, left: (
            jnp.sum(jnp.where(own_hit, own, 0.0), axis=1, keepdims=True)
            + jnp.sum(jnp.where(left_hit, left, 0.0), axis=1, keepdims=True) * keep
        )
        start = pick(from_ref[...].astype(F32), left_from.astype(F32)).astype(jnp.int32)
        end = pick(to_ref[...].astype(F32), left_to.astype(F32)).astype(jnp.int32)
        ends.append((start - base + RIM, end - base + RIM))
        susc.append(pick(susc_ref[...], left_susc))
        ends_ref[case : case + 1, :] = jnp.broadcast_to(ends[case][0].astype(F32), (1, RIM))
        ends_ref[4 + case : 5 + case, :] = jnp.broadcast_to(
            ends[case][1].astype(F32), (1, RIM)
        )
        ends_ref[8 + case : 9 + case, :] = jnp.broadcast_to(susc[case], (1, RIM))

    gen = gen_ref[...] - base
    gen_tile = gen // RIM
    spots = lax.broadcasted_iota(jnp.int32, (RIM, G_DEV), 0)
    gen_spots = jnp.where(spots == gen % RIM, 1.0, 0.0).astype(BF16)
    dispatch = dispatch_ref[...]
    dispatch_high, dispatch_low = split(dispatch)
    zero = jnp.zeros((), BF16)
    for part in range(4):
        tiles = range(part * TILES // 4, (part + 1) * TILES // 4)
        picked = jnp.concatenate(
            [jnp.where(gen_tile == tile, dispatch_high, zero) for tile in tiles]
            + [jnp.where(gen_tile == tile, dispatch_low, zero) for tile in tiles],
            axis=0,
        )
        spread = dot_last(picked, gen_spots)
        half = spread.shape[0] // 2
        inject[part * half : (part + 1) * half] = spread[:half] + spread[half:]

    def tile_of(tile):
        if tile < 0:
            return left_ref[136:200]
        if tile == TILES:
            return right_ref[...]
        return field_ref[:, tile * RIM : (tile + 1) * RIM]

    def emit(tile, result):
        rows = slice(tile * PERIODS, (tile + 1) * PERIODS)
        taken = inject[rows]
        resid = result - jnp.concatenate([taken] * CASES, axis=0)
        weighted = barrier_ref[:, tile * RIM : (tile + 1) * RIM].astype(F32) * resid
        weighted_ref[:, tile * RIM : (tile + 1) * RIM] = weighted
        if tile == 0:
            first_ref[...] = weighted
        if tile == TILES - 1:
            last_ref[...] = weighted
        total[rows] = (
            weighted[0:16] + weighted[16:32] + (weighted[32:48] + weighted[48:64])
        )

    apply_tiles(
        tile_of, stacks, high_ref, low_ref, cross_high, cross_low, ends, susc, emit
    )

    at_gens = jnp.zeros((PERIODS, G_DEV), F32)
    for part in range(4):
        size = TILES * PERIODS // 4
        high, low = split(total[part * size : (part + 1) * size])
        both = dot_plain(jnp.concatenate([high, low], axis=0), gen_spots)
        for k in range(TILES // 4):
            tile = part * TILES // 4 + k
            rows = slice(k * PERIODS, (k + 1) * PERIODS)
            value = both[rows] + both[size + k * PERIODS : size + (k + 1) * PERIODS]
            at_gens += jnp.where(gen_tile == tile, value, 0.0)
    partial_ref[...] = at_gens


def residuals(place, outage, field, barrier, band, raw, halos, dispatch, gen_bus):
    tile = jax.ShapeDtypeStruct((ROWS, RIM), F32)
    return pl.pallas_call(
        resid_kernel,
        in_specs=[whole(pltpu.SMEM)] * 2 + [whole()] * 11,
        out_specs=[whole()] * 7,
        out_shape=[
            jax.ShapeDtypeStruct((ROWS, BUS_DEV), F32),
            tile,
            tile,
            jax.ShapeDtypeStruct((PERIODS, G_DEV), F32),
            jax.ShapeDtypeStruct((RIM, RIM), BF16),
            jax.ShapeDtypeStruct((RIM, RIM), BF16),
            jax.ShapeDtypeStruct((16, RIM), F32),
        ],
        scratch_shapes=[
            pltpu.VMEM((TILES + 2, 2 * ROWS + 16, RIM), BF16),
            pltpu.VMEM((TILES * PERIODS, RIM), F32),
            pltpu.VMEM((TILES * PERIODS, RIM), F32),
        ],
        compiler_params=pltpu.CompilerParams(vmem_limit_bytes=VMEM_LIMIT),
        cost_estimate=pl.CostEstimate(flops=4 << 30, bytes_accessed=8 << 20, transcendentals=0),
        name="resid",
    )(place, outage, field, barrier, *band, *raw, *halos, dispatch, gen_bus)


def angle_kernel(
    weighted_ref,
    field_ref,
    reg_ref,
    high_ref,
    low_ref,
    cross_high_ref,
    cross_low_ref,
    ends_ref,
    left_ref,
    right_ref,
    out_ref,
    stacks,
):
    ends, susc = [], []
    for case in range(CASES):
        start = ends_ref[case : case + 1, 0:1].astype(jnp.int32)
        end = ends_ref[4 + case : 5 + case, 0:1].astype(jnp.int32)
        ends.append((start, end))
        susc.append(ends_ref[8 + case : 9 + case, 0:1])

    def tile_of(tile):
        if tile < 0:
            return left_ref[...]
        if tile == TILES:
            return right_ref[...]
        return weighted_ref[:, tile * RIM : (tile + 1) * RIM]

    def emit(tile, result):
        cols = slice(tile * RIM, (tile + 1) * RIM)
        scale = jnp.concatenate([reg_ref[:, cols]] * CASES, axis=0)
        out_ref[:, cols] = result + scale * field_ref[:, cols]

    apply_tiles(
        tile_of,
        stacks,
        high_ref,
        low_ref,
        cross_high_ref[...],
        cross_low_ref[...],
        ends,
        susc,
        emit,
    )


def angles(weighted, field, reg, band, cross, ends, halos):
    return pl.pallas_call(
        angle_kernel,
        in_specs=[whole()] * 10,
        out_specs=whole(),
        out_shape=jax.ShapeDtypeStruct((ROWS, BUS_DEV), F32),
        scratch_shapes=[pltpu.VMEM((TILES + 2, 2 * ROWS + 16, RIM), BF16)],
        compiler_params=pltpu.CompilerParams(vmem_limit_bytes=VMEM_LIMIT),
        cost_estimate=pl.CostEstimate(flops=4 << 30, bytes_accessed=8 << 20, transcendentals=0),
        name="angles",
    )(weighted, field, reg, *band, *cross, ends, *halos)


def shifted(block, distance):
    size = lax.axis_size("net")
    return lax.ppermute(block, "net", [(i, (i + distance) % size) for i in range(size)])


def sum_cases(value):
    size = lax.axis_size("ctg")
    for mask in (1, 3, 4, 8, 16, 56):
        value = value + lax.ppermute(value, "ctg", [(i, i ^ mask) for i in range(size)])
    return value


def body(
    angle_dir,
    dispatch_dir,
    barrier,
    angle_reg,
    dispatch_reg,
    susceptance,
    from_bus,
    to_bus,
    outage,
    gen_bus,
):
    block = lax.axis_index("net")
    place = jnp.reshape(block, (1,)).astype(jnp.int32)
    field = angle_dir.reshape(ROWS, BUS_DEV)
    weights = barrier.reshape(ROWS, BUS_DEV)
    raw = (
        from_bus.reshape(1, BR_DEV),
        to_bus.reshape(1, BR_DEV),
        susceptance.reshape(1, BR_DEV),
    )
    packed = pack(*raw, field)
    left = shifted(packed, 1)
    right = shifted(field[:, :RIM], -1)
    band = build_band(*raw, place * BUS_DEV)
    weighted, first, last, partial, cross_high, cross_low, ends = residuals(
        place,
        outage,
        field,
        weights,
        band,
        raw,
        (left, right),
        dispatch_dir,
        gen_bus.reshape(1, G_DEV),
    )
    halos = (shifted(last, 1), shifted(first, -1))
    summed = sum_cases(partial)
    angle_out = angles(
        weighted, field, angle_reg, band, (cross_high, cross_low), ends, halos
    )
    case_count = float(CASES * lax.axis_size("ctg"))
    dispatch_out = dispatch_reg * dispatch_dir - summed / case_count
    return (angle_out.reshape(angle_dir.shape), dispatch_out)


def solution(mesh):
    placed = (
        P("ctg", None, "net"),
        P(None, "net"),
        P("ctg", None, "net"),
        P(None, "net"),
        P(None, "net"),
        P("net"),
        P("net"),
        P("net"),
        P("ctg"),
        P("net"),
    )
    return jax.shard_map(
        body,
        mesh=mesh,
        in_specs=placed,
        out_specs=(P("ctg", None, "net"), P(None, "net")),
        check_vma=False,
    )
```

time: 954 us -> 78.2 us (0.08)
  waiting for transfers between devices: 702 us -> 12.9 us
  other arithmetic: 174 us -> 1.6 us
  Pallas kernels: 0 us -> 33.7 us
  matrix products: 22.5 us -> 0 us
  local copies, waits for them, and re-layouts: 28.9 us -> 6.72 us
  between operations: 14.8 us -> 0.7 us
  starting transfers between devices: 10.3 us -> 21.9 us
    psum x1 -> x0, waiting for transfers between devices: 701 us -> none  [body(): summed = lax.psum(local_total, 'ctg')]
    unnamed x12 -> x0, other arithmetic: 158 us -> none
    pallas_call x0 -> x4, Pallas kernels: none -> 33.7 us  [the longest x1 16 us: build_band(): pl.pallas_call(band_kernel, grid=(TILES // step,), in_specs=[row, row, ro...]
    unnamed x6 -> x0, matrix products: 22.5 us -> none
    ppermute x4 -> x10, starting transfers between devices: 10.3 us -> 21.9 us  [the longest x6 19.6 us: sum_cases(): lax.ppermute(value, 'ctg', [(i, i ^ mask) for i in range(size)])]
    ppermute x4 -> x10, waiting for transfers between devices: 1.36 us -> 12.9 us  [the longest x6 12.8 us: sum_cases(): lax.ppermute(value, 'ctg', [(i, i ^ mask) for i in range(size)])]
    scatter-add x1 -> x0, other arithmetic: 10.5 us -> none  [body(): jnp.zeros((dispatch_dir.shape[0], BUS_DEV), jnp.float32).at[:, gen_local]]
    gather x14 -> x0, local copies, waits for them, and re-layouts: 10.3 us -> none  [the longest x1 3.93 us: body(): summed[:, gen_local] / case_count]
  transfers between devices with their start and end apart: 5 -> 10, of which waited for: 2 -> 5; matrix products, arithmetic and copies ran while one was open for 19% -> 6% of each run, Pallas kernels for 0% -> 31%
where the time goes in v1:
time: 78.2 us; the launch traced here: 77.4 us
  Pallas kernels  33.7 us (43%)
  starting transfers between devices  21.9 us (28%)
  waiting for transfers between devices  12.9 us (16%)
  local copies, waits for them, and re-layouts  6.72 us (9%)
  other arithmetic  1.6 us (2%)
    ppermute x6, starting transfers between devices, sum_cases(): lax.ppermute(value, 'ctg', [(i, i ^ mask) for i in range(size)])  19.6 us
    pallas_call x1, Pallas kernels, build_band(): pl.pallas_call(band_kernel, grid=(TILES // step,), in_specs=[row, row, ro...  16 us
    ppermute x6, waiting for transfers between devices, sum_cases(): lax.ppermute(value, 'ctg', [(i, i ^ mask) for i in range(size)])  12.8 us
    pallas_call x1, Pallas kernels, residuals(): pl.pallas_call(resid_kernel, in_specs=[whole(pltpu.SMEM)] * 2 + [whole()]...  9.31 us
    pallas_call x1, Pallas kernels, angles(): pl.pallas_call(angle_kernel, in_specs=[whole()] * 10, out_specs=whole(),...  6.88 us
    ppermute x4, starting transfers between devices, shifted(): lax.ppermute(block, 'net', [(i, (i + distance) % size) for i in range(siz...  2.26 us
  transfers between devices with their start and end apart: 10, of which 5 were waited for; matrix products, arithmetic and copies ran while one was open for 6% of the time, Pallas kernels for 31%

profile of v1, /device:TPU:2, one launch (start us, length us, event | category | flops | bytes accessed | tf_op | source)
XLA Modules:
  0.0 77.4 jit_solution(333101689364703448)
XLA Ops:
  0.6 0.8 slice.4
  1.4 1.4 %reshape.33.susc_ref = f32[1,5632]{1,0:T(1,128)} reshape(f32[5632]{0:T(1024)} %param.15) | data formatting | bytes 45056 | tf_op jit(solution)/shard_map/reshape | solution.py:403
  2.8 1.4 %reshape.31.from_ref = s32[1,5632]{1,0:T(1,128)} reshape(s32[5632]{0:T(1024)} %param.16) | data formatting | bytes 45056 | tf_op jit(solution)/shard_map/reshape | solution.py:401
  4.1 1.4 %reshape.32.to_ref = s32[1,5632]{1,0:T(1,128)} reshape(s32[5632]{0:T(1024)} %param.17) | data formatting | bytes 45056 | tf_op jit(solution)/shard_map/reshape | solution.py:402
  5.5 1.5 %pack.1 = f32[200,128]{1,0:T(8,128)} custom-call(s32[1,5632]{1,0:T(1,128)} %reshape.31.from_ref, s32[1,5632]{1,0:T(1,128)} %reshape.32.to_ref, f32[1,5632]{1,0:T(1,128)} %reshape.33.susc_ref, f32[64,4096]{1,0:T(8,128)} %bitcast.5), custom_call_target="tpu_custom_call" | custom-call | tf_op jit(solution)/shard_map/pack/pallas_call | solution.py:53
  7.0 0.5 collective-permute-start
  7.5 16.0 %band.1 = (bf16[32,128,256]{2,1,0:T(8,128)(2,1)}, bf16[32,128,256]{2,1,0:T(8,128)(2,1)}) custom-call(s32[1,5632]{1,0:T(1,128)} %reshape.31.from_ref, s32[1,5632]{1,0:T(1,128)} %reshape.32.to_ref, f32[1,5632]{1,0:T(1,128)} %reshape.33.susc_ref, s32[1]{0:T(128)S(6)} %mul.6.base_ref), custom_call_target="tpu_custom_call" | custom-call | flops 11811160064 | bytes 4194304 | tf_op jit(solution)/shard_map/band/pallas_call | solution.py:108
  23.5 0.6 reshape.34.gen_ref
  24.1 0.0 collective-permute-done.1.right_ref
  24.1 0.0 collective-permute-done.left_ref
  24.1 0.0 copy-start.3
  24.1 0.6 copy-done.4
  24.7 0.0 copy-done.3
  24.7 9.3 %resid.1 = (f32[64,4096]{1,0:T(8,128)}, f32[64,128]{1,0:T(8,128)}, f32[64,128]{1,0:T(8,128)}, f32[16,1280]{1,0:T(8,128)}, bf16[128,128]{1,0:T(8,128)(2,1)}, /*index=5*/bf16[128,128]{1,0:T(8,128)(2,1)}, f32[16,128]{1,0:T(8,128)}) custom-call(s32[1]{0:T(128)} %bitcast.place_ref, s32[4]{0:T(128)} %outage_ref.1, f32[64,4096]{1,0:T(8,128)} %bitcast.6, ...), custom_call_target="tpu_custom_call" | custom-call | flops 4294967296 | bytes 8388608 | tf_op jit(solution)/shard_map/resid/pallas_call | solution.py:289
  34.0 1.6 %collective-permute-start.4 = (f32[16,1280]{1,0:T(8,128)}, f32[16,1280]{1,0:T(8,128)S(1)}, u32[]{:S(2)}, u32[]{:S(2)}) collective-permute-start(f32[16,1280]{1,0:T(8,128)} %get-tuple-element.19), channel_id=1, source_target_pairs={{0,1},{1,0},{2,3},{3,2},{4,5},{5,4},{6,7},{7,6},{8,9},{9,8},{10,11... | collective-permute-start | bytes 245768 | tf_op jit(solution)/shard_map/ppermute | solution.py:380
  35.6 3.1 %collective-permute-done.4 = f32[16,1280]{1,0:T(8,128)S(1)} collective-permute-done((f32[16,1280]{1,0:T(8,128)}, f32[16,1280]{1,0:T(8,128)S(1)}, u32[]{:S(2)}, u32[]{:S(2)}) %collective-permute-start.4) | collective-permute-done | bytes 81952 | tf_op jit(solution)/shard_map/ppermute | solution.py:380
  38.7 0.9 %add.18 = f32[16,1280]{1,0:T(8,128)S(1)} add(f32[16,1280]{1,0:T(8,128)} %get-tuple-element.19, f32[16,1280]{1,0:T(8,128)S(1)} %collective-permute-done.4) | non-fusion elementwise | flops 20480 | bytes 245760 | tf_op jit(solution)/shard_map/add | solution.py:380
  39.6 3.9 %collective-permute-start.5 = (f32[16,1280]{1,0:T(8,128)S(1)}, f32[16,1280]{1,0:T(8,128)S(1)}, u32[]{:S(2)}, u32[]{:S(2)}) collective-permute-start(f32[16,1280]{1,0:T(8,128)S(1)} %add.18), channel_id=1, source_target_pairs={{0,3},{1,2},{2,1},{3,0},{4,7},{5,6},{6,5},{7,4},{8,11},{9,10},{10,... | collective-permute-start | bytes 245768 | tf_op jit(solution)/shard_map/ppermute | solution.py:380
  43.5 2.7 %collective-permute-done.5 = f32[16,1280]{1,0:T(8,128)S(1)} collective-permute-done((f32[16,1280]{1,0:T(8,128)S(1)}, f32[16,1280]{1,0:T(8,128)S(1)}, u32[]{:S(2)}, u32[]{:S(2)}) %collective-permute-start.5) | collective-permute-done | bytes 81952 | tf_op jit(solution)/shard_map/ppermute | solution.py:380
  46.2 2.2 %collective-permute-start.6 = (f32[16,1280]{1,0:T(8,128)S(1)}, f32[16,1280]{1,0:T(8,128)S(1)}, u32[]{:S(2)}, u32[]{:S(2)}) collective-permute-start(f32[16,1280]{1,0:T(8,128)S(1)} %add.19), channel_id=1, source_target_pairs={{0,4},{1,5},{2,6},{3,7},{4,0},{5,1},{6,2},{7,3},{8,12},{9,13},{10,... | collective-permute-start | bytes 245768 | tf_op jit(solution)/shard_map/ppermute | solution.py:380
  48.4 3.8 %collective-permute-done.6 = f32[16,1280]{1,0:T(8,128)S(1)} collective-permute-done((f32[16,1280]{1,0:T(8,128)S(1)}, f32[16,1280]{1,0:T(8,128)S(1)}, u32[]{:S(2)}, u32[]{:S(2)}) %collective-permute-start.6) | collective-permute-done | bytes 81952 | tf_op jit(solution)/shard_map/ppermute | solution.py:380
  52.3 2.0 %collective-permute-start.7 = (f32[16,1280]{1,0:T(8,128)S(1)}, f32[16,1280]{1,0:T(8,128)S(1)}, u32[]{:S(2)}, u32[]{:S(2)}) collective-permute-start(f32[16,1280]{1,0:T(8,128)S(1)} %add.20), channel_id=1, source_target_pairs={{0,8},{1,9},{2,10},{3,11},{4,12},{5,13},{6,14},{7,15},{8,0},{9,1},... | collective-permute-start | bytes 245768 | tf_op jit(solution)/shard_map/ppermute | solution.py:380
  54.2 2.5 %collective-permute-done.7 = f32[16,1280]{1,0:T(8,128)S(1)} collective-permute-done((f32[16,1280]{1,0:T(8,128)S(1)}, f32[16,1280]{1,0:T(8,128)S(1)}, u32[]{:S(2)}, u32[]{:S(2)}) %collective-permute-start.7) | collective-permute-done | bytes 81952 | tf_op jit(solution)/shard_map/ppermute | solution.py:380
  56.8 3.5 %collective-permute-start.8 = (f32[16,1280]{1,0:T(8,128)S(1)}, f32[16,1280]{1,0:T(8,128)S(1)}, u32[]{:S(2)}, u32[]{:S(2)}) collective-permute-start(f32[16,1280]{1,0:T(8,128)S(1)} %add.21), channel_id=1, source_target_pairs={{0,16},{1,17},{2,18},{3,19},{4,20},{5,21},{6,22},{7,23},{8,24},{9,... | collective-permute-start | bytes 245768 | tf_op jit(solution)/shard_map/ppermute | solution.py:380
  60.3 0.0 collective-permute-start.2
  60.3 1.7 %collective-permute-start.3 = (f32[64,128]{1,0:T(8,128)}, f32[64,128]{1,0:T(8,128)S(1)}, u32[]{:S(2)}, u32[]{:S(2)}) collective-permute-start(f32[64,128]{1,0:T(8,128)} %get-tuple-element.18), channel_id=1, source_target_pairs={{0,192},{64,0},{128,64},{192,128},{1,193},{65,1},{129,65},{193,129... | collective-permute-start | bytes 98312 | tf_op jit(solution)/shard_map/ppermute | solution.py:374
  62.1 0.7 collective-permute-done.8
  62.8 6.5 %collective-permute-start.9 = (f32[16,1280]{1,0:T(8,128)S(1)}, f32[16,1280]{1,0:T(8,128)S(1)}, u32[]{:S(2)}, u32[]{:S(2)}) collective-permute-start(f32[16,1280]{1,0:T(8,128)S(1)} %add.22), channel_id=1, source_target_pairs={{0,56},{1,57},{2,58},{3,59},{4,60},{5,61},{6,62},{7,63},{8,48},{9,... | collective-permute-start | bytes 245768 | tf_op jit(solution)/shard_map/ppermute | solution.py:380
  69.2 0.6 copy-done.5
  69.8 0.0 copy-done.6
  69.9 6.9 %angles.1 = f32[64,4096]{1,0:T(8,128)} custom-call(f32[64,4096]{1,0:T(8,128)} %get-tuple-element.13.weighted_ref, f32[64,4096]{1,0:T(8,128)} %bitcast.7, f32[16,4096]{1,0:T(8,128)} %reg_ref.1, bf16[32,128,256]{2,1,0:T(8,128)(2,1)} %get-tuple-element.11.high_ref, bf16[32,128,256]{2,1,0:T(8,128)(2,1)} %get-tuple-element.12.low_ref, ...), custom_call_target="tpu_custom_call" | custom-call | flops 4294967296 | bytes 8388608 | tf_op jit(solution)/shard_map/angles/pallas_call | solution.py:360
  76.8 0.7 multiply_subtract_fusion
  (17 shorter events, 0.1 us)
Async XLA Ops:
  1.4 22.7 %collective-permute-start.1 = (f32[64,128]{1,0:T(8,128)S(1)}, f32[64,128]{1,0:T(8,128)S(1)}, u32[]{:S(2)}, u32[]{:S(2)}) collective-permute-start(f32[64,128]{1,0:T(8,128)S(1)} %slice.4), channel_id=1, source_target_pairs={{0,192},{64,0},{128,64},{192,128},{1,193},{65,1},{129,65},{193,129... | collective-permute-start | bytes 98312 | tf_op jit(solution)/shard_map/ppermute | solution.py:374
  7.0 17.1 %collective-permute-start = (f32[200,128]{1,0:T(8,128)}, f32[200,128]{1,0:T(8,128)S(1)}, u32[]{:S(2)}, u32[]{:S(2)}) collective-permute-start(f32[200,128]{1,0:T(8,128)} %pack.1), channel_id=1, source_target_pairs={{0,64},{64,128},{128,192},{192,0},{1,65},{65,129},{129,193},{193,1... | collective-permute-start | bytes 307208 | tf_op jit(solution)/shard_map/ppermute | solution.py:374
  7.5 16.0 %copy-start.2 = (s32[1280]{0:T(1024)S(1)}, s32[1280]{0:T(1024)}, u32[]{:S(2)}) copy-start(s32[1280]{0:T(1024)} %param.19) | copy-start | bytes 15364
  24.1 0.6 copy-start.4
  24.1 0.6 copy-start.3
  34.0 4.7 %collective-permute-start.4 = (f32[16,1280]{1,0:T(8,128)}, f32[16,1280]{1,0:T(8,128)S(1)}, u32[]{:S(2)}, u32[]{:S(2)}) collective-permute-start(f32[16,1280]{1,0:T(8,128)} %get-tuple-element.19), channel_id=1, source_target_pairs={{0,1},{1,0},{2,3},{3,2},{4,5},{5,4},{6,7},{7,6},{8,9},{9,8},{10,11... | collective-permute-start | bytes 245768 | tf_op jit(solution)/shard_map/ppermute | solution.py:380
  39.6 6.6 %collective-permute-start.5 = (f32[16,1280]{1,0:T(8,128)S(1)}, f32[16,1280]{1,0:T(8,128)S(1)}, u32[]{:S(2)}, u32[]{:S(2)}) collective-permute-start(f32[16,1280]{1,0:T(8,128)S(1)} %add.18), channel_id=1, source_target_pairs={{0,3},{1,2},{2,1},{3,0},{4,7},{5,6},{6,5},{7,4},{8,11},{9,10},{10,... | collective-permute-start | bytes 245768 | tf_op jit(solution)/shard_map/ppermute | solution.py:380
  46.2 6.0 %collective-permute-start.6 = (f32[16,1280]{1,0:T(8,128)S(1)}, f32[16,1280]{1,0:T(8,128)S(1)}, u32[]{:S(2)}, u32[]{:S(2)}) collective-permute-start(f32[16,1280]{1,0:T(8,128)S(1)} %add.19), channel_id=1, source_target_pairs={{0,4},{1,5},{2,6},{3,7},{4,0},{5,1},{6,2},{7,3},{8,12},{9,13},{10,... | collective-permute-start | bytes 245768 | tf_op jit(solution)/shard_map/ppermute | solution.py:380
  52.3 4.5 %collective-permute-start.7 = (f32[16,1280]{1,0:T(8,128)S(1)}, f32[16,1280]{1,0:T(8,128)S(1)}, u32[]{:S(2)}, u32[]{:S(2)}) collective-permute-start(f32[16,1280]{1,0:T(8,128)S(1)} %add.20), channel_id=1, source_target_pairs={{0,8},{1,9},{2,10},{3,11},{4,12},{5,13},{6,14},{7,15},{8,0},{9,1},... | collective-permute-start | bytes 245768 | tf_op jit(solution)/shard_map/ppermute | solution.py:380
  56.8 6.0 %collective-permute-start.8 = (f32[16,1280]{1,0:T(8,128)S(1)}, f32[16,1280]{1,0:T(8,128)S(1)}, u32[]{:S(2)}, u32[]{:S(2)}) collective-permute-start(f32[16,1280]{1,0:T(8,128)S(1)} %add.21), channel_id=1, source_target_pairs={{0,16},{1,17},{2,18},{3,19},{4,20},{5,21},{6,22},{7,23},{8,24},{9,... | collective-permute-start | bytes 245768 | tf_op jit(solution)/shard_map/ppermute | solution.py:380
  60.3 8.9 %collective-permute-start.2 = (f32[64,128]{1,0:T(8,128)}, f32[64,128]{1,0:T(8,128)S(1)}, u32[]{:S(2)}, u32[]{:S(2)}) collective-permute-start(f32[64,128]{1,0:T(8,128)} %get-tuple-element.17), channel_id=1, source_target_pairs={{0,64},{64,128},{128,192},{192,0},{1,65},{65,129},{129,193},{193,1... | collective-permute-start | bytes 98312 | tf_op jit(solution)/shard_map/ppermute | solution.py:374
  60.3 8.9 %collective-permute-start.3 = (f32[64,128]{1,0:T(8,128)}, f32[64,128]{1,0:T(8,128)S(1)}, u32[]{:S(2)}, u32[]{:S(2)}) collective-permute-start(f32[64,128]{1,0:T(8,128)} %get-tuple-element.18), channel_id=1, source_target_pairs={{0,192},{64,0},{128,64},{192,128},{1,193},{65,1},{129,65},{193,129... | collective-permute-start | bytes 98312 | tf_op jit(solution)/shard_map/ppermute | solution.py:374
  62.8 14.0 %collective-permute-start.9 = (f32[16,1280]{1,0:T(8,128)S(1)}, f32[16,1280]{1,0:T(8,128)S(1)}, u32[]{:S(2)}, u32[]{:S(2)}) collective-permute-start(f32[16,1280]{1,0:T(8,128)S(1)} %add.22), channel_id=1, source_target_pairs={{0,56},{1,57},{2,58},{3,59},{4,60},{5,61},{6,62},{7,63},{8,48},{9,... | collective-permute-start | bytes 245768 | tf_op jit(solution)/shard_map/ppermute | solution.py:380
  69.2 0.6 copy-start.5
  69.2 0.6 copy-start.6
  69.9 6.9 %copy-start = (f32[16,1280]{1,0:T(8,128)S(1)}, f32[16,1280]{1,0:T(8,128)}, u32[]{:S(2)}) copy-start(f32[16,1280]{1,0:T(8,128)} %dispatch_ref.1) | copy-start | bytes 245764
  69.9 6.9 %copy-start.1 = (f32[16,1280]{1,0:T(8,128)S(1)}, f32[16,1280]{1,0:T(8,128)}, u32[]{:S(2)}) copy-start(f32[16,1280]{1,0:T(8,128)} %param.14) | copy-start | bytes 245764

commit v2 on v1

v2 whole, which is shorter than its diff:
```python
import jax
import jax.numpy as jnp
from jax import lax
from jax.experimental import pallas as pl
from jax.experimental.pallas import tpu as pltpu
from jax.sharding import PartitionSpec as P

BUS_DEV = 4096
BR_DEV = 5632
G_DEV = 1280
RIM = 128
PERIODS = 16
TILES = BUS_DEV // RIM
BR_ROWS = BR_DEV // RIM
PAIRS = TILES // 2
CASES = 4
ROWS = CASES * PERIODS
VMEM_LIMIT = 20 * 1024 * 1024
SLOTS = 256
GROUPS = 64
WORK = 256
BF16 = jnp.bfloat16
F32 = jnp.float32


def split(value):
    high = value.astype(BF16)
    low = (value - high.astype(F32)).astype(BF16)
    return high, low


def dot_last(left, right):
    return lax.dot_general(
        left, right, (((1,), (1,)), ((), ())), preferred_element_type=F32
    )


def dot_plain(left, right):
    return jnp.dot(left, right, preferred_element_type=F32)


def whole(ref_space=pltpu.VMEM):
    return pl.BlockSpec(memory_space=ref_space)


def one_hot(rows, index):
    spots = lax.broadcasted_iota(jnp.int32, (rows, index.shape[1]), 0)
    return spots == index


def ones_at(mask):
    return jnp.where(mask, 1.0, 0.0).astype(BF16)


def held_at(mask, values):
    return jnp.where(mask, values, 0.0).astype(BF16)


def parts_of(values):
    high = values.astype(BF16).astype(F32)
    return high, values - high


def as_row(ref):
    return ref[...].reshape(1, ref.shape[0])


def pack_kernel(from_ref, to_ref, susc_ref, last_ref, lead_ref, out_ref, first_ref):
    for part, ref in enumerate((from_ref, to_ref, susc_ref)):
        row = as_row(ref).astype(F32)
        for k in range(BR_ROWS):
            at = part * BR_ROWS + k
            out_ref[at : at + 1, :] = row[:, k * RIM : (k + 1) * RIM]
    out_ref[136:200, :] = last_ref[...]
    first_ref[...] = lead_ref[...]


def pack(from_bus, to_bus, susceptance, field):
    row = pl.BlockSpec((BR_DEV,), lambda i: (0,))
    return pl.pallas_call(
        pack_kernel,
        grid=(1,),
        in_specs=[
            row,
            row,
            row,
            pl.BlockSpec((ROWS, RIM), lambda i: (0, TILES - 1)),
            pl.BlockSpec((ROWS, RIM), lambda i: (0, 0)),
        ],
        out_specs=[whole(), whole()],
        out_shape=[pltpu.VMEM((200, RIM), F32), pltpu.VMEM((ROWS, RIM), F32)],
        compiler_params=pltpu.CompilerParams(vmem_limit_bytes=4 << 20),
        name="pack",
    )(from_bus, to_bus, susceptance, field, field)


def tile_of_group(starts_row, to_row, high_row, low_row):
    starts = ones_at(one_hot(RIM, starts_row))
    hit = one_hot(RIM, to_row)
    ends = jnp.concatenate([held_at(hit, high_row), held_at(hit, low_row)], axis=0)
    both = dot_last(starts, ends)
    return both[:, :RIM] + both[:, RIM:]


def band_kernel(
    base_ref, from_ref, to_ref, susc_ref, high_ref, low_ref, degree_ref, tiles, table
):
    base = base_ref[0] * BUS_DEV
    from_local = as_row(from_ref) - base
    tile = from_local // RIM
    tile_hit = one_hot(TILES, tile)
    member = jnp.where(tile_hit, 1.0, 0.0)
    packed = member.astype(BF16)
    chunks = BR_DEV // WORK
    rows = lax.broadcasted_iota(jnp.int32, (WORK, WORK), 0)
    cols = lax.broadcasted_iota(jnp.int32, (WORK, WORK), 1)
    upto = jnp.where(rows <= cols, 1.0, 0.0).astype(BF16)
    counts = dot_plain(
        jnp.concatenate([packed[:, c * WORK : (c + 1) * WORK] for c in range(chunks)], axis=0),
        upto,
    )
    seen = jnp.zeros((TILES, 1), F32)
    ranks = []
    for c in range(chunks):
        local = counts[c * TILES : (c + 1) * TILES]
        part = member[:, c * WORK : (c + 1) * WORK] * (local + seen)
        ranks.append(jnp.sum(part, axis=0, keepdims=True) - 1.0)
        seen = seen + local[:, WORK - 1 : WORK]
    rank = jnp.concatenate(ranks, axis=1).astype(jnp.int32)

    extra = jnp.maximum((seen.astype(jnp.int32) + (SLOTS - 1)) // SLOTS - 1, 0).astype(F32)
    sub = lax.broadcasted_iota(jnp.int32, (TILES, RIM), 0)
    lane = lax.broadcasted_iota(jnp.int32, (TILES, RIM), 1)
    extra_row = jnp.sum(jnp.where(sub == lane, extra, 0.0), axis=0, keepdims=True)
    extra_from = jnp.sum(jnp.where(lane < sub, extra_row, 0.0), axis=1, keepdims=True)
    extra_upto = extra_from + extra
    spill = jnp.sum(extra).astype(jnp.int32)
    spill_at = jnp.sum(member * extra_from, axis=0, keepdims=True).astype(jnp.int32)
    group = jnp.where(rank < SLOTS, tile, TILES + spill_at + rank // SLOTS - 1)
    group_hit = one_hot(GROUPS, group)
    slot_hit = ones_at(one_hot(SLOTS, rank % SLOTS))
    susc_high, susc_low = parts_of(as_row(susc_ref))
    features = (
        (from_local % RIM).astype(F32),
        ((as_row(to_ref) - base) % RIM).astype(F32),
        susc_high,
        susc_low,
    )
    table[...] = dot_last(
        jnp.concatenate([held_at(group_hit, value) for value in features], axis=0), slot_hit
    )

    def group_tile(at):
        rows = [table[pl.ds(part * GROUPS + at, 1), :] for part in range(4)]
        return tile_of_group(rows[0].astype(jnp.int32), rows[1].astype(jnp.int32), *rows[2:])

    for at in range(TILES):
        tiles[at] = group_tile(at)

    @pl.loop(0, spill)
    def _(step):
        passed = jnp.where(extra_upto <= step.astype(F32), 1.0, 0.0)
        owner = jnp.sum(passed).astype(jnp.int32)
        tiles[owner] = tiles[owner] + group_tile(TILES + step)

    rows = lax.broadcasted_iota(jnp.int32, (RIM, RIM), 0)
    cols = lax.broadcasted_iota(jnp.int32, (RIM, RIM), 1)
    zero = jnp.zeros((RIM, RIM), BF16)
    carried = jnp.zeros((1, RIM), F32)
    for at in range(TILES):
        pair, odd = at // 2, at % 2
        block = tiles[at]
        turned = block.T
        inside = jnp.where(cols > rows, block, jnp.where(cols < rows, turned, 0.0))
        ahead = jnp.where(cols > rows, 0.0, block)
        back = jnp.where(cols < rows, 0.0, turned)
        own = slice((1 + odd) * RIM, (2 + odd) * RIM)
        mine = slice(odd * RIM, (odd + 1) * RIM)
        other = slice((1 - odd) * RIM, (2 - odd) * RIM)
        for ref, kind in ((high_ref, 0), (low_ref, 1)):
            inside_part = split(inside)[kind]
            ahead_part = split(ahead)[kind]
            back_part = split(back)[kind]
            ref[pair, own, mine] = inside_part
            if odd == 0:
                ref[pair, 2 * RIM : 3 * RIM, mine] = back_part
                ref[pair, 3 * RIM :, mine] = zero
                ref[pair, RIM : 2 * RIM, other] = ahead_part
                if pair == 0:
                    ref[pair, :RIM, mine] = zero
            else:
                ref[pair, 3 * RIM :, mine] = back_part
                ref[pair, :RIM, mine] = zero
                if pair + 1 < PAIRS:
                    ref[pair + 1, :RIM, :RIM] = ahead_part
        degree_ref[:, at * RIM : (at + 1) * RIM] = (
            jnp.sum(inside, axis=0, keepdims=True)
            + jnp.sum(back, axis=0, keepdims=True)
            + carried
        )
        carried = jnp.sum(ahead, axis=0, keepdims=True)


def build_band(place, from_bus, to_bus, susceptance):
    shape = pltpu.VMEM((PAIRS, 4 * RIM, 2 * RIM), BF16)
    return pl.pallas_call(
        band_kernel,
        in_specs=[whole(pltpu.SMEM)] + [whole()] * 3,
        out_specs=[whole()] * 3,
        out_shape=[shape, shape, pltpu.VMEM((1, BUS_DEV), F32)],
        scratch_shapes=[
            pltpu.VMEM((TILES, RIM, RIM), F32),
            pltpu.VMEM((4 * GROUPS, SLOTS), F32),
        ],
        compiler_params=pltpu.CompilerParams(vmem_limit_bytes=VMEM_LIMIT),
        cost_estimate=pl.CostEstimate(flops=8 << 30, bytes_accessed=16 << 20, transcendentals=0),
        name="band",
    )(place, from_bus, to_bus, susceptance)


def outage_row(from_at, to_at, start, width):
    spots = lax.broadcasted_iota(jnp.int32, (1, width), 1) + start
    return jnp.where(spots == from_at, 1.0, 0.0) - jnp.where(spots == to_at, 1.0, 0.0)


def apply_pairs(halo, inner, stacks, high_ref, low_ref, cross, degrees, ends, susc, emit):
    flows = [jnp.zeros((PERIODS, RIM), F32) for _ in range(CASES)]
    for tile in range(-1, TILES + 1):
        value = halo(tile) if tile in (-1, TILES) else inner(tile * RIM, RIM)
        high, low = split(value)
        cols = slice((tile + 1) * RIM, (tile + 2) * RIM)
        stacks[:ROWS, cols] = high
        stacks[ROWS:, cols] = low
        for case in range(CASES):
            mask = outage_row(*ends[case], (tile + 1) * RIM, RIM)
            flows[case] += value[case * PERIODS : (case + 1) * PERIODS] * mask
    drops = [
        susc[case] * jnp.sum(flows[case], axis=1, keepdims=True) for case in range(CASES)
    ]
    width = 2 * RIM
    for pair in range(PAIRS):
        near = stacks[:, pair * width : pair * width + 2 * width]
        sums = dot_plain(near, high_ref[pair]) + dot_plain(near, low_ref[pair])
        sums = sums[:ROWS] + sums[ROWS:]
        if pair == 0:
            outer = dot_plain(stacks[:, :RIM], cross)
            outer = outer[:ROWS] + outer[ROWS:]
            outer = outer[:, :RIM] + outer[:, RIM:]
            sums = sums + jnp.concatenate([outer, jnp.zeros((ROWS, RIM), F32)], axis=1)
        cols = slice(pair * width, (pair + 1) * width)
        result = degrees(cols) * inner(pair * width, width) - sums
        parts = []
        for case in range(CASES):
            mask = outage_row(*ends[case], pair * width + RIM, width)
            parts.append(result[case * PERIODS : (case + 1) * PERIODS] - drops[case] * mask)
        emit(pair, cols, jnp.concatenate(parts, axis=0))


def resid_kernel(
    place_ref,
    outage_ref,
    field_ref,
    barrier_ref,
    high_ref,
    low_ref,
    own_degree_ref,
    from_ref,
    to_ref,
    susc_ref,
    left_ref,
    right_ref,
    dispatch_ref,
    gen_ref,
    weighted_ref,
    first_ref,
    last_ref,
    partial_ref,
    cross_ref,
    degree_ref,
    ends_ref,
    stacks,
    inject,
    total,
):
    block = place_ref[0]
    base = block * BUS_DEV
    keep = jnp.where(block > 0, 1.0, 0.0)
    left_rows = [
        jnp.concatenate(
            [left_ref[part * BR_ROWS + k : part * BR_ROWS + k + 1] for k in range(BR_ROWS)],
            axis=1,
        )
        for part in range(3)
    ]
    left_from = left_rows[0].astype(jnp.int32)
    left_to = left_rows[1].astype(jnp.int32)
    left_susc = left_rows[2] * keep
    high, low = parts_of(jnp.where(left_to >= base, left_susc, 0.0))
    hit = one_hot(RIM, (left_to - base) % RIM)
    left_ends = jnp.concatenate([held_at(hit, high), held_at(hit, low)], axis=0)
    both = dot_last(ones_at(one_hot(RIM, left_from - (base - RIM))), left_ends)
    across = both[:, :RIM] + both[:, RIM:]
    cross = jnp.concatenate(split(across), axis=1)
    cross_ref[...] = cross
    degree_ref[...] = own_degree_ref[...]
    degree_ref[:, :RIM] = own_degree_ref[:, :RIM] + jnp.sum(across, axis=0, keepdims=True)

    branch = lax.broadcasted_iota(jnp.int32, (1, BR_DEV), 1)
    own_rows = [as_row(from_ref).astype(F32), as_row(to_ref).astype(F32), as_row(susc_ref)]
    left_rows = [left_rows[0] * keep, left_rows[1] * keep, left_susc]
    ends, susc = [], []
    for case in range(CASES):
        own_hit = branch == outage_ref[case] - block * BR_DEV
        left_hit = branch == outage_ref[case] - (block - 1) * BR_DEV
        start, end, value = [
            jnp.sum(
                jnp.where(own_hit, own, 0.0) + jnp.where(left_hit, left, 0.0),
                axis=1,
                keepdims=True,
            )
            for own, left in zip(own_rows, left_rows)
        ]
        ends.append(
            (start.astype(jnp.int32) - base + RIM, end.astype(jnp.int32) - base + RIM)
        )
        susc.append(value)
        for k, held in enumerate((*ends[case], value)):
            at = 4 * k + case
            ends_ref[at : at + 1, :] = jnp.broadcast_to(held.astype(F32), (1, RIM))

    gen = as_row(gen_ref) - base
    gen_tile = gen // RIM
    gen_spots = ones_at(one_hot(RIM, gen % RIM))
    dispatch_parts = parts_of(dispatch_ref[...])
    share = TILES // 4
    for part in range(4):
        tiles = range(part * share, (part + 1) * share)
        picked = jnp.concatenate(
            [held_at(gen_tile == tile, value) for value in dispatch_parts for tile in tiles],
            axis=0,
        )
        spread = dot_last(picked, gen_spots)
        half = spread.shape[0] // 2
        inject[part * half : (part + 1) * half] = spread[:half] + spread[half:]

    def halo(tile):
        return left_ref[136:200] if tile < 0 else right_ref[...]

    def inner(start, width):
        return field_ref[:, start : start + width]

    def emit(pair, cols, result):
        rows = [slice((2 * pair + k) * PERIODS, (2 * pair + k + 1) * PERIODS) for k in (0, 1)]
        taken = jnp.concatenate([inject[rows[0]], inject[rows[1]]], axis=1)
        resid = result - jnp.concatenate([taken] * CASES, axis=0)
        weighted = barrier_ref[:, cols].astype(F32) * resid
        weighted_ref[:, cols] = weighted
        if pair == 0:
            first_ref[...] = weighted[:, :RIM]
        if pair == PAIRS - 1:
            last_ref[...] = weighted[:, RIM:]
        summed = weighted[0:16] + weighted[16:32] + (weighted[32:48] + weighted[48:64])
        total[rows[0]] = summed[:, :RIM]
        total[rows[1]] = summed[:, RIM:]

    def degrees(cols):
        return degree_ref[:, cols]

    apply_pairs(halo, inner, stacks, high_ref, low_ref, cross, degrees, ends, susc, emit)

    at_gens = jnp.zeros((PERIODS, G_DEV), F32)
    size = share * PERIODS
    for part in range(4):
        high, low = split(total[part * size : (part + 1) * size])
        both = dot_plain(jnp.concatenate([high, low], axis=0), gen_spots)
        for k in range(share):
            rows = slice(k * PERIODS, (k + 1) * PERIODS)
            value = both[rows] + both[size + k * PERIODS : size + (k + 1) * PERIODS]
            at_gens += jnp.where(gen_tile == part * share + k, value, 0.0)
    partial_ref[...] = at_gens


def residuals(place, outage, field, barrier, band, raw, halos, dispatch, gen_bus):
    tile = pltpu.VMEM((ROWS, RIM), F32)
    return pl.pallas_call(
        resid_kernel,
        in_specs=[whole(pltpu.SMEM)] * 2 + [whole()] * 12,
        out_specs=[whole()] * 7,
        out_shape=[
            pltpu.VMEM((ROWS, BUS_DEV), F32),
            tile,
            tile,
            pltpu.VMEM((PERIODS, G_DEV), F32),
            pltpu.VMEM((RIM, 2 * RIM), BF16),
            pltpu.VMEM((1, BUS_DEV), F32),
            pltpu.VMEM((16, RIM), F32),
        ],
        scratch_shapes=[
            pltpu.VMEM((2 * ROWS, BUS_DEV + 2 * RIM), BF16),
            pltpu.VMEM((TILES * PERIODS, RIM), F32),
            pltpu.VMEM((TILES * PERIODS, RIM), F32),
        ],
        compiler_params=pltpu.CompilerParams(vmem_limit_bytes=VMEM_LIMIT),
        cost_estimate=pl.CostEstimate(flops=4 << 30, bytes_accessed=8 << 20, transcendentals=0),
        name="resid",
    )(place, outage, field, barrier, *band, *raw, *halos, dispatch, gen_bus)


def angle_kernel(
    weighted_ref,
    field_ref,
    reg_ref,
    high_ref,
    low_ref,
    cross_ref,
    degree_ref,
    ends_ref,
    left_ref,
    right_ref,
    out_ref,
    stacks,
):
    ends, susc = [], []
    for case in range(CASES):
        held = [ends_ref[4 * k + case : 4 * k + case + 1, 0:1] for k in range(3)]
        ends.append((held[0].astype(jnp.int32), held[1].astype(jnp.int32)))
        susc.append(held[2])

    def halo(tile):
        return left_ref[...] if tile < 0 else right_ref[...]

    def inner(start, width):
        return weighted_ref[:, start : start + width]

    def emit(pair, cols, result):
        scale = jnp.concatenate([reg_ref[:, cols]] * CASES, axis=0)
        out_ref[:, cols] = result + scale * field_ref[:, cols]

    def degrees(cols):
        return degree_ref[:, cols]

    apply_pairs(
        halo, inner, stacks, high_ref, low_ref, cross_ref[...], degrees, ends, susc, emit
    )


def angles(weighted, field, reg, band, cross, degree, ends, halos):
    return pl.pallas_call(
        angle_kernel,
        in_specs=[whole()] * 10,
        out_specs=whole(),
        out_shape=jax.ShapeDtypeStruct((ROWS, BUS_DEV), F32),
        scratch_shapes=[pltpu.VMEM((2 * ROWS, BUS_DEV + 2 * RIM), BF16)],
        compiler_params=pltpu.CompilerParams(vmem_limit_bytes=VMEM_LIMIT),
        cost_estimate=pl.CostEstimate(flops=4 << 30, bytes_accessed=8 << 20, transcendentals=0),
        name="angles",
    )(weighted, field, reg, *band, cross, degree, ends, *halos)


def shifted(block, distance):
    size = lax.axis_size("net")
    return lax.ppermute(block, "net", [(i, (i + distance) % size) for i in range(size)])


def sum_cases(value):
    size = lax.axis_size("ctg")
    for mask in (1, 3, 4, 8, 16, 56):
        value = value + lax.ppermute(value, "ctg", [(i, i ^ mask) for i in range(size)])
    return value


def body(
    angle_dir,
    dispatch_dir,
    barrier,
    angle_reg,
    dispatch_reg,
    susceptance,
    from_bus,
    to_bus,
    outage,
    gen_bus,
):
    block = lax.axis_index("net")
    place = jnp.reshape(block, (1,)).astype(jnp.int32)
    field = angle_dir.reshape(ROWS, BUS_DEV)
    weights = barrier.reshape(ROWS, BUS_DEV)
    raw = (from_bus, to_bus, susceptance)
    packed, lead = pack(*raw, field)
    left = shifted(packed, 1)
    right = shifted(lead, -1)
    high, low, own_degree = build_band(place, *raw)
    weighted, first, last, partial, cross, degree, ends = residuals(
        place,
        outage,
        field,
        weights,
        (high, low, own_degree),
        raw,
        (left, right),
        dispatch_dir,
        gen_bus,
    )
    halos = (shifted(last, 1), shifted(first, -1))
    summed = sum_cases(partial)
    angle_out = angles(
        weighted, field, angle_reg, (high, low), cross, degree, ends, halos
    )
    case_count = float(CASES * lax.axis_size("ctg"))
    dispatch_out = dispatch_reg * dispatch_dir - summed / case_count
    return (angle_out.reshape(angle_dir.shape), dispatch_out)


def solution(mesh):
    placed = (
        P("ctg", None, "net"),
        P(None, "net"),
        P("ctg", None, "net"),
        P(None, "net"),
        P(None, "net"),
        P("net"),
        P("net"),
        P("net"),
        P("ctg"),
        P("net"),
    )
    return jax.shard_map(
        body,
        mesh=mesh,
        in_specs=placed,
        out_specs=(P("ctg", None, "net"), P(None, "net")),
        check_vma=False,
    )
```

time: 78.2 us -> 57.1 us (0.73)
  Pallas kernels: 33.7 us -> 14 us
  local copies, waits for them, and re-layouts: 6.72 us -> 5.67 us
  other arithmetic: 1.6 us -> 0.72 us
    pallas_call x1, Pallas kernels: 16 us -> 6.32 us  [build_band(): pl.pallas_call(band_kernel, in_specs=[whole(pltpu.SMEM)] + [whole()] * 3,...]
    reshape x4 -> x0, local copies, waits for them, and re-layouts: 4.69 us -> none  [the longest x1 1.37 us: body(): susceptance.reshape(1, BR_DEV)]
    unnamed x14 -> x28, local copies, waits for them, and re-layouts: 1.28 us -> 5.67 us
    pallas_call x1, Pallas kernels: 9.31 us -> 4.99 us  [residuals(): pl.pallas_call(resid_kernel, in_specs=[whole(pltpu.SMEM)] * 2 + [whole()]...]
    pallas_call x1, Pallas kernels: 6.88 us -> 2.63 us  [angles(): pl.pallas_call(angle_kernel, in_specs=[whole()] * 10, out_specs=whole(),...]
    pallas_call x1, Pallas kernels: 1.48 us -> 0.05 us  [pack(): pl.pallas_call(pack_kernel, grid=(1,), in_specs=[row, row, row, pl.BlockS...]
    add x5, other arithmetic: 0.94 us -> 0.06 us  [sum_cases(): value + lax.ppermute(value, 'ctg', [(i, i ^ mask) for i in range(size)])]
    ppermute x6, starting transfers between devices: 19.6 us -> 18.9 us  [sum_cases(): lax.ppermute(value, 'ctg', [(i, i ^ mask) for i in range(size)])]
  transfers between devices with their start and end apart: 10 -> 10, of which waited for: 5 -> 6; matrix products, arithmetic and copies ran while one was open for 6% -> 0% of each run, Pallas kernels for 31% -> 16%
where the time goes in v2:
time: 57.1 us; the launch traced here: 56 us
  starting transfers between devices  21.2 us (37%)
  Pallas kernels  14 us (25%)
  waiting for transfers between devices  13.6 us (24%)
  local copies, waits for them, and re-layouts  5.67 us (10%)
  between operations  0.77 us (1%)
  other arithmetic  0.72 us (1%)
    ppermute x6, starting transfers between devices, sum_cases(): lax.ppermute(value, 'ctg', [(i, i ^ mask) for i in range(size)])  18.9 us
    ppermute x6, waiting for transfers between devices, sum_cases(): lax.ppermute(value, 'ctg', [(i, i ^ mask) for i in range(size)])  13.6 us
    pallas_call x1, Pallas kernels, build_band(): pl.pallas_call(band_kernel, in_specs=[whole(pltpu.SMEM)] + [whole()] * 3,...  6.32 us
    unnamed x28, local copies, waits for them, and re-layouts  5.67 us
    pallas_call x1, Pallas kernels, residuals(): pl.pallas_call(resid_kernel, in_specs=[whole(pltpu.SMEM)] * 2 + [whole()]...  4.99 us
    pallas_call x1, Pallas kernels, angles(): pl.pallas_call(angle_kernel, in_specs=[whole()] * 10, out_specs=whole(),...  2.63 us
    ppermute x4, starting transfers between devices, shifted(): lax.ppermute(block, 'net', [(i, (i + distance) % size) for i in range(siz...  2.32 us
  transfers between devices with their start and end apart: 10, of which 6 were waited for; matrix products, arithmetic and copies ran while one was open for 0% of the time, Pallas kernels for 16%

profile of v2, /device:TPU:2, one launch (start us, length us, event | category | flops | bytes accessed | tf_op | source)
XLA Modules:
  0.0 56.0 jit_solution(4334775147301619157)
XLA Ops:
  0.6 0.0 copy-start
  0.6 1.2 %copy-done = f32[4,16,4096]{2,1,0:T(8,128)S(1)} copy-done((f32[4,16,4096]{2,1,0:T(8,128)S(1)}, f32[4,16,4096]{2,1,0:T(8,128)}, u32[]{:S(2)}) %copy-start) | copy-done | bytes 1048600
  1.9 0.7 %copy-done.3 = s32[5632]{0:T(1024)S(1)} copy-done((s32[5632]{0:T(1024)S(1)}, s32[5632]{0:T(1024)}, u32[]{:S(2)}) %copy-start.3) | copy-done | bytes 22552
  2.6 0.7 %copy-done.5 = s32[5632]{0:T(1024)S(1)} copy-done((s32[5632]{0:T(1024)S(1)}, s32[5632]{0:T(1024)}, u32[]{:S(2)}) %copy-start.5) | copy-done | bytes 22552
  3.3 0.7 %copy-done.7 = f32[5632]{0:T(1024)S(1)} copy-done((f32[5632]{0:T(1024)S(1)}, f32[5632]{0:T(1024)}, u32[]{:S(2)}) %copy-start.7) | copy-done | bytes 22552
  4.1 0.1 pack.1
  4.1 0.1 collective-permute-start.1
  4.2 0.5 collective-permute-start
  4.7 0.7 %copy-done.4 = s32[5632]{0:T(1024)S(1)} copy-done((s32[5632]{0:T(1024)S(1)}, s32[5632]{0:T(1024)}, u32[]{:S(2)}) %copy-start.4) | copy-done | bytes 22552
  5.5 0.7 %copy-done.6 = s32[5632]{0:T(1024)S(1)} copy-done((s32[5632]{0:T(1024)S(1)}, s32[5632]{0:T(1024)}, u32[]{:S(2)}) %copy-start.6) | copy-done | bytes 22552
  6.2 0.7 %copy-done.8 = f32[5632]{0:T(1024)S(1)} copy-done((f32[5632]{0:T(1024)S(1)}, f32[5632]{0:T(1024)}, u32[]{:S(2)}) %copy-start.8) | copy-done | bytes 22552
  6.9 0.0 copy-start.12
  6.9 6.3 %band.1 = (bf16[16,512,256]{2,1,0:T(8,128)(2,1)S(1)}, bf16[16,512,256]{2,1,0:T(8,128)(2,1)S(1)}, f32[1,4096]{1,0:T(1,128)S(1)}) custom-call(s32[1]{0:T(128)} %bitcast.base_ref.place_ref, s32[5632]{0:T(1024)S(1)} %copy-done.4, s32[5632]{0:T(1024)S(1)} %copy-done.6, f32[5632]{0:T(1024)S(1)} %copy-done.8), custom_call_target="tpu_custom_call" | custom-call | flops 8589934592 | bytes 16777216 | tf_op jit(solution)/shard_map/band/pallas_call | solution.py:206
  13.3 0.0 collective-permute-done.1.right_ref
  13.3 0.0 copy-start.10
  13.4 5.0 %resid.1 = (f32[64,4096]{1,0:T(8,128)S(1)}, f32[64,128]{1,0:T(8,128)S(1)}, f32[64,128]{1,0:T(8,128)S(1)}, f32[16,1280]{1,0:T(8,128)S(1)}, bf16[128,256]{1,0:T(8,...) custom-call(s32[1]{0:T(128)} %bitcast.base_ref.place_ref, s32[4]{0:T(128)S(1)} %copy-done.12, ...), custom_call_target="tpu_custom_call" | custom-call | flops 4294967296 | bytes 8388608 | tf_op jit(solution)/shard_map/resid/pallas_call | solution.py:385
  18.4 1.8 %collective-permute-start.4 = (f32[16,1280]{1,0:T(8,128)S(1)}, f32[16,1280]{1,0:T(8,128)S(1)}, u32[]{:S(2)}, u32[]{:S(2)}) collective-permute-start(f32[16,1280]{1,0:T(8,128)S(1)} %get-tuple-element.25), channel_id=1, source_target_pairs={{0,1},{1,0},{2,3},{3,2},{4,5},{5,4},{6,7},{7,6},{8,9},{9,8},{10,11... | collective-permute-start | bytes 245768 | tf_op jit(solution)/shard_map/ppermute | solution.py:468
  20.2 2.9 %collective-permute-done.4 = f32[16,1280]{1,0:T(8,128)S(1)} collective-permute-done((f32[16,1280]{1,0:T(8,128)S(1)}, f32[16,1280]{1,0:T(8,128)S(1)}, u32[]{:S(2)}, u32[]{:S(2)}) %collective-permute-start.4) | collective-permute-done | bytes 81952 | tf_op jit(solution)/shard_map/ppermute | solution.py:468
  23.1 3.7 %collective-permute-start.5 = (f32[16,1280]{1,0:T(8,128)S(1)}, f32[16,1280]{1,0:T(8,128)S(1)}, u32[]{:S(2)}, u32[]{:S(2)}) collective-permute-start(f32[16,1280]{1,0:T(8,128)S(1)} %add.18), channel_id=1, source_target_pairs={{0,3},{1,2},{2,1},{3,0},{4,7},{5,6},{6,5},{7,4},{8,11},{9,10},{10,... | collective-permute-start | bytes 245768 | tf_op jit(solution)/shard_map/ppermute | solution.py:468
  26.7 3.0 %collective-permute-done.5 = f32[16,1280]{1,0:T(8,128)S(1)} collective-permute-done((f32[16,1280]{1,0:T(8,128)S(1)}, f32[16,1280]{1,0:T(8,128)S(1)}, u32[]{:S(2)}, u32[]{:S(2)}) %collective-permute-start.5) | collective-permute-done | bytes 81952 | tf_op jit(solution)/shard_map/ppermute | solution.py:468
  29.8 1.9 %collective-permute-start.6 = (f32[16,1280]{1,0:T(8,128)S(1)}, f32[16,1280]{1,0:T(8,128)S(1)}, u32[]{:S(2)}, u32[]{:S(2)}) collective-permute-start(f32[16,1280]{1,0:T(8,128)S(1)} %add.19), channel_id=1, source_target_pairs={{0,4},{1,5},{2,6},{3,7},{4,0},{5,1},{6,2},{7,3},{8,12},{9,13},{10,... | collective-permute-start | bytes 245768 | tf_op jit(solution)/shard_map/ppermute | solution.py:468
  31.7 4.1 %collective-permute-done.6 = f32[16,1280]{1,0:T(8,128)S(1)} collective-permute-done((f32[16,1280]{1,0:T(8,128)S(1)}, f32[16,1280]{1,0:T(8,128)S(1)}, u32[]{:S(2)}, u32[]{:S(2)}) %collective-permute-start.6) | collective-permute-done | bytes 81952 | tf_op jit(solution)/shard_map/ppermute | solution.py:468
  35.8 1.7 %collective-permute-start.7 = (f32[16,1280]{1,0:T(8,128)S(1)}, f32[16,1280]{1,0:T(8,128)S(1)}, u32[]{:S(2)}, u32[]{:S(2)}) collective-permute-start(f32[16,1280]{1,0:T(8,128)S(1)} %add.20), channel_id=1, source_target_pairs={{0,8},{1,9},{2,10},{3,11},{4,12},{5,13},{6,14},{7,15},{8,0},{9,1},... | collective-permute-start | bytes 245768 | tf_op jit(solution)/shard_map/ppermute | solution.py:468
  37.6 2.8 %collective-permute-done.7 = f32[16,1280]{1,0:T(8,128)S(1)} collective-permute-done((f32[16,1280]{1,0:T(8,128)S(1)}, f32[16,1280]{1,0:T(8,128)S(1)}, u32[]{:S(2)}, u32[]{:S(2)}) %collective-permute-start.7) | collective-permute-done | bytes 81952 | tf_op jit(solution)/shard_map/ppermute | solution.py:468
  40.4 3.2 %collective-permute-start.8 = (f32[16,1280]{1,0:T(8,128)S(1)}, f32[16,1280]{1,0:T(8,128)S(1)}, u32[]{:S(2)}, u32[]{:S(2)}) collective-permute-start(f32[16,1280]{1,0:T(8,128)S(1)} %add.21), channel_id=1, source_target_pairs={{0,16},{1,17},{2,18},{3,19},{4,20},{5,21},{6,22},{7,23},{8,24},{9,... | collective-permute-start | bytes 245768 | tf_op jit(solution)/shard_map/ppermute | solution.py:468
  43.5 1.7 %collective-permute-start.3 = (f32[64,128]{1,0:T(8,128)S(1)}, f32[64,128]{1,0:T(8,128)S(1)}, u32[]{:S(2)}, u32[]{:S(2)}) collective-permute-start(f32[64,128]{1,0:T(8,128)S(1)} %get-tuple-element.24), channel_id=1, source_target_pairs={{0,192},{64,0},{128,64},{192,128},{1,193},{65,1},{129,65},{193,129... | collective-permute-start | bytes 98312 | tf_op jit(solution)/shard_map/ppermute | solution.py:462
  45.3 0.7 %collective-permute-done.8 = f32[16,1280]{1,0:T(8,128)S(1)} collective-permute-done((f32[16,1280]{1,0:T(8,128)S(1)}, f32[16,1280]{1,0:T(8,128)S(1)}, u32[]{:S(2)}, u32[]{:S(2)}) %collective-permute-start.8) | collective-permute-done | bytes 81952 | tf_op jit(solution)/shard_map/ppermute | solution.py:468
  46.0 6.5 %collective-permute-start.9 = (f32[16,1280]{1,0:T(8,128)S(1)}, f32[16,1280]{1,0:T(8,128)S(1)}, u32[]{:S(2)}, u32[]{:S(2)}) collective-permute-start(f32[16,1280]{1,0:T(8,128)S(1)} %add.22), channel_id=1, source_target_pairs={{0,56},{1,57},{2,58},{3,59},{4,60},{5,61},{6,62},{7,63},{8,48},{9,... | collective-permute-start | bytes 245768 | tf_op jit(solution)/shard_map/ppermute | solution.py:468
  52.5 0.0 copy-start.13
  52.5 2.6 %angles.1 = f32[64,4096]{1,0:T(8,128)} custom-call(f32[64,4096]{1,0:T(8,128)S(1)} %get-tuple-element.19.weighted_ref, f32[64,4096]{1,0:T(8,128)S(1)} %bitcast.7, f32[16,4096]{1,0:T(8,128)S(1)} %copy-done.10, bf16[16,512,256]{2,1,0:T(8,128)(2,1)S(1)} %get-tuple-element.14.high_ref, bf16[16,512,256]{2,1,0:T(8,128)(2,1)S(1)} %get-tuple-element.15.low_ref, ...), custom_call_target="tpu_custom_call" | custom-call | flops 4294967296 | bytes 8388608 | tf_op jit(solution)/shard_map/angles/pallas_call | solution.py:448
  55.1 0.2 collective-permute-done.9
  55.3 0.7 %multiply_subtract_fusion = f32[16,1280]{1,0:T(8,128)} fusion(f32[16,1280]{1,0:T(8,128)S(1)} %add.22, f32[16,1280]{1,0:T(8,128)S(1)} %collective-permute-done.9, f32[16,1280]{1,0:T(8,128)S(1)} %copy-done.13, f32[16,1280]{1,0:T(8,128)S(1)} %copy-done.2), kind=kLoop, calls=%fused_computation | loop fusion | flops 81920 | bytes 409600 | tf_op jit(solution)/shard_map/sub | solution.py:510
  (26 shorter events, 0.1 us)
Async XLA Ops:
  0.6 1.2 %copy-start = (f32[4,16,4096]{2,1,0:T(8,128)S(1)}, f32[4,16,4096]{2,1,0:T(8,128)}, u32[]{:S(2)}) copy-start(f32[4,16,4096]{2,1,0:T(8,128)} %param.10) | copy-start | bytes 3145732
  1.9 0.7 %copy-start.3 = (s32[5632]{0:T(1024)S(1)}, s32[5632]{0:T(1024)}, u32[]{:S(2)}) copy-start(s32[5632]{0:T(1024)} %from_ref.5) | copy-start | bytes 67588
  2.6 0.7 %copy-start.5 = (s32[5632]{0:T(1024)S(1)}, s32[5632]{0:T(1024)}, u32[]{:S(2)}) copy-start(s32[5632]{0:T(1024)} %to_ref.5) | copy-start | bytes 67588
  3.3 0.7 %copy-start.7 = (f32[5632]{0:T(1024)S(1)}, f32[5632]{0:T(1024)}, u32[]{:S(2)}) copy-start(f32[5632]{0:T(1024)} %susc_ref.5) | copy-start | bytes 67588
  4.1 9.2 %collective-permute-start.1 = (f32[64,128]{1,0:T(8,128)S(1)}, f32[64,128]{1,0:T(8,128)S(1)}, u32[]{:S(2)}, u32[]{:S(2)}) collective-permute-start(f32[64,128]{1,0:T(8,128)S(1)} %get-tuple-element.18), channel_id=1, source_target_pairs={{0,192},{64,0},{128,64},{192,128},{1,193},{65,1},{129,65},{193,129... | collective-permute-start | bytes 98312 | tf_op jit(solution)/shard_map/ppermute | solution.py:462
  4.2 9.1 %collective-permute-start = (f32[200,128]{1,0:T(8,128)S(1)}, f32[200,128]{1,0:T(8,128)S(1)}, u32[]{:S(2)}, u32[]{:S(2)}) collective-permute-start(f32[200,128]{1,0:T(8,128)S(1)} %get-tuple-element.17), channel_id=1, source_target_pairs={{0,64},{64,128},{128,192},{192,0},{1,65},{65,129},{129,193},{193,1... | collective-permute-start | bytes 307208 | tf_op jit(solution)/shard_map/ppermute | solution.py:462
  4.7 0.7 %copy-start.4 = (s32[5632]{0:T(1024)S(1)}, s32[5632]{0:T(1024)}, u32[]{:S(2)}) copy-start(s32[5632]{0:T(1024)} %from_ref.5) | copy-start | bytes 67588
  5.4 0.7 %copy-start.6 = (s32[5632]{0:T(1024)S(1)}, s32[5632]{0:T(1024)}, u32[]{:S(2)}) copy-start(s32[5632]{0:T(1024)} %to_ref.5) | copy-start | bytes 67588
  6.2 0.7 %copy-start.8 = (f32[5632]{0:T(1024)S(1)}, f32[5632]{0:T(1024)}, u32[]{:S(2)}) copy-start(f32[5632]{0:T(1024)} %susc_ref.5) | copy-start | bytes 67588
  6.9 6.4 %copy-start.1 = (f32[4,16,4096]{2,1,0:T(8,128)S(1)}, f32[4,16,4096]{2,1,0:T(8,128)}, u32[]{:S(2)}) copy-start(f32[4,16,4096]{2,1,0:T(8,128)} %param.10) | copy-start | bytes 3145732
  6.9 6.4 %copy-start.2 = (f32[16,1280]{1,0:T(8,128)S(1)}, f32[16,1280]{1,0:T(8,128)}, u32[]{:S(2)}) copy-start(f32[16,1280]{1,0:T(8,128)} %dispatch_ref.1) | copy-start | bytes 245764
  6.9 6.4 %copy-start.9 = (bf16[4,16,4096]{2,1,0:T(8,128)(2,1)S(1)}, bf16[4,16,4096]{2,1,0:T(8,128)(2,1)}, u32[]{:S(2)}) copy-start(bf16[4,16,4096]{2,1,0:T(8,128)(2,1)} %param.12) | copy-start | bytes 1572868
  6.9 6.4 %copy-start.11 = (s32[1280]{0:T(1024)S(1)}, s32[1280]{0:T(1024)}, u32[]{:S(2)}) copy-start(s32[1280]{0:T(1024)} %gen_ref.1) | copy-start | bytes 15364
  6.9 6.4 %copy-start.12 = (s32[4]{0:T(128)S(1)}, s32[4]{0:T(128)}, u32[]{:S(2)}) copy-start(s32[4]{0:T(128)} %outage_ref.1) | copy-start | bytes 52
  13.3 39.1 %copy-start.10 = (f32[16,4096]{1,0:T(8,128)S(1)}, f32[16,4096]{1,0:T(8,128)}, u32[]{:S(2)}) copy-start(f32[16,4096]{1,0:T(8,128)} %reg_ref.1) | copy-start | bytes 786436
  18.4 4.7 %collective-permute-start.4 = (f32[16,1280]{1,0:T(8,128)S(1)}, f32[16,1280]{1,0:T(8,128)S(1)}, u32[]{:S(2)}, u32[]{:S(2)}) collective-permute-start(f32[16,1280]{1,0:T(8,128)S(1)} %get-tuple-element.25), channel_id=1, source_target_pairs={{0,1},{1,0},{2,3},{3,2},{4,5},{5,4},{6,7},{7,6},{8,9},{9,8},{10,11... | collective-permute-start | bytes 245768 | tf_op jit(solution)/shard_map/ppermute | solution.py:468
  23.1 6.7 %collective-permute-start.5 = (f32[16,1280]{1,0:T(8,128)S(1)}, f32[16,1280]{1,0:T(8,128)S(1)}, u32[]{:S(2)}, u32[]{:S(2)}) collective-permute-start(f32[16,1280]{1,0:T(8,128)S(1)} %add.18), channel_id=1, source_target_pairs={{0,3},{1,2},{2,1},{3,0},{4,7},{5,6},{6,5},{7,4},{8,11},{9,10},{10,... | collective-permute-start | bytes 245768 | tf_op jit(solution)/shard_map/ppermute | solution.py:468
  29.8 6.0 %collective-permute-start.6 = (f32[16,1280]{1,0:T(8,128)S(1)}, f32[16,1280]{1,0:T(8,128)S(1)}, u32[]{:S(2)}, u32[]{:S(2)}) collective-permute-start(f32[16,1280]{1,0:T(8,128)S(1)} %add.19), channel_id=1, source_target_pairs={{0,4},{1,5},{2,6},{3,7},{4,0},{5,1},{6,2},{7,3},{8,12},{9,13},{10,... | collective-permute-start | bytes 245768 | tf_op jit(solution)/shard_map/ppermute | solution.py:468
  35.8 4.5 %collective-permute-start.7 = (f32[16,1280]{1,0:T(8,128)S(1)}, f32[16,1280]{1,0:T(8,128)S(1)}, u32[]{:S(2)}, u32[]{:S(2)}) collective-permute-start(f32[16,1280]{1,0:T(8,128)S(1)} %add.20), channel_id=1, source_target_pairs={{0,8},{1,9},{2,10},{3,11},{4,12},{5,13},{6,14},{7,15},{8,0},{9,1},... | collective-permute-start | bytes 245768 | tf_op jit(solution)/shard_map/ppermute | solution.py:468
  40.4 5.6 %collective-permute-start.8 = (f32[16,1280]{1,0:T(8,128)S(1)}, f32[16,1280]{1,0:T(8,128)S(1)}, u32[]{:S(2)}, u32[]{:S(2)}) collective-permute-start(f32[16,1280]{1,0:T(8,128)S(1)} %add.21), channel_id=1, source_target_pairs={{0,16},{1,17},{2,18},{3,19},{4,20},{5,21},{6,22},{7,23},{8,24},{9,... | collective-permute-start | bytes 245768 | tf_op jit(solution)/shard_map/ppermute | solution.py:468
  43.5 8.9 %collective-permute-start.2 = (f32[64,128]{1,0:T(8,128)S(1)}, f32[64,128]{1,0:T(8,128)S(1)}, u32[]{:S(2)}, u32[]{:S(2)}) collective-permute-start(f32[64,128]{1,0:T(8,128)S(1)} %get-tuple-element.23), channel_id=1, source_target_pairs={{0,64},{64,128},{128,192},{192,0},{1,65},{65,129},{129,193},{193,1... | collective-permute-start | bytes 98312 | tf_op jit(solution)/shard_map/ppermute | solution.py:462
  43.5 8.9 %collective-permute-start.3 = (f32[64,128]{1,0:T(8,128)S(1)}, f32[64,128]{1,0:T(8,128)S(1)}, u32[]{:S(2)}, u32[]{:S(2)}) collective-permute-start(f32[64,128]{1,0:T(8,128)S(1)} %get-tuple-element.24), channel_id=1, source_target_pairs={{0,192},{64,0},{128,64},{192,128},{1,193},{65,1},{129,65},{193,129... | collective-permute-start | bytes 98312 | tf_op jit(solution)/shard_map/ppermute | solution.py:462
  46.0 9.3 %collective-permute-start.9 = (f32[16,1280]{1,0:T(8,128)S(1)}, f32[16,1280]{1,0:T(8,128)S(1)}, u32[]{:S(2)}, u32[]{:S(2)}) collective-permute-start(f32[16,1280]{1,0:T(8,128)S(1)} %add.22), channel_id=1, source_target_pairs={{0,56},{1,57},{2,58},{3,59},{4,60},{5,61},{6,62},{7,63},{8,48},{9,... | collective-permute-start | bytes 245768 | tf_op jit(solution)/shard_map/ppermute | solution.py:468
  52.5 2.9 %copy-start.13 = (f32[16,1280]{1,0:T(8,128)S(1)}, f32[16,1280]{1,0:T(8,128)}, u32[]{:S(2)}) copy-start(f32[16,1280]{1,0:T(8,128)} %param.14) | copy-start | bytes 245764

commit v3 on v2

--- a/solution.py
+++ b/solution.py
@@ -12,6 +12,8 @@
 PERIODS = 16
 TILES = BUS_DEV // RIM
 BR_ROWS = BR_DEV // RIM
+PART_ROWS = 48
+SENT_ROWS = 208
 PAIRS = TILES // 2
 CASES = 4
 ROWS = CASES * PERIODS
@@ -45,72 +47,82 @@
 
 def one_hot(rows, index):
     spots = lax.broadcasted_iota(jnp.int32, (rows, index.shape[1]), 0)
-    return spots == index
+    return spots.astype(F32).astype(BF16) == index.astype(F32).astype(BF16)
+
+
+def held_at(mask, values):
+    return jnp.where(mask, values, jnp.zeros((), BF16))
 
 
 def ones_at(mask):
-    return jnp.where(mask, 1.0, 0.0).astype(BF16)
-
-
-def held_at(mask, values):
-    return jnp.where(mask, values, 0.0).astype(BF16)
-
-
-def parts_of(values):
-    high = values.astype(BF16).astype(F32)
-    return high, values - high
+    return held_at(mask, jnp.ones((), BF16))
 
 
 def as_row(ref):
     return ref[...].reshape(1, ref.shape[0])
 
 
-def pack_kernel(from_ref, to_ref, susc_ref, last_ref, lead_ref, out_ref, first_ref):
+def pack_kernel(
+    from_hbm, to_hbm, susc_hbm, field_hbm, out_ref, first_ref, from_ref, to_ref, susc_ref, sems
+):
+    moves = (
+        (from_hbm, from_ref),
+        (to_hbm, to_ref),
+        (susc_hbm, susc_ref),
+        (field_hbm.at[:, pl.ds(BUS_DEV - RIM, RIM)], out_ref.at[pl.ds(3 * PART_ROWS, ROWS), :]),
+        (field_hbm.at[:, pl.ds(0, RIM)], first_ref),
+    )
+    copies = [pltpu.make_async_copy(*move, sems.at[k]) for k, move in enumerate(moves)]
+    for copy in copies:
+        copy.start()
     for part, ref in enumerate((from_ref, to_ref, susc_ref)):
+        copies[part].wait()
         row = as_row(ref).astype(F32)
         for k in range(BR_ROWS):
-            at = part * BR_ROWS + k
+            at = part * PART_ROWS + k
             out_ref[at : at + 1, :] = row[:, k * RIM : (k + 1) * RIM]
-    out_ref[136:200, :] = last_ref[...]
-    first_ref[...] = lead_ref[...]
+        out_ref[part * PART_ROWS + BR_ROWS : (part + 1) * PART_ROWS, :] = jnp.zeros(
+            (PART_ROWS - BR_ROWS, RIM), F32
+        )
+    copies[3].wait()
+    copies[4].wait()
 
 
 def pack(from_bus, to_bus, susceptance, field):
-    row = pl.BlockSpec((BR_DEV,), lambda i: (0,))
     return pl.pallas_call(
         pack_kernel,
-        grid=(1,),
-        in_specs=[
-            row,
-            row,
-            row,
-            pl.BlockSpec((ROWS, RIM), lambda i: (0, TILES - 1)),
-            pl.BlockSpec((ROWS, RIM), lambda i: (0, 0)),
+        in_specs=[whole(pltpu.HBM)] * 4,
+        out_specs=[whole()] * 5,
+        out_shape=[
+            pltpu.VMEM((SENT_ROWS, RIM), F32),
+            pltpu.VMEM((ROWS, RIM), F32),
+            pltpu.VMEM((BR_DEV,), jnp.int32),
+            pltpu.VMEM((BR_DEV,), jnp.int32),
+            pltpu.VMEM((BR_DEV,), F32),
         ],
-        out_specs=[whole(), whole()],
-        out_shape=[pltpu.VMEM((200, RIM), F32), pltpu.VMEM((ROWS, RIM), F32)],
-        compiler_params=pltpu.CompilerParams(vmem_limit_bytes=4 << 20),
+        scratch_shapes=[pltpu.SemaphoreType.DMA((5,))],
+        compiler_params=pltpu.CompilerParams(vmem_limit_bytes=63 << 20),
         name="pack",
-    )(from_bus, to_bus, susceptance, field, field)
-
-
-def tile_of_group(starts_row, to_row, high_row, low_row):
+    )(from_bus, to_bus, susceptance, field)
+
+
+def turned_tile(starts_row, to_row, high_row, low_row):
     starts = ones_at(one_hot(RIM, starts_row))
     hit = one_hot(RIM, to_row)
+    high_row, low_row = high_row.astype(BF16), low_row.astype(BF16)
     ends = jnp.concatenate([held_at(hit, high_row), held_at(hit, low_row)], axis=0)
-    both = dot_last(starts, ends)
-    return both[:, :RIM] + both[:, RIM:]
+    both = dot_last(ends, starts)
+    return both[:RIM] + both[RIM:]
 
 
 def band_kernel(
-    base_ref, from_ref, to_ref, susc_ref, high_ref, low_ref, degree_ref, tiles, table
+    from_ref, to_ref, susc_ref, high_ref, low_ref, degree_ref, tiles, table
 ):
-    base = base_ref[0] * BUS_DEV
+    base = lax.axis_index("net") * BUS_DEV
     from_local = as_row(from_ref) - base
     tile = from_local // RIM
-    tile_hit = one_hot(TILES, tile)
-    member = jnp.where(tile_hit, 1.0, 0.0)
-    packed = member.astype(BF16)
+    packed = ones_at(one_hot(TILES, tile))
+    member = packed.astype(F32)
     chunks = BR_DEV // WORK
     rows = lax.broadcasted_iota(jnp.int32, (WORK, WORK), 0)
     cols = lax.broadcasted_iota(jnp.int32, (WORK, WORK), 1)
@@ -139,12 +151,10 @@
     group = jnp.where(rank < SLOTS, tile, TILES + spill_at + rank // SLOTS - 1)
     group_hit = one_hot(GROUPS, group)
     slot_hit = ones_at(one_hot(SLOTS, rank % SLOTS))
-    susc_high, susc_low = parts_of(as_row(susc_ref))
     features = (
-        (from_local % RIM).astype(F32),
-        ((as_row(to_ref) - base) % RIM).astype(F32),
-        susc_high,
-        susc_low,
+        (from_local % RIM).astype(F32).astype(BF16),
+        ((as_row(to_ref) - base) % RIM).astype(F32).astype(BF16),
+        *split(as_row(susc_ref)),
     )
     table[...] = dot_last(
         jnp.concatenate([held_at(group_hit, value) for value in features], axis=0), slot_hit
@@ -152,35 +162,36 @@
 
     def group_tile(at):
         rows = [table[pl.ds(part * GROUPS + at, 1), :] for part in range(4)]
-        return tile_of_group(rows[0].astype(jnp.int32), rows[1].astype(jnp.int32), *rows[2:])
-
-    for at in range(TILES):
-        tiles[at] = group_tile(at)
-
-    @pl.loop(0, spill)
-    def _(step):
-        passed = jnp.where(extra_upto <= step.astype(F32), 1.0, 0.0)
-        owner = jnp.sum(passed).astype(jnp.int32)
-        tiles[owner] = tiles[owner] + group_tile(TILES + step)
+        return turned_tile(*rows)
+
+    @pl.when(spill > 0)
+    def _():
+        tiles[...] = jnp.zeros_like(tiles)
+
+        @pl.loop(0, spill)
+        def _(step):
+            passed = jnp.where(extra_upto <= step.astype(F32), 1.0, 0.0)
+            owner = jnp.sum(passed).astype(jnp.int32)
+            tiles[owner] = tiles[owner] + group_tile(TILES + step)
 
     rows = lax.broadcasted_iota(jnp.int32, (RIM, RIM), 0)
     cols = lax.broadcasted_iota(jnp.int32, (RIM, RIM), 1)
+    later = cols > rows
+    narrow = [x.astype(F32).astype(BF16) for x in (rows, cols)]
+    above, below = narrow[1] > narrow[0], narrow[1] < narrow[0]
     zero = jnp.zeros((RIM, RIM), BF16)
     carried = jnp.zeros((1, RIM), F32)
     for at in range(TILES):
         pair, odd = at // 2, at % 2
-        block = tiles[at]
-        turned = block.T
-        inside = jnp.where(cols > rows, block, jnp.where(cols < rows, turned, 0.0))
-        ahead = jnp.where(cols > rows, 0.0, block)
-        back = jnp.where(cols < rows, 0.0, turned)
+        turned = group_tile(at) + jnp.where(spill > 0, tiles[at], 0.0)
+        block = turned.T
         own = slice((1 + odd) * RIM, (2 + odd) * RIM)
         mine = slice(odd * RIM, (odd + 1) * RIM)
         other = slice((1 - odd) * RIM, (2 - odd) * RIM)
-        for ref, kind in ((high_ref, 0), (low_ref, 1)):
-            inside_part = split(inside)[kind]
-            ahead_part = split(ahead)[kind]
-            back_part = split(back)[kind]
+        for ref, part, back in zip((high_ref, low_ref), split(block), split(turned)):
+            inside_part = jnp.where(above, part, jnp.where(below, back, zero))
+            ahead_part = jnp.where(above, zero, part)
+            back_part = jnp.where(below, zero, back)
             ref[pair, own, mine] = inside_part
             if odd == 0:
                 ref[pair, 2 * RIM : 3 * RIM, mine] = back_part
@@ -193,19 +204,18 @@
                 ref[pair, :RIM, mine] = zero
                 if pair + 1 < PAIRS:
                     ref[pair + 1, :RIM, :RIM] = ahead_part
+        inside = jnp.sum(jnp.where(later, block, 0.0), axis=0, keepdims=True)
         degree_ref[:, at * RIM : (at + 1) * RIM] = (
-            jnp.sum(inside, axis=0, keepdims=True)
-            + jnp.sum(back, axis=0, keepdims=True)
-            + carried
+            inside + jnp.sum(turned, axis=0, keepdims=True) + carried
         )
-        carried = jnp.sum(ahead, axis=0, keepdims=True)
-
-
-def build_band(place, from_bus, to_bus, susceptance):
+        carried = jnp.sum(jnp.where(later, 0.0, block), axis=0, keepdims=True)
+
+
+def build_band(from_bus, to_bus, susceptance):
     shape = pltpu.VMEM((PAIRS, 4 * RIM, 2 * RIM), BF16)
     return pl.pallas_call(
         band_kernel,
-        in_specs=[whole(pltpu.SMEM)] + [whole()] * 3,
+        in_specs=[whole()] * 3,
         out_specs=[whole()] * 3,
         out_shape=[shape, shape, pltpu.VMEM((1, BUS_DEV), F32)],
         scratch_shapes=[
@@ -215,7 +225,7 @@
         compiler_params=pltpu.CompilerParams(vmem_limit_bytes=VMEM_LIMIT),
         cost_estimate=pl.CostEstimate(flops=8 << 30, bytes_accessed=16 << 20, transcendentals=0),
         name="band",
-    )(place, from_bus, to_bus, susceptance)
+    )(from_bus, to_bus, susceptance)
 
 
 def outage_row(from_at, to_at, start, width):
@@ -257,16 +267,13 @@
 
 
 def resid_kernel(
-    place_ref,
     outage_ref,
     field_ref,
     barrier_ref,
     high_ref,
     low_ref,
     own_degree_ref,
-    from_ref,
-    to_ref,
-    susc_ref,
+    own_ref,
     left_ref,
     right_ref,
     dispatch_ref,
@@ -282,61 +289,83 @@
     inject,
     total,
 ):
-    block = place_ref[0]
+    block = lax.axis_index("net")
     base = block * BUS_DEV
     keep = jnp.where(block > 0, 1.0, 0.0)
-    left_rows = [
-        jnp.concatenate(
-            [left_ref[part * BR_ROWS + k : part * BR_ROWS + k + 1] for k in range(BR_ROWS)],
-            axis=1,
+    shift = (base - RIM).astype(F32)
+    starts, stops, values = [
+        left_ref[part * PART_ROWS : (part + 1) * PART_ROWS] for part in range(3)
+    ]
+    starts, stops, values = starts - shift, stops - shift, values * keep
+    crossing = stops >= RIM
+    from_row, to_row, high_row, low_row = [
+        jnp.concatenate([part[k : k + 1] for k in range(BR_ROWS)], axis=1)
+        for part in (
+            starts,
+            stops - RIM,
+            *[part.astype(F32) for part in split(jnp.where(crossing, values, 0.0))],
         )
-        for part in range(3)
     ]
-    left_from = left_rows[0].astype(jnp.int32)
-    left_to = left_rows[1].astype(jnp.int32)
-    left_susc = left_rows[2] * keep
-    high, low = parts_of(jnp.where(left_to >= base, left_susc, 0.0))
-    hit = one_hot(RIM, (left_to - base) % RIM)
-    left_ends = jnp.concatenate([held_at(hit, high), held_at(hit, low)], axis=0)
-    both = dot_last(ones_at(one_hot(RIM, left_from - (base - RIM))), left_ends)
+    hit = one_hot(RIM, to_row)
+    left_ends = jnp.concatenate(
+        [held_at(hit, high_row.astype(BF16)), held_at(hit, low_row.astype(BF16))], axis=0
+    )
+    both = dot_last(ones_at(one_hot(RIM, from_row)), left_ends)
     across = both[:, :RIM] + both[:, RIM:]
     cross = jnp.concatenate(split(across), axis=1)
     cross_ref[...] = cross
     degree_ref[...] = own_degree_ref[...]
     degree_ref[:, :RIM] = own_degree_ref[:, :RIM] + jnp.sum(across, axis=0, keepdims=True)
 
-    branch = lax.broadcasted_iota(jnp.int32, (1, BR_DEV), 1)
-    own_rows = [as_row(from_ref).astype(F32), as_row(to_ref).astype(F32), as_row(susc_ref)]
-    left_rows = [left_rows[0] * keep, left_rows[1] * keep, left_susc]
+    own_starts, own_stops, own_values = [
+        own_ref[part * PART_ROWS : (part + 1) * PART_ROWS] for part in range(3)
+    ]
+    pairs = (
+        (own_starts - shift, starts * keep),
+        (own_stops - shift, stops * keep),
+        (own_values, values),
+    )
+    branch = (
+        lax.broadcasted_iota(jnp.int32, (PART_ROWS, RIM), 0) * RIM
+        + lax.broadcasted_iota(jnp.int32, (PART_ROWS, RIM), 1)
+        + block * BR_DEV
+    )
+    inside = lax.broadcasted_iota(jnp.int32, (PART_ROWS, RIM), 0) < BR_ROWS
+    branch = jnp.where(inside, branch, -BR_DEV - 1)
+    out_row = outage_ref[...].reshape(1, CASES)
     ends, susc = [], []
     for case in range(CASES):
-        own_hit = branch == outage_ref[case] - block * BR_DEV
-        left_hit = branch == outage_ref[case] - (block - 1) * BR_DEV
+        out = out_row[:, case : case + 1]
+        own_hit = branch == out
+        left_hit = branch == out + BR_DEV
         start, end, value = [
             jnp.sum(
-                jnp.where(own_hit, own, 0.0) + jnp.where(left_hit, left, 0.0),
+                jnp.sum(
+                    jnp.where(own_hit, own, 0.0) + jnp.where(left_hit, left, 0.0),
+                    axis=0,
+                    keepdims=True,
+                ),
                 axis=1,
                 keepdims=True,
             )
-            for own, left in zip(own_rows, left_rows)
+            for own, left in pairs
         ]
-        ends.append(
-            (start.astype(jnp.int32) - base + RIM, end.astype(jnp.int32) - base + RIM)
-        )
+        ends.append((start.astype(jnp.int32), end.astype(jnp.int32)))
         susc.append(value)
-        for k, held in enumerate((*ends[case], value)):
+        for k, held in enumerate((start, end, value)):
             at = 4 * k + case
-            ends_ref[at : at + 1, :] = jnp.broadcast_to(held.astype(F32), (1, RIM))
+            ends_ref[at : at + 1, :] = jnp.broadcast_to(held, (1, RIM))
 
     gen = as_row(gen_ref) - base
     gen_tile = gen // RIM
+    gen_hits = [gen_tile.astype(F32).astype(BF16) == tile for tile in range(TILES)]
     gen_spots = ones_at(one_hot(RIM, gen % RIM))
-    dispatch_parts = parts_of(dispatch_ref[...])
+    dispatch_parts = split(dispatch_ref[...])
     share = TILES // 4
     for part in range(4):
         tiles = range(part * share, (part + 1) * share)
         picked = jnp.concatenate(
-            [held_at(gen_tile == tile, value) for value in dispatch_parts for tile in tiles],
+            [held_at(gen_hits[tile], value) for value in dispatch_parts for tile in tiles],
             axis=0,
         )
         spread = dot_last(picked, gen_spots)
@@ -344,7 +373,7 @@
         inject[part * half : (part + 1) * half] = spread[:half] + spread[half:]
 
     def halo(tile):
-        return left_ref[136:200] if tile < 0 else right_ref[...]
+        return left_ref[3 * PART_ROWS :] if tile < 0 else right_ref[...]
 
     def inner(start, width):
         return field_ref[:, start : start + width]
@@ -380,11 +409,11 @@
     partial_ref[...] = at_gens
 
 
-def residuals(place, outage, field, barrier, band, raw, halos, dispatch, gen_bus):
+def residuals(outage, field, barrier, band, own, halos, dispatch, gen_bus):
     tile = pltpu.VMEM((ROWS, RIM), F32)
     return pl.pallas_call(
         resid_kernel,
-        in_specs=[whole(pltpu.SMEM)] * 2 + [whole()] * 12,
+        in_specs=[whole()] * 11,
         out_specs=[whole()] * 7,
         out_shape=[
             pltpu.VMEM((ROWS, BUS_DEV), F32),
@@ -403,7 +432,7 @@
         compiler_params=pltpu.CompilerParams(vmem_limit_bytes=VMEM_LIMIT),
         cost_estimate=pl.CostEstimate(flops=4 << 30, bytes_accessed=8 << 20, transcendentals=0),
         name="resid",
-    )(place, outage, field, barrier, *band, *raw, *halos, dispatch, gen_bus)
+    )(outage, field, barrier, *band, own, *halos, dispatch, gen_bus)
 
 
 def angle_kernel(
@@ -464,8 +493,12 @@
 
 def sum_cases(value):
     size = lax.axis_size("ctg")
-    for mask in (1, 3, 4, 8, 16, 56):
-        value = value + lax.ppermute(value, "ctg", [(i, i ^ mask) for i in range(size)])
+    for masks in ((8,), (16,), (1, 2, 3), (4,), (40,)):
+        parts = [
+            lax.ppermute(value, "ctg", [(i, i ^ mask) for i in range(size)]) for mask in masks
+        ]
+        for part in parts:
+            value = value + part
     return value
 
 
@@ -481,22 +514,18 @@
     outage,
     gen_bus,
 ):
-    block = lax.axis_index("net")
-    place = jnp.reshape(block, (1,)).astype(jnp.int32)
     field = angle_dir.reshape(ROWS, BUS_DEV)
     weights = barrier.reshape(ROWS, BUS_DEV)
-    raw = (from_bus, to_bus, susceptance)
-    packed, lead = pack(*raw, field)
+    packed, lead, *raw = pack(from_bus, to_bus, susceptance, field)
     left = shifted(packed, 1)
     right = shifted(lead, -1)
-    high, low, own_degree = build_band(place, *raw)
+    high, low, own_degree = build_band(*raw)
     weighted, first, last, partial, cross, degree, ends = residuals(
-        place,
         outage,
         field,
         weights,
         (high, low, own_degree),
-        raw,
+        packed,
         (left, right),
         dispatch_dir,
         gen_bus,

time: 57.1 us -> 48.2 us (0.84); the launches traced: 56 us -> 48.1 us
  local copies, waits for them, and re-layouts: 5.67 us -> 0.03 us
  waiting for transfers between devices: 13.6 us -> 16.3 us
  starting transfers between devices: 21.2 us -> 18.5 us
  Pallas kernels: 14 us -> 11.8 us
    unnamed x28 -> x14, local copies, waits for them, and re-layouts: 5.67 us -> 0.03 us
    ppermute x6 -> x7, starting transfers between devices: 18.9 us -> 16.2 us  [sum_cases(): lax.ppermute(value, 'ctg', [(i, i ^ mask) for i in range(size)])]
    ppermute x6 -> x7, waiting for transfers between devices: 13.6 us -> 16.1 us  [sum_cases(): lax.ppermute(value, 'ctg', [(i, i ^ mask) for i in range(size)])]
    pallas_call x3, Pallas kernels: 11.4 us -> 9.19 us  [the longest x1 4.42 us: build_band(): pl.pallas_call(band_kernel, in_specs=[whole()] * 3, out_specs=[whole()] *...]
  transfers between devices with their start and end apart: 10 -> 11, of which waited for: 6 -> 7; matrix products, arithmetic and copies ran while one was open for 0% -> 0% of each run, Pallas kernels for 16% -> 15%
where the time goes in v3:
time: 48.2 us; the launch traced here: 48.1 us
  starting transfers between devices  18.5 us (38%)
  waiting for transfers between devices  16.3 us (34%)
  Pallas kernels  11.8 us (24%)
  between operations  0.74 us (2%)
  other arithmetic  0.71 us (1%)
    ppermute x7, starting transfers between devices, sum_cases(): lax.ppermute(value, 'ctg', [(i, i ^ mask) for i in range(size)])  16.2 us
    ppermute x7, waiting for transfers between devices, sum_cases(): lax.ppermute(value, 'ctg', [(i, i ^ mask) for i in range(size)])  16.1 us
    pallas_call x1, Pallas kernels, build_band(): pl.pallas_call(band_kernel, in_specs=[whole()] * 3, out_specs=[whole()] *...  4.42 us
    pallas_call x1, Pallas kernels, residuals(): pl.pallas_call(resid_kernel, in_specs=[whole()] * 11, out_specs=[whole()]...  3.9 us
    pallas_call x1, Pallas kernels, angles(): pl.pallas_call(angle_kernel, in_specs=[whole()] * 10, out_specs=whole(),...  2.58 us
    ppermute x4, starting transfers between devices, shifted(): lax.ppermute(block, 'net', [(i, (i + distance) % size) for i in range(siz...  2.35 us
  transfers between devices with their start and end apart: 11, of which 7 were waited for; matrix products, arithmetic and copies ran while one was open for 0% of the time, Pallas kernels for 15%

profile of v3, /device:TPU:2, one launch (start us, length us, event | category | flops | bytes accessed | tf_op | source)
XLA Modules:
  0.0 48.1 jit_solution(9835504465636287769)
XLA Ops:
  0.6 0.9 %pack.1 = (f32[208,128]{1,0:T(8,128)S(1)}, f32[64,128]{1,0:T(8,128)S(1)}, s32[5632]{0:T(1024)S(1)}, s32[5632]{0:T(1024)S(1)}, f32[5632]{0:T(1024)S(1)}) custom-call(s32[5632]{0:T(1024)} %from_hbm.1, s32[5632]{0:T(1024)} %to_hbm.1, f32[5632]{0:T(1024)} %susc_hbm.1, f32[64,4096]{1,0:T(8,128)} %bitcast.3), custom_call_target="tpu_custom_call" | custom-call | tf_op jit(solution)/shard_map/pack/pallas_call | solution.py:92
  1.5 0.1 collective-permute-start.1
  1.6 0.5 %collective-permute-start = (f32[208,128]{1,0:T(8,128)S(1)}, f32[208,128]{1,0:T(8,128)S(1)}, u32[]{:S(2)}, u32[]{:S(2)}) collective-permute-start(f32[208,128]{1,0:T(8,128)S(1)} %get-tuple-element.23.own_ref), channel_id=1, source_target_pairs={{0,64},{64,128},{128,192},{192,0},{1,65},{65,129},{129,193},{193,1... | collective-permute-start | bytes 319496 | tf_op jit(solution)/shard_map/ppermute | solution.py:491
  2.1 0.0 copy-start.5
  2.1 4.4 %band.1 = (bf16[16,512,256]{2,1,0:T(8,128)(2,1)S(1)}, bf16[16,512,256]{2,1,0:T(8,128)(2,1)S(1)}, f32[1,4096]{1,0:T(1,128)S(1)}) custom-call(s32[5632]{0:T(1024)S(1)} %get-tuple-element.17.from_ref, s32[5632]{0:T(1024)S(1)} %get-tuple-element.18.to_ref, f32[5632]{0:T(1024)S(1)} %get-tuple-element.19.susc_ref), custom_call_target="tpu_custom_call" | custom-call | flops 8589934592 | bytes 16777216 | tf_op jit(solution)/shard_map/band/pallas_call | solution.py:216
  6.5 0.0 collective-permute-done.1.right_ref
  6.6 0.2 collective-permute-done.left_ref
  6.7 0.0 copy-done
  6.7 0.0 copy-done.2
  6.7 0.0 copy-start.3
  6.8 3.9 %resid.1 = (f32[64,4096]{1,0:T(8,128)S(1)}, f32[64,128]{1,0:T(8,128)S(1)}, f32[64,128]{1,0:T(8,128)S(1)}, f32[16,1280]{1,0:T(8,128)S(1)}, bf16[128,256]{1,0:T(8,...) custom-call(s32[4]{0:T(128)S(1)} %copy-done.5, f32[64,4096]{1,0:T(8,128)S(1)} %bitcast.4, ...), custom_call_target="tpu_custom_call" | custom-call | flops 4294967296 | bytes 8388608 | tf_op jit(solution)/shard_map/resid/pallas_call | solution.py:414
  10.7 1.9 %collective-permute-start.4 = (f32[16,1280]{1,0:T(8,128)S(1)}, f32[16,1280]{1,0:T(8,128)S(1)}, u32[]{:S(2)}, u32[]{:S(2)}) collective-permute-start(f32[16,1280]{1,0:T(8,128)S(1)} %get-tuple-element.31), channel_id=1, source_target_pairs={{0,8},{1,9},{2,10},{3,11},{4,12},{5,13},{6,14},{7,15},{8,0},{9,1},... | collective-permute-start | bytes 245768 | tf_op jit(solution)/shard_map/ppermute | solution.py:498
  12.5 2.6 %collective-permute-done.4 = f32[16,1280]{1,0:T(8,128)S(1)} collective-permute-done((f32[16,1280]{1,0:T(8,128)S(1)}, f32[16,1280]{1,0:T(8,128)S(1)}, u32[]{:S(2)}, u32[]{:S(2)}) %collective-permute-start.4) | collective-permute-done | bytes 81952 | tf_op jit(solution)/shard_map/ppermute | solution.py:498
  15.2 3.6 %collective-permute-start.5 = (f32[16,1280]{1,0:T(8,128)S(1)}, f32[16,1280]{1,0:T(8,128)S(1)}, u32[]{:S(2)}, u32[]{:S(2)}) collective-permute-start(f32[16,1280]{1,0:T(8,128)S(1)} %add.21), channel_id=1, source_target_pairs={{0,16},{1,17},{2,18},{3,19},{4,20},{5,21},{6,22},{7,23},{8,24},{9,... | collective-permute-start | bytes 245768 | tf_op jit(solution)/shard_map/ppermute | solution.py:498
  18.8 4.7 %collective-permute-done.5 = f32[16,1280]{1,0:T(8,128)S(1)} collective-permute-done((f32[16,1280]{1,0:T(8,128)S(1)}, f32[16,1280]{1,0:T(8,128)S(1)}, u32[]{:S(2)}, u32[]{:S(2)}) %collective-permute-start.5) | collective-permute-done | bytes 81952 | tf_op jit(solution)/shard_map/ppermute | solution.py:498
  23.5 3.1 %collective-permute-start.8 = (f32[16,1280]{1,0:T(8,128)S(1)}, f32[16,1280]{1,0:T(8,128)S(1)}, u32[]{:S(2)}, u32[]{:S(2)}) collective-permute-start(f32[16,1280]{1,0:T(8,128)S(1)} %add.22), channel_id=1, source_target_pairs={{0,3},{1,2},{2,1},{3,0},{4,7},{5,6},{6,5},{7,4},{8,11},{9,10},{10,... | collective-permute-start | bytes 245768 | tf_op jit(solution)/shard_map/ppermute | solution.py:498
  26.6 0.6 %collective-permute-start.7 = (f32[16,1280]{1,0:T(8,128)S(1)}, f32[16,1280]{1,0:T(8,128)S(1)}, u32[]{:S(2)}, u32[]{:S(2)}) collective-permute-start(f32[16,1280]{1,0:T(8,128)S(1)} %add.22), channel_id=1, source_target_pairs={{0,2},{1,3},{2,0},{3,1},{4,6},{5,7},{6,4},{7,5},{8,10},{9,11},{10,... | collective-permute-start | bytes 245768 | tf_op jit(solution)/shard_map/ppermute | solution.py:498
  27.3 0.4 collective-permute-start.6
  27.7 2.4 %collective-permute-done.8 = f32[16,1280]{1,0:T(8,128)S(1)} collective-permute-done((f32[16,1280]{1,0:T(8,128)S(1)}, f32[16,1280]{1,0:T(8,128)S(1)}, u32[]{:S(2)}, u32[]{:S(2)}) %collective-permute-start.8) | collective-permute-done | bytes 81952 | tf_op jit(solution)/shard_map/ppermute | solution.py:498
  30.1 2.4 %collective-permute-done.7 = f32[16,1280]{1,0:T(8,128)S(1)} collective-permute-done((f32[16,1280]{1,0:T(8,128)S(1)}, f32[16,1280]{1,0:T(8,128)S(1)}, u32[]{:S(2)}, u32[]{:S(2)}) %collective-permute-start.7) | collective-permute-done | bytes 81952 | tf_op jit(solution)/shard_map/ppermute | solution.py:498
  32.6 0.0 collective-permute-done.6
  32.6 2.2 %collective-permute-start.9 = (f32[16,1280]{1,0:T(8,128)S(1)}, f32[16,1280]{1,0:T(8,128)S(1)}, u32[]{:S(2)}, u32[]{:S(2)}) collective-permute-start(f32[16,1280]{1,0:T(8,128)S(1)} %add_add_fusion), channel_id=1, source_target_pairs={{0,4},{1,5},{2,6},{3,7},{4,0},{5,1},{6,2},{7,3},{8,12},{9,13},{10,... | collective-permute-start | bytes 245768 | tf_op jit(solution)/shard_map/ppermute | solution.py:498
  34.8 0.0 collective-permute-start.2
  34.8 1.8 %collective-permute-start.3 = (f32[64,128]{1,0:T(8,128)S(1)}, f32[64,128]{1,0:T(8,128)S(1)}, u32[]{:S(2)}, u32[]{:S(2)}) collective-permute-start(f32[64,128]{1,0:T(8,128)S(1)} %get-tuple-element.30), channel_id=1, source_target_pairs={{0,192},{64,0},{128,64},{192,128},{1,193},{65,1},{129,65},{193,129... | collective-permute-start | bytes 98312 | tf_op jit(solution)/shard_map/ppermute | solution.py:491
  36.6 2.4 %collective-permute-done.9 = f32[16,1280]{1,0:T(8,128)S(1)} collective-permute-done((f32[16,1280]{1,0:T(8,128)S(1)}, f32[16,1280]{1,0:T(8,128)S(1)}, u32[]{:S(2)}, u32[]{:S(2)}) %collective-permute-start.9) | collective-permute-done | bytes 81952 | tf_op jit(solution)/shard_map/ppermute | solution.py:498
  39.0 4.3 %collective-permute-start.10 = (f32[16,1280]{1,0:T(8,128)S(1)}, f32[16,1280]{1,0:T(8,128)S(1)}, u32[]{:S(2)}, u32[]{:S(2)}) collective-permute-start(f32[16,1280]{1,0:T(8,128)S(1)} %add.26), channel_id=1, source_target_pairs={{0,40},{1,41},{2,42},{3,43},{4,44},{5,45},{6,46},{7,47},{8,32},{9,... | collective-permute-start | bytes 245768 | tf_op jit(solution)/shard_map/ppermute | solution.py:498
  43.3 0.0 collective-permute-done.2.left_ref
  43.3 0.0 collective-permute-done.3.right_ref
  43.3 0.0 copy-start.6
  43.3 2.6 %angles.1 = f32[64,4096]{1,0:T(8,128)} custom-call(f32[64,4096]{1,0:T(8,128)S(1)} %get-tuple-element.25.weighted_ref, f32[64,4096]{1,0:T(8,128)S(1)} %bitcast.5, f32[16,4096]{1,0:T(8,128)S(1)} %copy-done.3, bf16[16,512,256]{2,1,0:T(8,128)(2,1)S(1)} %get-tuple-element.20.high_ref, bf16[16,512,256]{2,1,0:T(8,128)(2,1)S(1)} %get-tuple-element.21.low_ref, ...), custom_call_target="tpu_custom_call" | custom-call | flops 4294967296 | bytes 8388608 | tf_op jit(solution)/shard_map/angles/pallas_call | solution.py:477
  45.9 1.5 %collective-permute-done.10 = f32[16,1280]{1,0:T(8,128)S(1)} collective-permute-done((f32[16,1280]{1,0:T(8,128)S(1)}, f32[16,1280]{1,0:T(8,128)S(1)}, u32[]{:S(2)}, u32[]{:S(2)}) %collective-permute-start.10) | collective-permute-done | bytes 81952 | tf_op jit(solution)/shard_map/ppermute | solution.py:498
  47.4 0.7 %multiply_subtract_fusion = f32[16,1280]{1,0:T(8,128)} fusion(f32[16,1280]{1,0:T(8,128)S(1)} %add.26, f32[16,1280]{1,0:T(8,128)S(1)} %collective-permute-done.10, f32[16,1280]{1,0:T(8,128)S(1)} %copy-done.6, f32[16,1280]{1,0:T(8,128)S(1)} %copy-done.1), kind=kLoop, calls=%fused_computation | loop fusion | flops 81920 | bytes 409600 | tf_op jit(solution)/shard_map/sub | solution.py:539
  (13 shorter events, 0.1 us)
Async XLA Ops:
  1.5 5.0 %collective-permute-start.1 = (f32[64,128]{1,0:T(8,128)S(1)}, f32[64,128]{1,0:T(8,128)S(1)}, u32[]{:S(2)}, u32[]{:S(2)}) collective-permute-start(f32[64,128]{1,0:T(8,128)S(1)} %get-tuple-element.24), channel_id=1, source_target_pairs={{0,192},{64,0},{128,64},{192,128},{1,193},{65,1},{129,65},{193,129... | collective-permute-start | bytes 98312 | tf_op jit(solution)/shard_map/ppermute | solution.py:491
  1.6 5.1 %collective-permute-start = (f32[208,128]{1,0:T(8,128)S(1)}, f32[208,128]{1,0:T(8,128)S(1)}, u32[]{:S(2)}, u32[]{:S(2)}) collective-permute-start(f32[208,128]{1,0:T(8,128)S(1)} %get-tuple-element.23.own_ref), channel_id=1, source_target_pairs={{0,64},{64,128},{128,192},{192,0},{1,65},{65,129},{129,193},{193,1... | collective-permute-start | bytes 319496 | tf_op jit(solution)/shard_map/ppermute | solution.py:491
  2.1 4.6 %copy-start = (f32[4,16,4096]{2,1,0:T(8,128)S(1)}, f32[4,16,4096]{2,1,0:T(8,128)}, u32[]{:S(2)}) copy-start(f32[4,16,4096]{2,1,0:T(8,128)} %param.10) | copy-start | bytes 3145732
  2.1 4.6 %copy-start.1 = (f32[16,1280]{1,0:T(8,128)S(1)}, f32[16,1280]{1,0:T(8,128)}, u32[]{:S(2)}) copy-start(f32[16,1280]{1,0:T(8,128)} %dispatch_ref.1) | copy-start | bytes 245764
  2.1 4.6 %copy-start.2 = (bf16[4,16,4096]{2,1,0:T(8,128)(2,1)S(1)}, bf16[4,16,4096]{2,1,0:T(8,128)(2,1)}, u32[]{:S(2)}) copy-start(bf16[4,16,4096]{2,1,0:T(8,128)(2,1)} %param.12) | copy-start | bytes 1572868
  2.1 4.6 %copy-start.4 = (s32[1280]{0:T(1024)S(1)}, s32[1280]{0:T(1024)}, u32[]{:S(2)}) copy-start(s32[1280]{0:T(1024)} %gen_ref.1) | copy-start | bytes 15364
  2.1 4.6 %copy-start.5 = (s32[4]{0:T(128)S(1)}, s32[4]{0:T(128)}, u32[]{:S(2)}) copy-start(s32[4]{0:T(128)} %outage_ref.1) | copy-start | bytes 52
  6.7 36.6 %copy-start.3 = (f32[16,4096]{1,0:T(8,128)S(1)}, f32[16,4096]{1,0:T(8,128)}, u32[]{:S(2)}) copy-start(f32[16,4096]{1,0:T(8,128)} %reg_ref.1) | copy-start | bytes 786436
  10.7 4.5 %collective-permute-start.4 = (f32[16,1280]{1,0:T(8,128)S(1)}, f32[16,1280]{1,0:T(8,128)S(1)}, u32[]{:S(2)}, u32[]{:S(2)}) collective-permute-start(f32[16,1280]{1,0:T(8,128)S(1)} %get-tuple-element.31), channel_id=1, source_target_pairs={{0,8},{1,9},{2,10},{3,11},{4,12},{5,13},{6,14},{7,15},{8,0},{9,1},... | collective-permute-start | bytes 245768 | tf_op jit(solution)/shard_map/ppermute | solution.py:498
  15.2 8.3 %collective-permute-start.5 = (f32[16,1280]{1,0:T(8,128)S(1)}, f32[16,1280]{1,0:T(8,128)S(1)}, u32[]{:S(2)}, u32[]{:S(2)}) collective-permute-start(f32[16,1280]{1,0:T(8,128)S(1)} %add.21), channel_id=1, source_target_pairs={{0,16},{1,17},{2,18},{3,19},{4,20},{5,21},{6,22},{7,23},{8,24},{9,... | collective-permute-start | bytes 245768 | tf_op jit(solution)/shard_map/ppermute | solution.py:498
  23.5 6.6 %collective-permute-start.8 = (f32[16,1280]{1,0:T(8,128)S(1)}, f32[16,1280]{1,0:T(8,128)S(1)}, u32[]{:S(2)}, u32[]{:S(2)}) collective-permute-start(f32[16,1280]{1,0:T(8,128)S(1)} %add.22), channel_id=1, source_target_pairs={{0,3},{1,2},{2,1},{3,0},{4,7},{5,6},{6,5},{7,4},{8,11},{9,10},{10,... | collective-permute-start | bytes 245768 | tf_op jit(solution)/shard_map/ppermute | solution.py:498
  26.6 5.9 %collective-permute-start.7 = (f32[16,1280]{1,0:T(8,128)S(1)}, f32[16,1280]{1,0:T(8,128)S(1)}, u32[]{:S(2)}, u32[]{:S(2)}) collective-permute-start(f32[16,1280]{1,0:T(8,128)S(1)} %add.22), channel_id=1, source_target_pairs={{0,2},{1,3},{2,0},{3,1},{4,6},{5,7},{6,4},{7,5},{8,10},{9,11},{10,... | collective-permute-start | bytes 245768 | tf_op jit(solution)/shard_map/ppermute | solution.py:498
  27.3 5.3 %collective-permute-start.6 = (f32[16,1280]{1,0:T(8,128)S(1)}, f32[16,1280]{1,0:T(8,128)S(1)}, u32[]{:S(2)}, u32[]{:S(2)}) collective-permute-start(f32[16,1280]{1,0:T(8,128)S(1)} %add.22), channel_id=1, source_target_pairs={{0,1},{1,0},{2,3},{3,2},{4,5},{5,4},{6,7},{7,6},{8,9},{9,8},{10,11... | collective-permute-start | bytes 245768 | tf_op jit(solution)/shard_map/ppermute | solution.py:498
  32.6 6.4 %collective-permute-start.9 = (f32[16,1280]{1,0:T(8,128)S(1)}, f32[16,1280]{1,0:T(8,128)S(1)}, u32[]{:S(2)}, u32[]{:S(2)}) collective-permute-start(f32[16,1280]{1,0:T(8,128)S(1)} %add_add_fusion), channel_id=1, source_target_pairs={{0,4},{1,5},{2,6},{3,7},{4,0},{5,1},{6,2},{7,3},{8,12},{9,13},{10,... | collective-permute-start | bytes 245768 | tf_op jit(solution)/shard_map/ppermute | solution.py:498
  34.8 8.5 %collective-permute-start.2 = (f32[64,128]{1,0:T(8,128)S(1)}, f32[64,128]{1,0:T(8,128)S(1)}, u32[]{:S(2)}, u32[]{:S(2)}) collective-permute-start(f32[64,128]{1,0:T(8,128)S(1)} %get-tuple-element.29), channel_id=1, source_target_pairs={{0,64},{64,128},{128,192},{192,0},{1,65},{65,129},{129,193},{193,1... | collective-permute-start | bytes 98312 | tf_op jit(solution)/shard_map/ppermute | solution.py:491
  34.8 8.5 %collective-permute-start.3 = (f32[64,128]{1,0:T(8,128)S(1)}, f32[64,128]{1,0:T(8,128)S(1)}, u32[]{:S(2)}, u32[]{:S(2)}) collective-permute-start(f32[64,128]{1,0:T(8,128)S(1)} %get-tuple-element.30), channel_id=1, source_target_pairs={{0,192},{64,0},{128,64},{192,128},{1,193},{65,1},{129,65},{193,129... | collective-permute-start | bytes 98312 | tf_op jit(solution)/shard_map/ppermute | solution.py:491
  39.0 8.4 %collective-permute-start.10 = (f32[16,1280]{1,0:T(8,128)S(1)}, f32[16,1280]{1,0:T(8,128)S(1)}, u32[]{:S(2)}, u32[]{:S(2)}) collective-permute-start(f32[16,1280]{1,0:T(8,128)S(1)} %add.26), channel_id=1, source_target_pairs={{0,40},{1,41},{2,42},{3,43},{4,44},{5,45},{6,46},{7,47},{8,32},{9,... | collective-permute-start | bytes 245768 | tf_op jit(solution)/shard_map/ppermute | solution.py:498
  43.3 4.1 %copy-start.6 = (f32[16,1280]{1,0:T(8,128)S(1)}, f32[16,1280]{1,0:T(8,128)}, u32[]{:S(2)}) copy-start(f32[16,1280]{1,0:T(8,128)} %param.14) | copy-start | bytes 245764

commit v4 on v3

--- a/solution.py
+++ b/solution.py
@@ -18,6 +18,7 @@
 CASES = 4
 ROWS = CASES * PERIODS
 VMEM_LIMIT = 20 * 1024 * 1024
+WIDE = 2 * RIM
 SLOTS = 256
 GROUPS = 64
 WORK = 256
@@ -48,6 +49,11 @@
 def one_hot(rows, index):
     spots = lax.broadcasted_iota(jnp.int32, (rows, index.shape[1]), 0)
     return spots.astype(F32).astype(BF16) == index.astype(F32).astype(BF16)
+
+
+def one_hot_turned(index, columns):
+    spots = lax.broadcasted_iota(jnp.int32, (index.shape[0], columns), 1)
+    return spots.astype(F32).astype(BF16) == index.astype(BF16)
 
 
 def held_at(mask, values):
@@ -310,8 +316,13 @@
     left_ends = jnp.concatenate(
         [held_at(hit, high_row.astype(BF16)), held_at(hit, low_row.astype(BF16))], axis=0
     )
-    both = dot_last(ones_at(one_hot(RIM, from_row)), left_ends)
-    across = both[:, :RIM] + both[:, RIM:]
+    columns = starts.T
+    turned_starts = jnp.concatenate(
+        [ones_at(one_hot_turned(columns[:, k : k + 1], RIM)) for k in range(BR_ROWS)],
+        axis=0,
+    )
+    both = dot_plain(left_ends, turned_starts)
+    across = (both[:RIM] + both[RIM:]).T
     cross = jnp.concatenate(split(across), axis=1)
     cross_ref[...] = cross
     degree_ref[...] = own_degree_ref[...]
@@ -357,20 +368,14 @@
             ends_ref[at : at + 1, :] = jnp.broadcast_to(held, (1, RIM))
 
     gen = as_row(gen_ref) - base
-    gen_tile = gen // RIM
-    gen_hits = [gen_tile.astype(F32).astype(BF16) == tile for tile in range(TILES)]
-    gen_spots = ones_at(one_hot(RIM, gen % RIM))
-    dispatch_parts = split(dispatch_ref[...])
-    share = TILES // 4
-    for part in range(4):
-        tiles = range(part * share, (part + 1) * share)
-        picked = jnp.concatenate(
-            [held_at(gen_hits[tile], value) for value in dispatch_parts for tile in tiles],
-            axis=0,
-        )
-        spread = dot_last(picked, gen_spots)
-        half = spread.shape[0] // 2
-        inject[part * half : (part + 1) * half] = spread[:half] + spread[half:]
+    gen_pair = gen // WIDE
+    gen_hits = [gen_pair.astype(F32).astype(BF16) == pair for pair in range(PAIRS)]
+    gen_spots = ones_at(one_hot(WIDE, gen % WIDE))
+    picked = jnp.concatenate(
+        [held_at(hit, value) for value in split(dispatch_ref[...]) for hit in gen_hits], axis=0
+    )
+    spread = dot_last(picked, gen_spots)
+    inject[...] = spread[: PAIRS * PERIODS] + spread[PAIRS * PERIODS :]
 
     def halo(tile):
         return left_ref[3 * PART_ROWS :] if tile < 0 else right_ref[...]
@@ -379,8 +384,8 @@
         return field_ref[:, start : start + width]
 
     def emit(pair, cols, result):
-        rows = [slice((2 * pair + k) * PERIODS, (2 * pair + k + 1) * PERIODS) for k in (0, 1)]
-        taken = jnp.concatenate([inject[rows[0]], inject[rows[1]]], axis=1)
+        rows = slice(pair * PERIODS, (pair + 1) * PERIODS)
+        taken = inject[rows]
         resid = result - jnp.concatenate([taken] * CASES, axis=0)
         weighted = barrier_ref[:, cols].astype(F32) * resid
         weighted_ref[:, cols] = weighted
@@ -388,9 +393,9 @@
             first_ref[...] = weighted[:, :RIM]
         if pair == PAIRS - 1:
             last_ref[...] = weighted[:, RIM:]
-        summed = weighted[0:16] + weighted[16:32] + (weighted[32:48] + weighted[48:64])
-        total[rows[0]] = summed[:, :RIM]
-        total[rows[1]] = summed[:, RIM:]
+        total[rows] = (
+            weighted[0:16] + weighted[16:32] + (weighted[32:48] + weighted[48:64])
+        )
 
     def degrees(cols):
         return degree_ref[:, cols]
@@ -398,14 +403,14 @@
     apply_pairs(halo, inner, stacks, high_ref, low_ref, cross, degrees, ends, susc, emit)
 
     at_gens = jnp.zeros((PERIODS, G_DEV), F32)
-    size = share * PERIODS
-    for part in range(4):
+    size = PAIRS * PERIODS // 2
+    for part in range(2):
         high, low = split(total[part * size : (part + 1) * size])
         both = dot_plain(jnp.concatenate([high, low], axis=0), gen_spots)
-        for k in range(share):
+        for k in range(PAIRS // 2):
             rows = slice(k * PERIODS, (k + 1) * PERIODS)
             value = both[rows] + both[size + k * PERIODS : size + (k + 1) * PERIODS]
-            at_gens += jnp.where(gen_tile == part * share + k, value, 0.0)
+            at_gens += jnp.where(gen_pair == part * (PAIRS // 2) + k, value, 0.0)
     partial_ref[...] = at_gens
 
 
@@ -426,8 +431,8 @@
         ],
         scratch_shapes=[
             pltpu.VMEM((2 * ROWS, BUS_DEV + 2 * RIM), BF16),
-            pltpu.VMEM((TILES * PERIODS, RIM), F32),
-            pltpu.VMEM((TILES * PERIODS, RIM), F32),
+            pltpu.VMEM((PAIRS * PERIODS, WIDE), F32),
+            pltpu.VMEM((PAIRS * PERIODS, WIDE), F32),
         ],
         compiler_params=pltpu.CompilerParams(vmem_limit_bytes=VMEM_LIMIT),
         cost_estimate=pl.CostEstimate(flops=4 << 30, bytes_accessed=8 << 20, transcendentals=0),

time: 48.2 us -> 47.9 us (level)
  Pallas kernels: 11.8 us -> 11.3 us
where the time goes in v4:
time: 47.9 us; the launch traced here: 47.8 us
  starting transfers between devices  18.7 us (39%)
  waiting for transfers between devices  16.3 us (34%)
  Pallas kernels  11.3 us (24%)
  between operations  0.74 us (2%)
  other arithmetic  0.71 us (1%)
    ppermute x7, starting transfers between devices, sum_cases(): lax.ppermute(value, 'ctg', [(i, i ^ mask) for i in range(size)])  16.3 us
    ppermute x7, waiting for transfers between devices, sum_cases(): lax.ppermute(value, 'ctg', [(i, i ^ mask) for i in range(size)])  16.2 us
    pallas_call x1, Pallas kernels, build_band(): pl.pallas_call(band_kernel, in_specs=[whole()] * 3, out_specs=[whole()] *...  4.42 us
    pallas_call x1, Pallas kernels, residuals(): pl.pallas_call(resid_kernel, in_specs=[whole()] * 11, out_specs=[whole()]...  3.45 us
    pallas_call x1, Pallas kernels, angles(): pl.pallas_call(angle_kernel, in_specs=[whole()] * 10, out_specs=whole(),...  2.58 us
    ppermute x4, starting transfers between devices, shifted(): lax.ppermute(block, 'net', [(i, (i + distance) % size) for i in range(siz...  2.35 us
  transfers between devices with their start and end apart: 11, of which 7 were waited for; matrix products, arithmetic and copies ran while one was open for 0% of the time, Pallas kernels for 15%

profile of v4, /device:TPU:2, one launch (start us, length us, event | category | flops | bytes accessed | tf_op | source)
XLA Modules:
  0.0 47.8 jit_solution(9705410112245584528)
XLA Ops:
  0.6 0.9 %pack.1 = (f32[208,128]{1,0:T(8,128)S(1)}, f32[64,128]{1,0:T(8,128)S(1)}, s32[5632]{0:T(1024)S(1)}, s32[5632]{0:T(1024)S(1)}, f32[5632]{0:T(1024)S(1)}) custom-call(s32[5632]{0:T(1024)} %from_hbm.1, s32[5632]{0:T(1024)} %to_hbm.1, f32[5632]{0:T(1024)} %susc_hbm.1, f32[64,4096]{1,0:T(8,128)} %bitcast.3), custom_call_target="tpu_custom_call" | custom-call | tf_op jit(solution)/shard_map/pack/pallas_call | solution.py:98
  1.5 0.1 collective-permute-start.1
  1.6 0.5 %collective-permute-start = (f32[208,128]{1,0:T(8,128)S(1)}, f32[208,128]{1,0:T(8,128)S(1)}, u32[]{:S(2)}, u32[]{:S(2)}) collective-permute-start(f32[208,128]{1,0:T(8,128)S(1)} %get-tuple-element.23.own_ref), channel_id=1, source_target_pairs={{0,64},{64,128},{128,192},{192,0},{1,65},{65,129},{129,193},{193,1... | collective-permute-start | bytes 319496 | tf_op jit(solution)/shard_map/ppermute | solution.py:496
  2.1 0.0 copy-start.5
  2.1 4.4 %band.1 = (bf16[16,512,256]{2,1,0:T(8,128)(2,1)S(1)}, bf16[16,512,256]{2,1,0:T(8,128)(2,1)S(1)}, f32[1,4096]{1,0:T(1,128)S(1)}) custom-call(s32[5632]{0:T(1024)S(1)} %get-tuple-element.17.from_ref, s32[5632]{0:T(1024)S(1)} %get-tuple-element.18.to_ref, f32[5632]{0:T(1024)S(1)} %get-tuple-element.19.susc_ref), custom_call_target="tpu_custom_call" | custom-call | flops 8589934592 | bytes 16777216 | tf_op jit(solution)/shard_map/band/pallas_call | solution.py:222
  6.5 0.0 collective-permute-done.1.right_ref
  6.6 0.2 collective-permute-done.left_ref
  6.7 0.0 copy-done.4
  6.7 0.0 copy-done.5
  6.7 0.0 copy-start.3
  6.8 3.4 %resid.1 = (f32[64,4096]{1,0:T(8,128)S(1)}, f32[64,128]{1,0:T(8,128)S(1)}, f32[64,128]{1,0:T(8,128)S(1)}, f32[16,1280]{1,0:T(8,128)S(1)}, bf16[128,256]{1,0:T(8,...) custom-call(s32[4]{0:T(128)S(1)} %copy-done.5, f32[64,4096]{1,0:T(8,128)S(1)} %bitcast.4, ...), custom_call_target="tpu_custom_call" | custom-call | flops 4294967296 | bytes 8388608 | tf_op jit(solution)/shard_map/resid/pallas_call | solution.py:419
  10.2 1.9 %collective-permute-start.4 = (f32[16,1280]{1,0:T(8,128)S(1)}, f32[16,1280]{1,0:T(8,128)S(1)}, u32[]{:S(2)}, u32[]{:S(2)}) collective-permute-start(f32[16,1280]{1,0:T(8,128)S(1)} %get-tuple-element.31), channel_id=1, source_target_pairs={{0,8},{1,9},{2,10},{3,11},{4,12},{5,13},{6,14},{7,15},{8,0},{9,1},... | collective-permute-start | bytes 245768 | tf_op jit(solution)/shard_map/ppermute | solution.py:503
  12.1 2.7 %collective-permute-done.4 = f32[16,1280]{1,0:T(8,128)S(1)} collective-permute-done((f32[16,1280]{1,0:T(8,128)S(1)}, f32[16,1280]{1,0:T(8,128)S(1)}, u32[]{:S(2)}, u32[]{:S(2)}) %collective-permute-start.4) | collective-permute-done | bytes 81952 | tf_op jit(solution)/shard_map/ppermute | solution.py:503
  14.7 3.6 %collective-permute-start.5 = (f32[16,1280]{1,0:T(8,128)S(1)}, f32[16,1280]{1,0:T(8,128)S(1)}, u32[]{:S(2)}, u32[]{:S(2)}) collective-permute-start(f32[16,1280]{1,0:T(8,128)S(1)} %add.21), channel_id=1, source_target_pairs={{0,16},{1,17},{2,18},{3,19},{4,20},{5,21},{6,22},{7,23},{8,24},{9,... | collective-permute-start | bytes 245768 | tf_op jit(solution)/shard_map/ppermute | solution.py:503
  18.3 4.7 %collective-permute-done.5 = f32[16,1280]{1,0:T(8,128)S(1)} collective-permute-done((f32[16,1280]{1,0:T(8,128)S(1)}, f32[16,1280]{1,0:T(8,128)S(1)}, u32[]{:S(2)}, u32[]{:S(2)}) %collective-permute-start.5) | collective-permute-done | bytes 81952 | tf_op jit(solution)/shard_map/ppermute | solution.py:503
  23.1 3.1 %collective-permute-start.8 = (f32[16,1280]{1,0:T(8,128)S(1)}, f32[16,1280]{1,0:T(8,128)S(1)}, u32[]{:S(2)}, u32[]{:S(2)}) collective-permute-start(f32[16,1280]{1,0:T(8,128)S(1)} %add.22), channel_id=1, source_target_pairs={{0,3},{1,2},{2,1},{3,0},{4,7},{5,6},{6,5},{7,4},{8,11},{9,10},{10,... | collective-permute-start | bytes 245768 | tf_op jit(solution)/shard_map/ppermute | solution.py:503
  26.2 0.6 %collective-permute-start.7 = (f32[16,1280]{1,0:T(8,128)S(1)}, f32[16,1280]{1,0:T(8,128)S(1)}, u32[]{:S(2)}, u32[]{:S(2)}) collective-permute-start(f32[16,1280]{1,0:T(8,128)S(1)} %add.22), channel_id=1, source_target_pairs={{0,2},{1,3},{2,0},{3,1},{4,6},{5,7},{6,4},{7,5},{8,10},{9,11},{10,... | collective-permute-start | bytes 245768 | tf_op jit(solution)/shard_map/ppermute | solution.py:503
  26.8 0.4 collective-permute-start.6
  27.2 2.4 %collective-permute-done.8 = f32[16,1280]{1,0:T(8,128)S(1)} collective-permute-done((f32[16,1280]{1,0:T(8,128)S(1)}, f32[16,1280]{1,0:T(8,128)S(1)}, u32[]{:S(2)}, u32[]{:S(2)}) %collective-permute-start.8) | collective-permute-done | bytes 81952 | tf_op jit(solution)/shard_map/ppermute | solution.py:503
  29.7 2.4 %collective-permute-done.7 = f32[16,1280]{1,0:T(8,128)S(1)} collective-permute-done((f32[16,1280]{1,0:T(8,128)S(1)}, f32[16,1280]{1,0:T(8,128)S(1)}, u32[]{:S(2)}, u32[]{:S(2)}) %collective-permute-start.7) | collective-permute-done | bytes 81952 | tf_op jit(solution)/shard_map/ppermute | solution.py:503
  32.1 0.0 collective-permute-done.6
  32.1 2.4 %collective-permute-start.9 = (f32[16,1280]{1,0:T(8,128)S(1)}, f32[16,1280]{1,0:T(8,128)S(1)}, u32[]{:S(2)}, u32[]{:S(2)}) collective-permute-start(f32[16,1280]{1,0:T(8,128)S(1)} %add_add_fusion), channel_id=1, source_target_pairs={{0,4},{1,5},{2,6},{3,7},{4,0},{5,1},{6,2},{7,3},{8,12},{9,13},{10,... | collective-permute-start | bytes 245768 | tf_op jit(solution)/shard_map/ppermute | solution.py:503
  34.5 0.0 collective-permute-start.2
  34.5 1.8 %collective-permute-start.3 = (f32[64,128]{1,0:T(8,128)S(1)}, f32[64,128]{1,0:T(8,128)S(1)}, u32[]{:S(2)}, u32[]{:S(2)}) collective-permute-start(f32[64,128]{1,0:T(8,128)S(1)} %get-tuple-element.30), channel_id=1, source_target_pairs={{0,192},{64,0},{128,64},{192,128},{1,193},{65,1},{129,65},{193,129... | collective-permute-start | bytes 98312 | tf_op jit(solution)/shard_map/ppermute | solution.py:496
  36.3 2.4 %collective-permute-done.9 = f32[16,1280]{1,0:T(8,128)S(1)} collective-permute-done((f32[16,1280]{1,0:T(8,128)S(1)}, f32[16,1280]{1,0:T(8,128)S(1)}, u32[]{:S(2)}, u32[]{:S(2)}) %collective-permute-start.9) | collective-permute-done | bytes 81952 | tf_op jit(solution)/shard_map/ppermute | solution.py:503
  38.7 4.3 %collective-permute-start.10 = (f32[16,1280]{1,0:T(8,128)S(1)}, f32[16,1280]{1,0:T(8,128)S(1)}, u32[]{:S(2)}, u32[]{:S(2)}) collective-permute-start(f32[16,1280]{1,0:T(8,128)S(1)} %add.26), channel_id=1, source_target_pairs={{0,40},{1,41},{2,42},{3,43},{4,44},{5,45},{6,46},{7,47},{8,32},{9,... | collective-permute-start | bytes 245768 | tf_op jit(solution)/shard_map/ppermute | solution.py:503
  43.0 0.0 collective-permute-done.2.left_ref
  43.0 0.0 collective-permute-done.3.right_ref
  43.0 0.0 copy-start.6
  43.0 2.6 %angles.1 = f32[64,4096]{1,0:T(8,128)} custom-call(f32[64,4096]{1,0:T(8,128)S(1)} %get-tuple-element.25.weighted_ref, f32[64,4096]{1,0:T(8,128)S(1)} %bitcast.5, f32[16,4096]{1,0:T(8,128)S(1)} %copy-done.3, bf16[16,512,256]{2,1,0:T(8,128)(2,1)S(1)} %get-tuple-element.20.high_ref, bf16[16,512,256]{2,1,0:T(8,128)(2,1)S(1)} %get-tuple-element.21.low_ref, ...), custom_call_target="tpu_custom_call" | custom-call | flops 4294967296 | bytes 8388608 | tf_op jit(solution)/shard_map/angles/pallas_call | solution.py:482
  45.6 1.5 %collective-permute-done.10 = f32[16,1280]{1,0:T(8,128)S(1)} collective-permute-done((f32[16,1280]{1,0:T(8,128)S(1)}, f32[16,1280]{1,0:T(8,128)S(1)}, u32[]{:S(2)}, u32[]{:S(2)}) %collective-permute-start.10) | collective-permute-done | bytes 81952 | tf_op jit(solution)/shard_map/ppermute | solution.py:503
  47.1 0.7 %multiply_subtract_fusion = f32[16,1280]{1,0:T(8,128)} fusion(f32[16,1280]{1,0:T(8,128)S(1)} %add.26, f32[16,1280]{1,0:T(8,128)S(1)} %collective-permute-done.10, f32[16,1280]{1,0:T(8,128)S(1)} %copy-done.6, f32[16,1280]{1,0:T(8,128)S(1)} %copy-done.1), kind=kLoop, calls=%fused_computation | loop fusion | flops 81920 | bytes 409600 | tf_op jit(solution)/shard_map/sub | solution.py:544
  (13 shorter events, 0.1 us)
Async XLA Ops:
  1.5 5.0 %collective-permute-start.1 = (f32[64,128]{1,0:T(8,128)S(1)}, f32[64,128]{1,0:T(8,128)S(1)}, u32[]{:S(2)}, u32[]{:S(2)}) collective-permute-start(f32[64,128]{1,0:T(8,128)S(1)} %get-tuple-element.24), channel_id=1, source_target_pairs={{0,192},{64,0},{128,64},{192,128},{1,193},{65,1},{129,65},{193,129... | collective-permute-start | bytes 98312 | tf_op jit(solution)/shard_map/ppermute | solution.py:496
  1.6 5.1 %collective-permute-start = (f32[208,128]{1,0:T(8,128)S(1)}, f32[208,128]{1,0:T(8,128)S(1)}, u32[]{:S(2)}, u32[]{:S(2)}) collective-permute-start(f32[208,128]{1,0:T(8,128)S(1)} %get-tuple-element.23.own_ref), channel_id=1, source_target_pairs={{0,64},{64,128},{128,192},{192,0},{1,65},{65,129},{129,193},{193,1... | collective-permute-start | bytes 319496 | tf_op jit(solution)/shard_map/ppermute | solution.py:496
  2.1 4.6 %copy-start = (f32[4,16,4096]{2,1,0:T(8,128)S(1)}, f32[4,16,4096]{2,1,0:T(8,128)}, u32[]{:S(2)}) copy-start(f32[4,16,4096]{2,1,0:T(8,128)} %param.10) | copy-start | bytes 3145732
  2.1 4.6 %copy-start.1 = (f32[16,1280]{1,0:T(8,128)S(1)}, f32[16,1280]{1,0:T(8,128)}, u32[]{:S(2)}) copy-start(f32[16,1280]{1,0:T(8,128)} %dispatch_ref.1) | copy-start | bytes 245764
  2.1 4.6 %copy-start.2 = (bf16[4,16,4096]{2,1,0:T(8,128)(2,1)S(1)}, bf16[4,16,4096]{2,1,0:T(8,128)(2,1)}, u32[]{:S(2)}) copy-start(bf16[4,16,4096]{2,1,0:T(8,128)(2,1)} %param.12) | copy-start | bytes 1572868
  2.1 4.6 %copy-start.4 = (s32[1280]{0:T(1024)S(1)}, s32[1280]{0:T(1024)}, u32[]{:S(2)}) copy-start(s32[1280]{0:T(1024)} %gen_ref.1) | copy-start | bytes 15364
  2.1 4.6 %copy-start.5 = (s32[4]{0:T(128)S(1)}, s32[4]{0:T(128)}, u32[]{:S(2)}) copy-start(s32[4]{0:T(128)} %outage_ref.1) | copy-start | bytes 52
  6.7 36.3 %copy-start.3 = (f32[16,4096]{1,0:T(8,128)S(1)}, f32[16,4096]{1,0:T(8,128)}, u32[]{:S(2)}) copy-start(f32[16,4096]{1,0:T(8,128)} %reg_ref.1) | copy-start | bytes 786436
  10.2 4.5 %collective-permute-start.4 = (f32[16,1280]{1,0:T(8,128)S(1)}, f32[16,1280]{1,0:T(8,128)S(1)}, u32[]{:S(2)}, u32[]{:S(2)}) collective-permute-start(f32[16,1280]{1,0:T(8,128)S(1)} %get-tuple-element.31), channel_id=1, source_target_pairs={{0,8},{1,9},{2,10},{3,11},{4,12},{5,13},{6,14},{7,15},{8,0},{9,1},... | collective-permute-start | bytes 245768 | tf_op jit(solution)/shard_map/ppermute | solution.py:503
  14.7 8.3 %collective-permute-start.5 = (f32[16,1280]{1,0:T(8,128)S(1)}, f32[16,1280]{1,0:T(8,128)S(1)}, u32[]{:S(2)}, u32[]{:S(2)}) collective-permute-start(f32[16,1280]{1,0:T(8,128)S(1)} %add.21), channel_id=1, source_target_pairs={{0,16},{1,17},{2,18},{3,19},{4,20},{5,21},{6,22},{7,23},{8,24},{9,... | collective-permute-start | bytes 245768 | tf_op jit(solution)/shard_map/ppermute | solution.py:503
  23.1 6.6 %collective-permute-start.8 = (f32[16,1280]{1,0:T(8,128)S(1)}, f32[16,1280]{1,0:T(8,128)S(1)}, u32[]{:S(2)}, u32[]{:S(2)}) collective-permute-start(f32[16,1280]{1,0:T(8,128)S(1)} %add.22), channel_id=1, source_target_pairs={{0,3},{1,2},{2,1},{3,0},{4,7},{5,6},{6,5},{7,4},{8,11},{9,10},{10,... | collective-permute-start | bytes 245768 | tf_op jit(solution)/shard_map/ppermute | solution.py:503
  26.2 5.9 %collective-permute-start.7 = (f32[16,1280]{1,0:T(8,128)S(1)}, f32[16,1280]{1,0:T(8,128)S(1)}, u32[]{:S(2)}, u32[]{:S(2)}) collective-permute-start(f32[16,1280]{1,0:T(8,128)S(1)} %add.22), channel_id=1, source_target_pairs={{0,2},{1,3},{2,0},{3,1},{4,6},{5,7},{6,4},{7,5},{8,10},{9,11},{10,... | collective-permute-start | bytes 245768 | tf_op jit(solution)/shard_map/ppermute | solution.py:503
  26.8 5.3 %collective-permute-start.6 = (f32[16,1280]{1,0:T(8,128)S(1)}, f32[16,1280]{1,0:T(8,128)S(1)}, u32[]{:S(2)}, u32[]{:S(2)}) collective-permute-start(f32[16,1280]{1,0:T(8,128)S(1)} %add.22), channel_id=1, source_target_pairs={{0,1},{1,0},{2,3},{3,2},{4,5},{5,4},{6,7},{7,6},{8,9},{9,8},{10,11... | collective-permute-start | bytes 245768 | tf_op jit(solution)/shard_map/ppermute | solution.py:503
  32.1 6.6 %collective-permute-start.9 = (f32[16,1280]{1,0:T(8,128)S(1)}, f32[16,1280]{1,0:T(8,128)S(1)}, u32[]{:S(2)}, u32[]{:S(2)}) collective-permute-start(f32[16,1280]{1,0:T(8,128)S(1)} %add_add_fusion), channel_id=1, source_target_pairs={{0,4},{1,5},{2,6},{3,7},{4,0},{5,1},{6,2},{7,3},{8,12},{9,13},{10,... | collective-permute-start | bytes 245768 | tf_op jit(solution)/shard_map/ppermute | solution.py:503
  34.5 8.5 %collective-permute-start.2 = (f32[64,128]{1,0:T(8,128)S(1)}, f32[64,128]{1,0:T(8,128)S(1)}, u32[]{:S(2)}, u32[]{:S(2)}) collective-permute-start(f32[64,128]{1,0:T(8,128)S(1)} %get-tuple-element.29), channel_id=1, source_target_pairs={{0,64},{64,128},{128,192},{192,0},{1,65},{65,129},{129,193},{193,1... | collective-permute-start | bytes 98312 | tf_op jit(solution)/shard_map/ppermute | solution.py:496
  34.5 8.5 %collective-permute-start.3 = (f32[64,128]{1,0:T(8,128)S(1)}, f32[64,128]{1,0:T(8,128)S(1)}, u32[]{:S(2)}, u32[]{:S(2)}) collective-permute-start(f32[64,128]{1,0:T(8,128)S(1)} %get-tuple-element.30), channel_id=1, source_target_pairs={{0,192},{64,0},{128,64},{192,128},{1,193},{65,1},{129,65},{193,129... | collective-permute-start | bytes 98312 | tf_op jit(solution)/shard_map/ppermute | solution.py:496
  38.7 8.4 %collective-permute-start.10 = (f32[16,1280]{1,0:T(8,128)S(1)}, f32[16,1280]{1,0:T(8,128)S(1)}, u32[]{:S(2)}, u32[]{:S(2)}) collective-permute-start(f32[16,1280]{1,0:T(8,128)S(1)} %add.26), channel_id=1, source_target_pairs={{0,40},{1,41},{2,42},{3,43},{4,44},{5,45},{6,46},{7,47},{8,32},{9,... | collective-permute-start | bytes 245768 | tf_op jit(solution)/shard_map/ppermute | solution.py:503
  43.0 4.1 %copy-start.6 = (f32[16,1280]{1,0:T(8,128)S(1)}, f32[16,1280]{1,0:T(8,128)}, u32[]{:S(2)}) copy-start(f32[16,1280]{1,0:T(8,128)} %param.14) | copy-start | bytes 245764

commit v5 on v4

--- a/solution.py
+++ b/solution.py
@@ -496,9 +496,9 @@
     return lax.ppermute(block, "net", [(i, (i + distance) % size) for i in range(size)])
 
 
-def sum_cases(value):
+def sum_cases(value, masks_of_steps):
     size = lax.axis_size("ctg")
-    for masks in ((8,), (16,), (1, 2, 3), (4,), (40,)):
+    for masks in masks_of_steps:
         parts = [
             lax.ppermute(value, "ctg", [(i, i ^ mask) for i in range(size)]) for mask in masks
         ]
@@ -535,8 +535,11 @@
         dispatch_dir,
         gen_bus,
     )
-    halos = (shifted(last, 1), shifted(first, -1))
-    summed = sum_cases(partial)
+    partial = sum_cases(partial, ((8,), (16,)))
+    partial, *halos = lax.optimization_barrier(
+        (partial, shifted(last, 1), shifted(first, -1))
+    )
+    summed = sum_cases(partial, ((1, 2, 3), (4,), (40,)))
     angle_out = angles(
         weighted, field, angle_reg, (high, low), cross, degree, ends, halos
     )

time: 47.9 us -> 47.9 us (level)
  waiting for transfers between devices: 16.3 us -> 15.7 us
    ppermute x7, waiting for transfers between devices: 16.2 us -> 15.6 us  [sum_cases(): lax.ppermute(value, 'ctg', [(i, i ^ mask) for i in range(size)])]
    ppermute x7, starting transfers between devices: 16.3 us -> 16.8 us  [sum_cases(): lax.ppermute(value, 'ctg', [(i, i ^ mask) for i in range(size)])]
where the time goes in v5:
time: 47.9 us; the launch traced here: 47.7 us
  starting transfers between devices  19.1 us (40%)
  waiting for transfers between devices  15.7 us (33%)
  Pallas kernels  11.3 us (24%)
  between operations  0.74 us (2%)
  other arithmetic  0.71 us (1%)
    ppermute x7, starting transfers between devices, sum_cases(): lax.ppermute(value, 'ctg', [(i, i ^ mask) for i in range(size)])  16.8 us
    ppermute x7, waiting for transfers between devices, sum_cases(): lax.ppermute(value, 'ctg', [(i, i ^ mask) for i in range(size)])  15.6 us
    pallas_call x1, Pallas kernels, build_band(): pl.pallas_call(band_kernel, in_specs=[whole()] * 3, out_specs=[whole()] *...  4.42 us
    pallas_call x1, Pallas kernels, residuals(): pl.pallas_call(resid_kernel, in_specs=[whole()] * 11, out_specs=[whole()]...  3.45 us
    pallas_call x1, Pallas kernels, angles(): pl.pallas_call(angle_kernel, in_specs=[whole()] * 10, out_specs=whole(),...  2.58 us
    ppermute x4, starting transfers between devices, shifted(): lax.ppermute(block, 'net', [(i, (i + distance) % size) for i in range(siz...  2.32 us
  transfers between devices with their start and end apart: 11, of which 7 were waited for; matrix products, arithmetic and copies ran while one was open for 0% of the time, Pallas kernels for 15%

profile of v5, /device:TPU:2, one launch (start us, length us, event | category | flops | bytes accessed | tf_op | source)
XLA Modules:
  0.0 47.7 jit_solution(8659318150059579512)
XLA Ops:
  0.6 0.9 %pack.1 = (f32[208,128]{1,0:T(8,128)S(1)}, f32[64,128]{1,0:T(8,128)S(1)}, s32[5632]{0:T(1024)S(1)}, s32[5632]{0:T(1024)S(1)}, f32[5632]{0:T(1024)S(1)}) custom-call(s32[5632]{0:T(1024)} %from_hbm.1, s32[5632]{0:T(1024)} %to_hbm.1, f32[5632]{0:T(1024)} %susc_hbm.1, f32[64,4096]{1,0:T(8,128)} %bitcast.3), custom_call_target="tpu_custom_call" | custom-call | tf_op jit(solution)/shard_map/pack/pallas_call | solution.py:98
  1.5 0.1 collective-permute-start.1
  1.6 0.5 %collective-permute-start = (f32[208,128]{1,0:T(8,128)S(1)}, f32[208,128]{1,0:T(8,128)S(1)}, u32[]{:S(2)}, u32[]{:S(2)}) collective-permute-start(f32[208,128]{1,0:T(8,128)S(1)} %get-tuple-element.26.own_ref), channel_id=1, source_target_pairs={{0,64},{64,128},{128,192},{192,0},{1,65},{65,129},{129,193},{193,1... | collective-permute-start | bytes 319496 | tf_op jit(solution)/shard_map/ppermute | solution.py:496
  2.1 0.0 copy-start.5
  2.1 4.4 %band.1 = (bf16[16,512,256]{2,1,0:T(8,128)(2,1)S(1)}, bf16[16,512,256]{2,1,0:T(8,128)(2,1)S(1)}, f32[1,4096]{1,0:T(1,128)S(1)}) custom-call(s32[5632]{0:T(1024)S(1)} %get-tuple-element.20.from_ref, s32[5632]{0:T(1024)S(1)} %get-tuple-element.21.to_ref, f32[5632]{0:T(1024)S(1)} %get-tuple-element.22.susc_ref), custom_call_target="tpu_custom_call" | custom-call | flops 8589934592 | bytes 16777216 | tf_op jit(solution)/shard_map/band/pallas_call | solution.py:222
  6.5 0.0 collective-permute-done.1.right_ref
  6.6 0.2 collective-permute-done.left_ref
  6.7 0.0 copy-done
  6.7 0.0 copy-done.1
  6.7 0.0 copy-start.3
  6.8 3.4 %resid.1 = (f32[64,4096]{1,0:T(8,128)S(1)}, f32[64,128]{1,0:T(8,128)S(1)}, f32[64,128]{1,0:T(8,128)S(1)}, f32[16,1280]{1,0:T(8,128)S(1)}, bf16[128,256]{1,0:T(8,...) custom-call(s32[4]{0:T(128)S(1)} %copy-done.5, f32[64,4096]{1,0:T(8,128)S(1)} %bitcast.4, ...), custom_call_target="tpu_custom_call" | custom-call | flops 4294967296 | bytes 8388608 | tf_op jit(solution)/shard_map/resid/pallas_call | solution.py:419
  10.2 1.9 %collective-permute-start.2 = (f32[16,1280]{1,0:T(8,128)S(1)}, f32[16,1280]{1,0:T(8,128)S(1)}, u32[]{:S(2)}, u32[]{:S(2)}) collective-permute-start(f32[16,1280]{1,0:T(8,128)S(1)} %get-tuple-element.32), channel_id=1, source_target_pairs={{0,8},{1,9},{2,10},{3,11},{4,12},{5,13},{6,14},{7,15},{8,0},{9,1},... | collective-permute-start | bytes 245768 | tf_op jit(solution)/shard_map/ppermute | solution.py:503
  12.1 2.7 %collective-permute-done.2 = f32[16,1280]{1,0:T(8,128)S(1)} collective-permute-done((f32[16,1280]{1,0:T(8,128)S(1)}, f32[16,1280]{1,0:T(8,128)S(1)}, u32[]{:S(2)}, u32[]{:S(2)}) %collective-permute-start.2) | collective-permute-done | bytes 81952 | tf_op jit(solution)/shard_map/ppermute | solution.py:503
  14.7 3.6 %collective-permute-start.3 = (f32[16,1280]{1,0:T(8,128)S(1)}, f32[16,1280]{1,0:T(8,128)S(1)}, u32[]{:S(2)}, u32[]{:S(2)}) collective-permute-start(f32[16,1280]{1,0:T(8,128)S(1)} %add.21), channel_id=1, source_target_pairs={{0,16},{1,17},{2,18},{3,19},{4,20},{5,21},{6,22},{7,23},{8,24},{9,... | collective-permute-start | bytes 245768 | tf_op jit(solution)/shard_map/ppermute | solution.py:503
  18.3 0.1 collective-permute-start.4
  18.4 1.7 %collective-permute-start.5 = (f32[64,128]{1,0:T(8,128)S(1)}, f32[64,128]{1,0:T(8,128)S(1)}, u32[]{:S(2)}, u32[]{:S(2)}) collective-permute-start(f32[64,128]{1,0:T(8,128)S(1)} %get-tuple-element.34), channel_id=1, source_target_pairs={{0,192},{64,0},{128,64},{192,128},{1,193},{65,1},{129,65},{193,129... | collective-permute-start | bytes 98312 | tf_op jit(solution)/shard_map/ppermute | solution.py:496
  20.1 3.0 %collective-permute-done.3 = f32[16,1280]{1,0:T(8,128)S(1)} collective-permute-done((f32[16,1280]{1,0:T(8,128)S(1)}, f32[16,1280]{1,0:T(8,128)S(1)}, u32[]{:S(2)}, u32[]{:S(2)}) %collective-permute-start.3) | collective-permute-done | bytes 81952 | tf_op jit(solution)/shard_map/ppermute | solution.py:503
  23.1 0.0 collective-permute-done.4.left_ref
  23.1 0.0 collective-permute-done.5.right_ref
  23.1 3.3 %collective-permute-start.8 = (f32[16,1280]{1,0:T(8,128)S(1)}, f32[16,1280]{1,0:T(8,128)S(1)}, u32[]{:S(2)}, u32[]{:S(2)}) collective-permute-start(f32[16,1280]{1,0:T(8,128)S(1)} %add.22), channel_id=1, source_target_pairs={{0,3},{1,2},{2,1},{3,0},{4,7},{5,6},{6,5},{7,4},{8,11},{9,10},{10,... | collective-permute-start | bytes 245768 | tf_op jit(solution)/shard_map/ppermute | solution.py:503
  26.4 0.6 %collective-permute-start.7 = (f32[16,1280]{1,0:T(8,128)S(1)}, f32[16,1280]{1,0:T(8,128)S(1)}, u32[]{:S(2)}, u32[]{:S(2)}) collective-permute-start(f32[16,1280]{1,0:T(8,128)S(1)} %add.22), channel_id=1, source_target_pairs={{0,2},{1,3},{2,0},{3,1},{4,6},{5,7},{6,4},{7,5},{8,10},{9,11},{10,... | collective-permute-start | bytes 245768 | tf_op jit(solution)/shard_map/ppermute | solution.py:503
  27.0 0.4 collective-permute-start.6
  27.4 2.5 %collective-permute-done.8 = f32[16,1280]{1,0:T(8,128)S(1)} collective-permute-done((f32[16,1280]{1,0:T(8,128)S(1)}, f32[16,1280]{1,0:T(8,128)S(1)}, u32[]{:S(2)}, u32[]{:S(2)}) %collective-permute-start.8) | collective-permute-done | bytes 81952 | tf_op jit(solution)/shard_map/ppermute | solution.py:503
  29.9 2.8 %collective-permute-done.7 = f32[16,1280]{1,0:T(8,128)S(1)} collective-permute-done((f32[16,1280]{1,0:T(8,128)S(1)}, f32[16,1280]{1,0:T(8,128)S(1)}, u32[]{:S(2)}, u32[]{:S(2)}) %collective-permute-start.7) | collective-permute-done | bytes 81952 | tf_op jit(solution)/shard_map/ppermute | solution.py:503
  32.7 0.0 collective-permute-done.6
  32.7 2.1 %collective-permute-start.9 = (f32[16,1280]{1,0:T(8,128)S(1)}, f32[16,1280]{1,0:T(8,128)S(1)}, u32[]{:S(2)}, u32[]{:S(2)}) collective-permute-start(f32[16,1280]{1,0:T(8,128)S(1)} %add_add_fusion), channel_id=1, source_target_pairs={{0,4},{1,5},{2,6},{3,7},{4,0},{5,1},{6,2},{7,3},{8,12},{9,13},{10,... | collective-permute-start | bytes 245768 | tf_op jit(solution)/shard_map/ppermute | solution.py:503
  34.9 3.9 %collective-permute-done.9 = f32[16,1280]{1,0:T(8,128)S(1)} collective-permute-done((f32[16,1280]{1,0:T(8,128)S(1)}, f32[16,1280]{1,0:T(8,128)S(1)}, u32[]{:S(2)}, u32[]{:S(2)}) %collective-permute-start.9) | collective-permute-done | bytes 81952 | tf_op jit(solution)/shard_map/ppermute | solution.py:503
  38.8 4.9 %collective-permute-start.10 = (f32[16,1280]{1,0:T(8,128)S(1)}, f32[16,1280]{1,0:T(8,128)S(1)}, u32[]{:S(2)}, u32[]{:S(2)}) collective-permute-start(f32[16,1280]{1,0:T(8,128)S(1)} %add.26), channel_id=1, source_target_pairs={{0,40},{1,41},{2,42},{3,43},{4,44},{5,45},{6,46},{7,47},{8,32},{9,... | collective-permute-start | bytes 245768 | tf_op jit(solution)/shard_map/ppermute | solution.py:503
  43.6 0.0 copy-done.3
  43.6 2.6 %angles.1 = f32[64,4096]{1,0:T(8,128)} custom-call(f32[64,4096]{1,0:T(8,128)S(1)} %get-tuple-element.28.weighted_ref, f32[64,4096]{1,0:T(8,128)S(1)} %bitcast.5, f32[16,4096]{1,0:T(8,128)S(1)} %copy-done.3, bf16[16,512,256]{2,1,0:T(8,128)(2,1)S(1)} %get-tuple-element.23.high_ref, bf16[16,512,256]{2,1,0:T(8,128)(2,1)S(1)} %get-tuple-element.24.low_ref, ...), custom_call_target="tpu_custom_call" | custom-call | flops 4294967296 | bytes 8388608 | tf_op jit(solution)/shard_map/angles/pallas_call | solution.py:482
  46.2 0.8 %collective-permute-done.10 = f32[16,1280]{1,0:T(8,128)S(1)} collective-permute-done((f32[16,1280]{1,0:T(8,128)S(1)}, f32[16,1280]{1,0:T(8,128)S(1)}, u32[]{:S(2)}, u32[]{:S(2)}) %collective-permute-start.10) | collective-permute-done | bytes 81952 | tf_op jit(solution)/shard_map/ppermute | solution.py:503
  47.0 0.7 %multiply_subtract_fusion = f32[16,1280]{1,0:T(8,128)} fusion(f32[16,1280]{1,0:T(8,128)S(1)} %add.26, f32[16,1280]{1,0:T(8,128)S(1)} %collective-permute-done.10, f32[16,1280]{1,0:T(8,128)S(1)} %copy-done.6, f32[16,1280]{1,0:T(8,128)S(1)} %copy-done.1), kind=kLoop, calls=%fused_computation | loop fusion | flops 81920 | bytes 409600 | tf_op jit(solution)/shard_map/sub | solution.py:547
  (13 shorter events, 0.1 us)
Async XLA Ops:
  1.5 5.0 %collective-permute-start.1 = (f32[64,128]{1,0:T(8,128)S(1)}, f32[64,128]{1,0:T(8,128)S(1)}, u32[]{:S(2)}, u32[]{:S(2)}) collective-permute-start(f32[64,128]{1,0:T(8,128)S(1)} %get-tuple-element.27), channel_id=1, source_target_pairs={{0,192},{64,0},{128,64},{192,128},{1,193},{65,1},{129,65},{193,129... | collective-permute-start | bytes 98312 | tf_op jit(solution)/shard_map/ppermute | solution.py:496
  1.6 5.1 %collective-permute-start = (f32[208,128]{1,0:T(8,128)S(1)}, f32[208,128]{1,0:T(8,128)S(1)}, u32[]{:S(2)}, u32[]{:S(2)}) collective-permute-start(f32[208,128]{1,0:T(8,128)S(1)} %get-tuple-element.26.own_ref), channel_id=1, source_target_pairs={{0,64},{64,128},{128,192},{192,0},{1,65},{65,129},{129,193},{193,1... | collective-permute-start | bytes 319496 | tf_op jit(solution)/shard_map/ppermute | solution.py:496
  2.1 4.6 %copy-start = (f32[4,16,4096]{2,1,0:T(8,128)S(1)}, f32[4,16,4096]{2,1,0:T(8,128)}, u32[]{:S(2)}) copy-start(f32[4,16,4096]{2,1,0:T(8,128)} %param.10) | copy-start | bytes 3145732
  2.1 4.6 %copy-start.1 = (f32[16,1280]{1,0:T(8,128)S(1)}, f32[16,1280]{1,0:T(8,128)}, u32[]{:S(2)}) copy-start(f32[16,1280]{1,0:T(8,128)} %dispatch_ref.1) | copy-start | bytes 245764
  2.1 4.6 %copy-start.2 = (bf16[4,16,4096]{2,1,0:T(8,128)(2,1)S(1)}, bf16[4,16,4096]{2,1,0:T(8,128)(2,1)}, u32[]{:S(2)}) copy-start(bf16[4,16,4096]{2,1,0:T(8,128)(2,1)} %param.12) | copy-start | bytes 1572868
  2.1 4.6 %copy-start.4 = (s32[1280]{0:T(1024)S(1)}, s32[1280]{0:T(1024)}, u32[]{:S(2)}) copy-start(s32[1280]{0:T(1024)} %gen_ref.1) | copy-start | bytes 15364
  2.1 4.6 %copy-start.5 = (s32[4]{0:T(128)S(1)}, s32[4]{0:T(128)}, u32[]{:S(2)}) copy-start(s32[4]{0:T(128)} %outage_ref.1) | copy-start | bytes 52
  6.7 36.9 %copy-start.3 = (f32[16,4096]{1,0:T(8,128)S(1)}, f32[16,4096]{1,0:T(8,128)}, u32[]{:S(2)}) copy-start(f32[16,4096]{1,0:T(8,128)} %reg_ref.1) | copy-start | bytes 786436
  10.2 4.5 %collective-permute-start.2 = (f32[16,1280]{1,0:T(8,128)S(1)}, f32[16,1280]{1,0:T(8,128)S(1)}, u32[]{:S(2)}, u32[]{:S(2)}) collective-permute-start(f32[16,1280]{1,0:T(8,128)S(1)} %get-tuple-element.32), channel_id=1, source_target_pairs={{0,8},{1,9},{2,10},{3,11},{4,12},{5,13},{6,14},{7,15},{8,0},{9,1},... | collective-permute-start | bytes 245768 | tf_op jit(solution)/shard_map/ppermute | solution.py:503
  14.7 8.3 %collective-permute-start.3 = (f32[16,1280]{1,0:T(8,128)S(1)}, f32[16,1280]{1,0:T(8,128)S(1)}, u32[]{:S(2)}, u32[]{:S(2)}) collective-permute-start(f32[16,1280]{1,0:T(8,128)S(1)} %add.21), channel_id=1, source_target_pairs={{0,16},{1,17},{2,18},{3,19},{4,20},{5,21},{6,22},{7,23},{8,24},{9,... | collective-permute-start | bytes 245768 | tf_op jit(solution)/shard_map/ppermute | solution.py:503
  18.3 4.7 %collective-permute-start.4 = (f32[64,128]{1,0:T(8,128)S(1)}, f32[64,128]{1,0:T(8,128)S(1)}, u32[]{:S(2)}, u32[]{:S(2)}) collective-permute-start(f32[64,128]{1,0:T(8,128)S(1)} %get-tuple-element.33), channel_id=1, source_target_pairs={{0,64},{64,128},{128,192},{192,0},{1,65},{65,129},{129,193},{193,1... | collective-permute-start | bytes 98312 | tf_op jit(solution)/shard_map/ppermute | solution.py:496
  18.4 4.7 %collective-permute-start.5 = (f32[64,128]{1,0:T(8,128)S(1)}, f32[64,128]{1,0:T(8,128)S(1)}, u32[]{:S(2)}, u32[]{:S(2)}) collective-permute-start(f32[64,128]{1,0:T(8,128)S(1)} %get-tuple-element.34), channel_id=1, source_target_pairs={{0,192},{64,0},{128,64},{192,128},{1,193},{65,1},{129,65},{193,129... | collective-permute-start | bytes 98312 | tf_op jit(solution)/shard_map/ppermute | solution.py:496
  23.1 6.8 %collective-permute-start.8 = (f32[16,1280]{1,0:T(8,128)S(1)}, f32[16,1280]{1,0:T(8,128)S(1)}, u32[]{:S(2)}, u32[]{:S(2)}) collective-permute-start(f32[16,1280]{1,0:T(8,128)S(1)} %add.22), channel_id=1, source_target_pairs={{0,3},{1,2},{2,1},{3,0},{4,7},{5,6},{6,5},{7,4},{8,11},{9,10},{10,... | collective-permute-start | bytes 245768 | tf_op jit(solution)/shard_map/ppermute | solution.py:503
  26.4 6.3 %collective-permute-start.7 = (f32[16,1280]{1,0:T(8,128)S(1)}, f32[16,1280]{1,0:T(8,128)S(1)}, u32[]{:S(2)}, u32[]{:S(2)}) collective-permute-start(f32[16,1280]{1,0:T(8,128)S(1)} %add.22), channel_id=1, source_target_pairs={{0,2},{1,3},{2,0},{3,1},{4,6},{5,7},{6,4},{7,5},{8,10},{9,11},{10,... | collective-permute-start | bytes 245768 | tf_op jit(solution)/shard_map/ppermute | solution.py:503
  27.0 5.7 %collective-permute-start.6 = (f32[16,1280]{1,0:T(8,128)S(1)}, f32[16,1280]{1,0:T(8,128)S(1)}, u32[]{:S(2)}, u32[]{:S(2)}) collective-permute-start(f32[16,1280]{1,0:T(8,128)S(1)} %add.22), channel_id=1, source_target_pairs={{0,1},{1,0},{2,3},{3,2},{4,5},{5,4},{6,7},{7,6},{8,9},{9,8},{10,11... | collective-permute-start | bytes 245768 | tf_op jit(solution)/shard_map/ppermute | solution.py:503
  32.7 6.0 %collective-permute-start.9 = (f32[16,1280]{1,0:T(8,128)S(1)}, f32[16,1280]{1,0:T(8,128)S(1)}, u32[]{:S(2)}, u32[]{:S(2)}) collective-permute-start(f32[16,1280]{1,0:T(8,128)S(1)} %add_add_fusion), channel_id=1, source_target_pairs={{0,4},{1,5},{2,6},{3,7},{4,0},{5,1},{6,2},{7,3},{8,12},{9,13},{10,... | collective-permute-start | bytes 245768 | tf_op jit(solution)/shard_map/ppermute | solution.py:503
  38.8 8.2 %collective-permute-start.10 = (f32[16,1280]{1,0:T(8,128)S(1)}, f32[16,1280]{1,0:T(8,128)S(1)}, u32[]{:S(2)}, u32[]{:S(2)}) collective-permute-start(f32[16,1280]{1,0:T(8,128)S(1)} %add.26), channel_id=1, source_target_pairs={{0,40},{1,41},{2,42},{3,43},{4,44},{5,45},{6,46},{7,47},{8,32},{9,... | collective-permute-start | bytes 245768 | tf_op jit(solution)/shard_map/ppermute | solution.py:503
  43.6 3.4 %copy-start.6 = (f32[16,1280]{1,0:T(8,128)S(1)}, f32[16,1280]{1,0:T(8,128)}, u32[]{:S(2)}) copy-start(f32[16,1280]{1,0:T(8,128)} %param.14) | copy-start | bytes 245764

commit v6 on v5

--- a/solution.py
+++ b/solution.py
@@ -186,35 +186,41 @@
     narrow = [x.astype(F32).astype(BF16) for x in (rows, cols)]
     above, below = narrow[1] > narrow[0], narrow[1] < narrow[0]
     zero = jnp.zeros((RIM, RIM), BF16)
-    carried = jnp.zeros((1, RIM), F32)
-    for at in range(TILES):
-        pair, odd = at // 2, at % 2
-        turned = group_tile(at) + jnp.where(spill > 0, tiles[at], 0.0)
-        block = turned.T
-        own = slice((1 + odd) * RIM, (2 + odd) * RIM)
-        mine = slice(odd * RIM, (odd + 1) * RIM)
-        other = slice((1 - odd) * RIM, (2 - odd) * RIM)
-        for ref, part, back in zip((high_ref, low_ref), split(block), split(turned)):
-            inside_part = jnp.where(above, part, jnp.where(below, back, zero))
-            ahead_part = jnp.where(above, zero, part)
-            back_part = jnp.where(below, zero, back)
-            ref[pair, own, mine] = inside_part
-            if odd == 0:
-                ref[pair, 2 * RIM : 3 * RIM, mine] = back_part
-                ref[pair, 3 * RIM :, mine] = zero
-                ref[pair, RIM : 2 * RIM, other] = ahead_part
-                if pair == 0:
+    def finish(spilled):
+        carried = jnp.zeros((1, RIM), F32)
+        for at in range(TILES):
+            pair, odd = at // 2, at % 2
+            turned = group_tile(at)
+            if spilled:
+                turned = turned + tiles[at]
+            block = turned.T
+            own = slice((1 + odd) * RIM, (2 + odd) * RIM)
+            mine = slice(odd * RIM, (odd + 1) * RIM)
+            other = slice((1 - odd) * RIM, (2 - odd) * RIM)
+            for ref, part, back in zip((high_ref, low_ref), split(block), split(turned)):
+                inside_part = jnp.where(above, part, jnp.where(below, back, zero))
+                ahead_part = jnp.where(above, zero, part)
+                back_part = jnp.where(below, zero, back)
+                ref[pair, own, mine] = inside_part
+                if odd == 0:
+                    ref[pair, 2 * RIM : 3 * RIM, mine] = back_part
+                    ref[pair, 3 * RIM :, mine] = zero
+                    ref[pair, RIM : 2 * RIM, other] = ahead_part
+                    if pair == 0:
+                        ref[pair, :RIM, mine] = zero
+                else:
+                    ref[pair, 3 * RIM :, mine] = back_part
                     ref[pair, :RIM, mine] = zero
-            else:
-                ref[pair, 3 * RIM :, mine] = back_part
-                ref[pair, :RIM, mine] = zero
-                if pair + 1 < PAIRS:
-                    ref[pair + 1, :RIM, :RIM] = ahead_part
-        inside = jnp.sum(jnp.where(later, block, 0.0), axis=0, keepdims=True)
-        degree_ref[:, at * RIM : (at + 1) * RIM] = (
-            inside + jnp.sum(turned, axis=0, keepdims=True) + carried
-        )
-        carried = jnp.sum(jnp.where(later, 0.0, block), axis=0, keepdims=True)
+                    if pair + 1 < PAIRS:
+                        ref[pair + 1, :RIM, :RIM] = ahead_part
+            inside = jnp.sum(jnp.where(later, block, 0.0), axis=0, keepdims=True)
+            degree_ref[:, at * RIM : (at + 1) * RIM] = (
+                inside + jnp.sum(turned, axis=0, keepdims=True) + carried
+            )
+            carried = jnp.sum(jnp.where(later, 0.0, block), axis=0, keepdims=True)
+
+    pl.when(spill == 0)(lambda: finish(False))
+    pl.when(spill > 0)(lambda: finish(True))
 
 
 def build_band(from_bus, to_bus, susceptance):

time: 47.9 us -> 48 us (level)
  waiting for transfers between devices: 15.7 us -> 16.3 us
  transfers between devices with their start and end apart: 11 -> 11, of which waited for: 7 -> 7; matrix products, arithmetic and copies ran while one was open for 0% -> 0% of each run, Pallas kernels for 15% -> 14%
where the time goes in v6:
time: 48 us; the launch traced here: 47.7 us
  starting transfers between devices  18.7 us (39%)
  waiting for transfers between devices  16.3 us (34%)
  Pallas kernels  11.2 us (23%)
  between operations  0.75 us (2%)
  other arithmetic  0.71 us (1%)
    ppermute x7, starting transfers between devices, sum_cases(): lax.ppermute(value, 'ctg', [(i, i ^ mask) for i in range(size)])  16.4 us
    ppermute x7, waiting for transfers between devices, sum_cases(): lax.ppermute(value, 'ctg', [(i, i ^ mask) for i in range(size)])  16 us
    pallas_call x1, Pallas kernels, build_band(): pl.pallas_call(band_kernel, in_specs=[whole()] * 3, out_specs=[whole()] *...  4.32 us
    pallas_call x1, Pallas kernels, residuals(): pl.pallas_call(resid_kernel, in_specs=[whole()] * 11, out_specs=[whole()]...  3.45 us
    pallas_call x1, Pallas kernels, angles(): pl.pallas_call(angle_kernel, in_specs=[whole()] * 10, out_specs=whole(),...  2.58 us
    ppermute x4, starting transfers between devices, shifted(): lax.ppermute(block, 'net', [(i, (i + distance) % size) for i in range(siz...  2.32 us
  transfers between devices with their start and end apart: 11, of which 7 were waited for; matrix products, arithmetic and copies ran while one was open for 0% of the time, Pallas kernels for 14%

profile of v6, /device:TPU:2, one launch (start us, length us, event | category | flops | bytes accessed | tf_op | source)
XLA Modules:
  0.0 47.7 jit_solution(18052526390510431745)
XLA Ops:
  0.6 0.9 %pack.1 = (f32[208,128]{1,0:T(8,128)S(1)}, f32[64,128]{1,0:T(8,128)S(1)}, s32[5632]{0:T(1024)S(1)}, s32[5632]{0:T(1024)S(1)}, f32[5632]{0:T(1024)S(1)}) custom-call(s32[5632]{0:T(1024)} %from_hbm.1, s32[5632]{0:T(1024)} %to_hbm.1, f32[5632]{0:T(1024)} %susc_hbm.1, f32[64,4096]{1,0:T(8,128)} %bitcast.3), custom_call_target="tpu_custom_call" | custom-call | tf_op jit(solution)/shard_map/pack/pallas_call | solution.py:98
  1.5 0.1 collective-permute-start.1
  1.6 0.5 %collective-permute-start = (f32[208,128]{1,0:T(8,128)S(1)}, f32[208,128]{1,0:T(8,128)S(1)}, u32[]{:S(2)}, u32[]{:S(2)}) collective-permute-start(f32[208,128]{1,0:T(8,128)S(1)} %get-tuple-element.26.own_ref), channel_id=1, source_target_pairs={{0,64},{64,128},{128,192},{192,0},{1,65},{65,129},{129,193},{193,1... | collective-permute-start | bytes 319496 | tf_op jit(solution)/shard_map/ppermute | solution.py:502
  2.1 0.0 copy-start.5
  2.1 4.3 %band.1 = (bf16[16,512,256]{2,1,0:T(8,128)(2,1)S(1)}, bf16[16,512,256]{2,1,0:T(8,128)(2,1)S(1)}, f32[1,4096]{1,0:T(1,128)S(1)}) custom-call(s32[5632]{0:T(1024)S(1)} %get-tuple-element.20.from_ref, s32[5632]{0:T(1024)S(1)} %get-tuple-element.21.to_ref, f32[5632]{0:T(1024)S(1)} %get-tuple-element.22.susc_ref), custom_call_target="tpu_custom_call" | custom-call | flops 8589934592 | bytes 16777216 | tf_op jit(solution)/shard_map/band/pallas_call | solution.py:228
  6.4 0.0 collective-permute-done.1.right_ref
  6.5 0.2 collective-permute-done.left_ref
  6.7 0.0 copy-done
  6.7 0.0 copy-done.1
  6.7 0.0 copy-done.2
  6.7 0.0 copy-start.3
  6.8 3.4 %resid.1 = (f32[64,4096]{1,0:T(8,128)S(1)}, f32[64,128]{1,0:T(8,128)S(1)}, f32[64,128]{1,0:T(8,128)S(1)}, f32[16,1280]{1,0:T(8,128)S(1)}, bf16[128,256]{1,0:T(8,...) custom-call(s32[4]{0:T(128)S(1)} %copy-done.5, f32[64,4096]{1,0:T(8,128)S(1)} %bitcast.4, ...), custom_call_target="tpu_custom_call" | custom-call | flops 4294967296 | bytes 8388608 | tf_op jit(solution)/shard_map/resid/pallas_call | solution.py:425
  10.2 2.0 %collective-permute-start.2 = (f32[16,1280]{1,0:T(8,128)S(1)}, f32[16,1280]{1,0:T(8,128)S(1)}, u32[]{:S(2)}, u32[]{:S(2)}) collective-permute-start(f32[16,1280]{1,0:T(8,128)S(1)} %get-tuple-element.32), channel_id=1, source_target_pairs={{0,8},{1,9},{2,10},{3,11},{4,12},{5,13},{6,14},{7,15},{8,0},{9,1},... | collective-permute-start | bytes 245768 | tf_op jit(solution)/shard_map/ppermute | solution.py:509
  12.2 2.7 %collective-permute-done.2 = f32[16,1280]{1,0:T(8,128)S(1)} collective-permute-done((f32[16,1280]{1,0:T(8,128)S(1)}, f32[16,1280]{1,0:T(8,128)S(1)}, u32[]{:S(2)}, u32[]{:S(2)}) %collective-permute-start.2) | collective-permute-done | bytes 81952 | tf_op jit(solution)/shard_map/ppermute | solution.py:509
  14.9 3.3 %collective-permute-start.3 = (f32[16,1280]{1,0:T(8,128)S(1)}, f32[16,1280]{1,0:T(8,128)S(1)}, u32[]{:S(2)}, u32[]{:S(2)}) collective-permute-start(f32[16,1280]{1,0:T(8,128)S(1)} %add.21), channel_id=1, source_target_pairs={{0,16},{1,17},{2,18},{3,19},{4,20},{5,21},{6,22},{7,23},{8,24},{9,... | collective-permute-start | bytes 245768 | tf_op jit(solution)/shard_map/ppermute | solution.py:509
  18.2 0.3 collective-permute-start.4
  18.5 1.5 %collective-permute-start.5 = (f32[64,128]{1,0:T(8,128)S(1)}, f32[64,128]{1,0:T(8,128)S(1)}, u32[]{:S(2)}, u32[]{:S(2)}) collective-permute-start(f32[64,128]{1,0:T(8,128)S(1)} %get-tuple-element.34), channel_id=1, source_target_pairs={{0,192},{64,0},{128,64},{192,128},{1,193},{65,1},{129,65},{193,129... | collective-permute-start | bytes 98312 | tf_op jit(solution)/shard_map/ppermute | solution.py:502
  20.0 3.2 %collective-permute-done.3 = f32[16,1280]{1,0:T(8,128)S(1)} collective-permute-done((f32[16,1280]{1,0:T(8,128)S(1)}, f32[16,1280]{1,0:T(8,128)S(1)}, u32[]{:S(2)}, u32[]{:S(2)}) %collective-permute-start.3) | collective-permute-done | bytes 81952 | tf_op jit(solution)/shard_map/ppermute | solution.py:509
  23.1 0.0 collective-permute-done.4.left_ref
  23.2 0.0 collective-permute-done.5.right_ref
  23.2 3.1 %collective-permute-start.8 = (f32[16,1280]{1,0:T(8,128)S(1)}, f32[16,1280]{1,0:T(8,128)S(1)}, u32[]{:S(2)}, u32[]{:S(2)}) collective-permute-start(f32[16,1280]{1,0:T(8,128)S(1)} %add.22), channel_id=1, source_target_pairs={{0,3},{1,2},{2,1},{3,0},{4,7},{5,6},{6,5},{7,4},{8,11},{9,10},{10,... | collective-permute-start | bytes 245768 | tf_op jit(solution)/shard_map/ppermute | solution.py:509
  26.3 0.6 %collective-permute-start.7 = (f32[16,1280]{1,0:T(8,128)S(1)}, f32[16,1280]{1,0:T(8,128)S(1)}, u32[]{:S(2)}, u32[]{:S(2)}) collective-permute-start(f32[16,1280]{1,0:T(8,128)S(1)} %add.22), channel_id=1, source_target_pairs={{0,2},{1,3},{2,0},{3,1},{4,6},{5,7},{6,4},{7,5},{8,10},{9,11},{10,... | collective-permute-start | bytes 245768 | tf_op jit(solution)/shard_map/ppermute | solution.py:509
  26.9 0.5 collective-permute-start.6
  27.3 2.7 %collective-permute-done.8 = f32[16,1280]{1,0:T(8,128)S(1)} collective-permute-done((f32[16,1280]{1,0:T(8,128)S(1)}, f32[16,1280]{1,0:T(8,128)S(1)}, u32[]{:S(2)}, u32[]{:S(2)}) %collective-permute-start.8) | collective-permute-done | bytes 81952 | tf_op jit(solution)/shard_map/ppermute | solution.py:509
  30.0 2.8 %collective-permute-done.7 = f32[16,1280]{1,0:T(8,128)S(1)} collective-permute-done((f32[16,1280]{1,0:T(8,128)S(1)}, f32[16,1280]{1,0:T(8,128)S(1)}, u32[]{:S(2)}, u32[]{:S(2)}) %collective-permute-start.7) | collective-permute-done | bytes 81952 | tf_op jit(solution)/shard_map/ppermute | solution.py:509
  32.8 0.0 collective-permute-done.6
  32.8 2.1 %collective-permute-start.9 = (f32[16,1280]{1,0:T(8,128)S(1)}, f32[16,1280]{1,0:T(8,128)S(1)}, u32[]{:S(2)}, u32[]{:S(2)}) collective-permute-start(f32[16,1280]{1,0:T(8,128)S(1)} %add_add_fusion), channel_id=1, source_target_pairs={{0,4},{1,5},{2,6},{3,7},{4,0},{5,1},{6,2},{7,3},{8,12},{9,13},{10,... | collective-permute-start | bytes 245768 | tf_op jit(solution)/shard_map/ppermute | solution.py:509
  34.9 3.9 %collective-permute-done.9 = f32[16,1280]{1,0:T(8,128)S(1)} collective-permute-done((f32[16,1280]{1,0:T(8,128)S(1)}, f32[16,1280]{1,0:T(8,128)S(1)}, u32[]{:S(2)}, u32[]{:S(2)}) %collective-permute-start.9) | collective-permute-done | bytes 81952 | tf_op jit(solution)/shard_map/ppermute | solution.py:509
  38.9 4.8 %collective-permute-start.10 = (f32[16,1280]{1,0:T(8,128)S(1)}, f32[16,1280]{1,0:T(8,128)S(1)}, u32[]{:S(2)}, u32[]{:S(2)}) collective-permute-start(f32[16,1280]{1,0:T(8,128)S(1)} %add.26), channel_id=1, source_target_pairs={{0,40},{1,41},{2,42},{3,43},{4,44},{5,45},{6,46},{7,47},{8,32},{9,... | collective-permute-start | bytes 245768 | tf_op jit(solution)/shard_map/ppermute | solution.py:509
  43.7 2.6 %angles.1 = f32[64,4096]{1,0:T(8,128)} custom-call(f32[64,4096]{1,0:T(8,128)S(1)} %get-tuple-element.28.weighted_ref, f32[64,4096]{1,0:T(8,128)S(1)} %bitcast.5, f32[16,4096]{1,0:T(8,128)S(1)} %copy-done.3, bf16[16,512,256]{2,1,0:T(8,128)(2,1)S(1)} %get-tuple-element.23.high_ref, bf16[16,512,256]{2,1,0:T(8,128)(2,1)S(1)} %get-tuple-element.24.low_ref, ...), custom_call_target="tpu_custom_call" | custom-call | flops 4294967296 | bytes 8388608 | tf_op jit(solution)/shard_map/angles/pallas_call | solution.py:488
  46.3 0.7 %collective-permute-done.10 = f32[16,1280]{1,0:T(8,128)S(1)} collective-permute-done((f32[16,1280]{1,0:T(8,128)S(1)}, f32[16,1280]{1,0:T(8,128)S(1)}, u32[]{:S(2)}, u32[]{:S(2)}) %collective-permute-start.10) | collective-permute-done | bytes 81952 | tf_op jit(solution)/shard_map/ppermute | solution.py:509
  47.0 0.7 %multiply_subtract_fusion = f32[16,1280]{1,0:T(8,128)} fusion(f32[16,1280]{1,0:T(8,128)S(1)} %add.26, f32[16,1280]{1,0:T(8,128)S(1)} %collective-permute-done.10, f32[16,1280]{1,0:T(8,128)S(1)} %copy-done.6, f32[16,1280]{1,0:T(8,128)S(1)} %copy-done.1), kind=kLoop, calls=%fused_computation | loop fusion | flops 81920 | bytes 409600 | tf_op jit(solution)/shard_map/sub | solution.py:553
  (13 shorter events, 0.1 us)
Async XLA Ops:
  1.5 4.9 %collective-permute-start.1 = (f32[64,128]{1,0:T(8,128)S(1)}, f32[64,128]{1,0:T(8,128)S(1)}, u32[]{:S(2)}, u32[]{:S(2)}) collective-permute-start(f32[64,128]{1,0:T(8,128)S(1)} %get-tuple-element.27), channel_id=1, source_target_pairs={{0,192},{64,0},{128,64},{192,128},{1,193},{65,1},{129,65},{193,129... | collective-permute-start | bytes 98312 | tf_op jit(solution)/shard_map/ppermute | solution.py:502
  1.6 5.1 %collective-permute-start = (f32[208,128]{1,0:T(8,128)S(1)}, f32[208,128]{1,0:T(8,128)S(1)}, u32[]{:S(2)}, u32[]{:S(2)}) collective-permute-start(f32[208,128]{1,0:T(8,128)S(1)} %get-tuple-element.26.own_ref), channel_id=1, source_target_pairs={{0,64},{64,128},{128,192},{192,0},{1,65},{65,129},{129,193},{193,1... | collective-permute-start | bytes 319496 | tf_op jit(solution)/shard_map/ppermute | solution.py:502
  2.1 4.6 %copy-start = (f32[4,16,4096]{2,1,0:T(8,128)S(1)}, f32[4,16,4096]{2,1,0:T(8,128)}, u32[]{:S(2)}) copy-start(f32[4,16,4096]{2,1,0:T(8,128)} %param.10) | copy-start | bytes 3145732
  2.1 4.6 %copy-start.1 = (f32[16,1280]{1,0:T(8,128)S(1)}, f32[16,1280]{1,0:T(8,128)}, u32[]{:S(2)}) copy-start(f32[16,1280]{1,0:T(8,128)} %dispatch_ref.1) | copy-start | bytes 245764
  2.1 4.6 %copy-start.2 = (bf16[4,16,4096]{2,1,0:T(8,128)(2,1)S(1)}, bf16[4,16,4096]{2,1,0:T(8,128)(2,1)}, u32[]{:S(2)}) copy-start(bf16[4,16,4096]{2,1,0:T(8,128)(2,1)} %param.12) | copy-start | bytes 1572868
  2.1 4.6 %copy-start.4 = (s32[1280]{0:T(1024)S(1)}, s32[1280]{0:T(1024)}, u32[]{:S(2)}) copy-start(s32[1280]{0:T(1024)} %gen_ref.1) | copy-start | bytes 15364
  2.1 4.6 %copy-start.5 = (s32[4]{0:T(128)S(1)}, s32[4]{0:T(128)}, u32[]{:S(2)}) copy-start(s32[4]{0:T(128)} %outage_ref.1) | copy-start | bytes 52
  6.7 37.0 %copy-start.3 = (f32[16,4096]{1,0:T(8,128)S(1)}, f32[16,4096]{1,0:T(8,128)}, u32[]{:S(2)}) copy-start(f32[16,4096]{1,0:T(8,128)} %reg_ref.1) | copy-start | bytes 786436
  10.2 4.7 %collective-permute-start.2 = (f32[16,1280]{1,0:T(8,128)S(1)}, f32[16,1280]{1,0:T(8,128)S(1)}, u32[]{:S(2)}, u32[]{:S(2)}) collective-permute-start(f32[16,1280]{1,0:T(8,128)S(1)} %get-tuple-element.32), channel_id=1, source_target_pairs={{0,8},{1,9},{2,10},{3,11},{4,12},{5,13},{6,14},{7,15},{8,0},{9,1},... | collective-permute-start | bytes 245768 | tf_op jit(solution)/shard_map/ppermute | solution.py:509
  14.9 8.2 %collective-permute-start.3 = (f32[16,1280]{1,0:T(8,128)S(1)}, f32[16,1280]{1,0:T(8,128)S(1)}, u32[]{:S(2)}, u32[]{:S(2)}) collective-permute-start(f32[16,1280]{1,0:T(8,128)S(1)} %add.21), channel_id=1, source_target_pairs={{0,16},{1,17},{2,18},{3,19},{4,20},{5,21},{6,22},{7,23},{8,24},{9,... | collective-permute-start | bytes 245768 | tf_op jit(solution)/shard_map/ppermute | solution.py:509
  18.2 4.9 %collective-permute-start.4 = (f32[64,128]{1,0:T(8,128)S(1)}, f32[64,128]{1,0:T(8,128)S(1)}, u32[]{:S(2)}, u32[]{:S(2)}) collective-permute-start(f32[64,128]{1,0:T(8,128)S(1)} %get-tuple-element.33), channel_id=1, source_target_pairs={{0,64},{64,128},{128,192},{192,0},{1,65},{65,129},{129,193},{193,1... | collective-permute-start | bytes 98312 | tf_op jit(solution)/shard_map/ppermute | solution.py:502
  18.5 4.7 %collective-permute-start.5 = (f32[64,128]{1,0:T(8,128)S(1)}, f32[64,128]{1,0:T(8,128)S(1)}, u32[]{:S(2)}, u32[]{:S(2)}) collective-permute-start(f32[64,128]{1,0:T(8,128)S(1)} %get-tuple-element.34), channel_id=1, source_target_pairs={{0,192},{64,0},{128,64},{192,128},{1,193},{65,1},{129,65},{193,129... | collective-permute-start | bytes 98312 | tf_op jit(solution)/shard_map/ppermute | solution.py:502
  23.2 6.8 %collective-permute-start.8 = (f32[16,1280]{1,0:T(8,128)S(1)}, f32[16,1280]{1,0:T(8,128)S(1)}, u32[]{:S(2)}, u32[]{:S(2)}) collective-permute-start(f32[16,1280]{1,0:T(8,128)S(1)} %add.22), channel_id=1, source_target_pairs={{0,3},{1,2},{2,1},{3,0},{4,7},{5,6},{6,5},{7,4},{8,11},{9,10},{10,... | collective-permute-start | bytes 245768 | tf_op jit(solution)/shard_map/ppermute | solution.py:509
  26.3 6.5 %collective-permute-start.7 = (f32[16,1280]{1,0:T(8,128)S(1)}, f32[16,1280]{1,0:T(8,128)S(1)}, u32[]{:S(2)}, u32[]{:S(2)}) collective-permute-start(f32[16,1280]{1,0:T(8,128)S(1)} %add.22), channel_id=1, source_target_pairs={{0,2},{1,3},{2,0},{3,1},{4,6},{5,7},{6,4},{7,5},{8,10},{9,11},{10,... | collective-permute-start | bytes 245768 | tf_op jit(solution)/shard_map/ppermute | solution.py:509
  26.9 5.9 %collective-permute-start.6 = (f32[16,1280]{1,0:T(8,128)S(1)}, f32[16,1280]{1,0:T(8,128)S(1)}, u32[]{:S(2)}, u32[]{:S(2)}) collective-permute-start(f32[16,1280]{1,0:T(8,128)S(1)} %add.22), channel_id=1, source_target_pairs={{0,1},{1,0},{2,3},{3,2},{4,5},{5,4},{6,7},{7,6},{8,9},{9,8},{10,11... | collective-permute-start | bytes 245768 | tf_op jit(solution)/shard_map/ppermute | solution.py:509
  32.8 6.0 %collective-permute-start.9 = (f32[16,1280]{1,0:T(8,128)S(1)}, f32[16,1280]{1,0:T(8,128)S(1)}, u32[]{:S(2)}, u32[]{:S(2)}) collective-permute-start(f32[16,1280]{1,0:T(8,128)S(1)} %add_add_fusion), channel_id=1, source_target_pairs={{0,4},{1,5},{2,6},{3,7},{4,0},{5,1},{6,2},{7,3},{8,12},{9,13},{10,... | collective-permute-start | bytes 245768 | tf_op jit(solution)/shard_map/ppermute | solution.py:509
  38.9 8.2 %collective-permute-start.10 = (f32[16,1280]{1,0:T(8,128)S(1)}, f32[16,1280]{1,0:T(8,128)S(1)}, u32[]{:S(2)}, u32[]{:S(2)}) collective-permute-start(f32[16,1280]{1,0:T(8,128)S(1)} %add.26), channel_id=1, source_target_pairs={{0,40},{1,41},{2,42},{3,43},{4,44},{5,45},{6,46},{7,47},{8,32},{9,... | collective-permute-start | bytes 245768 | tf_op jit(solution)/shard_map/ppermute | solution.py:509
  43.7 3.3 %copy-start.6 = (f32[16,1280]{1,0:T(8,128)S(1)}, f32[16,1280]{1,0:T(8,128)}, u32[]{:S(2)}) copy-start(f32[16,1280]{1,0:T(8,128)} %param.14) | copy-start | bytes 245764
